TPU v7x, 32 devices: a whole 2x2x4 slice. The times are simulated.
32 devices in a mesh: grp: 2 (over x), seq: 8 (over z, y), tp: 2 (over core).
Axes of the slice: x: 2, y: 2, z: 4, core: 2. Of those that a mesh axis runs over, the one named last changes fastest.
Arguments:
- queries: bfloat16 [16384, 1536], P(('grp', 'seq'), 'tp'), parts along dimension 0, may hold values from -6 to 6
- attn_keys: bfloat16 [16384, 1536], P(('grp', 'seq'), 'tp'), parts along dimension 0, may hold values from -6 to 6
- attn_values: bfloat16 [16384, 1536], P(('grp', 'seq'), 'tp'), parts along dimension 0, may hold values from -6 to 6
- out_weight: bfloat16 [1536, 3072], P('tp'), may hold values from -0.15625 to 0.15625
- residual: bfloat16 [16384, 3072], P(('grp', 'seq'), 'tp'), parts along dimension 0, may hold values from -40 to 40
- norm_gain: float32 [3072], P('tp'), may hold values from 0.1 to 1.9
- conv_weight: float32 [31, 3072], P(None, 'tp'), may hold values from -1 to 1
- record_starts: int32 [16], P('grp'), parts along dimension 0, may hold values from 0 to 7039, as said below
- record_lengths: int32 [16], P('grp'), parts along dimension 0, may hold values from 256 to 1153, as said below
Outputs:
- block_out: bfloat16 [16384, 3072], P(('grp', 'seq'), 'tp'), parts along dimension 0
There are 2 independent parts, one for each index of `grp`. A program takes and returns all parts, laid end to end along the dimension named above; an argument that names none is the same for every part. Nothing has to cross between parts.
Inputs may be any that keep to these rules, and one draw needn't show every extreme that they name: `record_starts`: recording r lies in its stretch: frames 0 to 511 for r = 0; frames r * 1024 - 1024 // 2 to (r + 1) * 1024 - 1024 // 2 - 1 for 0 < r < 7; frames (7) * 1024 - 1024 // 2 to 8191 for the last. It starts within the first quarter of its stretch; recording 0 starts at frame 0. `record_lengths`: each recording ends inside its stretch.
All inputs are finite; a program needn't handle non-finite values.
Results may differ from a plain program's by a relative error of at most 0.0025.
Values may be sent and summed in bfloat16 or wider, within the bound.
No kernel may reach another device: no remote copies, remote signals or barrier semaphores. Data moves between devices by JAX's collectives and lax.ppermute only.
A program may use at most 128 MiB of HBM per device.

v0:
```python
import jax
import jax.numpy as jnp
from jax import lax
from jax.sharding import PartitionSpec as P

D = 3072
HSIZE = 64
WIN = 128
KHALF = 15
REC = 8
KERNEL = 31


def with_halo(cells, sides, width):
    for axis, dim in sides:
        count = lax.axis_size(axis)
        ends = count - 1
        head = lax.slice_in_dim(cells, 0, width, axis=dim)
        tail = lax.slice_in_dim(cells, cells.shape[dim] - width, cells.shape[dim], axis=dim)
        cells = jnp.concatenate(
            [
                lax.ppermute(tail, axis, [(i, (i + 1) % count) for i in range(ends)]),
                cells,
                lax.ppermute(head, axis, [((i + 1) % count, i) for i in range(ends)]),
            ],
            axis=dim,
        )
    return cells


def segment_of(positions, record_starts, record_lengths):
    inside = (positions[:, None] >= record_starts[None, :]) & (
        positions[:, None] < (record_starts + record_lengths)[None, :]
    )
    labels = jnp.arange(1, REC + 1, dtype=jnp.int32)
    return jnp.sum(jnp.where(inside, labels[None, :], 0), axis=1) - 1


def attend(query_block, key_block, value_block, query_segment, key_segment):
    block_rows = query_block.shape[0]
    key_span = key_block.shape[0]
    head_count = query_block.shape[1] // HSIZE
    query_heads = query_block.reshape(block_rows, head_count, HSIZE)
    key_heads = key_block.reshape(key_span, head_count, HSIZE)
    value_heads = value_block.reshape(key_span, head_count, HSIZE)
    scores = jnp.einsum(
        "qhd,khd->hqk", query_heads, key_heads, preferred_element_type=jnp.float32
    ) * HSIZE ** (-0.5)
    distance = jnp.arange(key_span)[None, :] - jnp.arange(block_rows)[:, None] - WIN
    allowed = (
        (jnp.abs(distance) <= WIN)
        & (query_segment[:, None] == key_segment[None, :])
        & (query_segment[:, None] >= 0)
    )
    masked = jnp.where(allowed[None], scores, jnp.float32(-1e30))
    row_max = jnp.max(masked, axis=-1, keepdims=True)
    exponent = jnp.where(allowed[None], jnp.exp(masked - row_max), jnp.float32(0.0))
    row_total = jnp.sum(exponent, axis=-1)
    divisor = jnp.where(query_segment[None, :] >= 0, row_total, jnp.float32(1.0))
    weights = exponent.astype(jnp.bfloat16)
    mixed_heads = jnp.einsum(
        "hqk,khd->qhd", weights, value_heads, preferred_element_type=jnp.float32
    )
    mixed_heads = mixed_heads / jnp.transpose(divisor)[:, :, None]
    mixed_heads = jnp.where(query_segment[:, None, None] >= 0, mixed_heads, jnp.float32(0.0))
    return mixed_heads.reshape(block_rows, head_count * HSIZE).astype(jnp.bfloat16)


def on_device(
    queries,
    attn_keys,
    attn_values,
    out_weight,
    residual,
    norm_gain,
    conv_weight,
    record_starts,
    record_lengths,
):
    frames = queries.shape[0]
    anchor = lax.axis_index("seq") * frames
    positions = anchor + jnp.arange(frames, dtype=jnp.int32)
    segment = segment_of(positions, record_starts, record_lengths)
    valid = segment >= 0
    paired = jnp.stack([attn_keys, attn_values])
    widened = with_halo(paired, (("seq", 1),), WIN)
    wide_segment = segment_of(
        anchor - WIN + jnp.arange(frames + 2 * WIN, dtype=jnp.int32), record_starts, record_lengths
    )
    block_rows = min(256, frames)

    def one_block(block_id):
        block_start = block_id * block_rows
        query_block = lax.dynamic_slice_in_dim(queries, block_start, block_rows, 0)
        key_block = lax.dynamic_slice_in_dim(widened[0], block_start, block_rows + 2 * WIN, 0)
        value_block = lax.dynamic_slice_in_dim(widened[1], block_start, block_rows + 2 * WIN, 0)
        query_segment = lax.dynamic_slice_in_dim(segment, block_start, block_rows, 0)
        key_segment = lax.dynamic_slice_in_dim(wide_segment, block_start, block_rows + 2 * WIN, 0)
        return attend(query_block, key_block, value_block, query_segment, key_segment)

    blocks = lax.map(one_block, jnp.arange(frames // block_rows, dtype=jnp.int32))
    attended = blocks.reshape(frames, -1)
    all_heads = lax.all_gather(attended, "tp", axis=1, tiled=True)
    columns = lax.all_to_all(out_weight, "tp", split_axis=1, concat_axis=0, tiled=True)
    projected = jnp.dot(all_heads, columns, preferred_element_type=jnp.float32)
    hidden_sum = residual.astype(jnp.float32) + projected
    row_mean = lax.psum(jnp.sum(hidden_sum, axis=1), "tp") / D
    centered = hidden_sum - row_mean[:, None]
    row_var = lax.psum(jnp.sum(centered * centered, axis=1), "tp") / D
    normed = centered * lax.rsqrt(row_var + jnp.float32(1e-05))[:, None] * norm_gain[None, :]
    normed = jnp.where(valid[:, None], normed, jnp.float32(0.0)).astype(jnp.bfloat16)
    padded_normed = with_halo(normed, (("seq", 0),), KHALF)
    normed_segment = segment_of(
        anchor - KHALF + jnp.arange(frames + 2 * KHALF, dtype=jnp.int32),
        record_starts,
        record_lengths,
    )
    conv_sum = jnp.zeros(hidden_sum.shape, jnp.float32)
    for tap_index in range(KERNEL):
        shifted = padded_normed[tap_index : tap_index + frames].astype(jnp.float32)
        same_record = normed_segment[tap_index : tap_index + frames] == segment
        conv_sum = conv_sum + jnp.where(
            same_record[:, None], conv_weight[tap_index][None, :] * shifted, jnp.float32(0.0)
        )
    return (hidden_sum + jax.nn.silu(conv_sum)).astype(jnp.bfloat16)


def solution(mesh):
    placed = (
        P(("grp", "seq"), "tp"),
        P(("grp", "seq"), "tp"),
        P(("grp", "seq"), "tp"),
        P("tp", None),
        P(("grp", "seq"), "tp"),
        P("tp"),
        P(None, "tp"),
        P("grp"),
        P("grp"),
    )
    return jax.shard_map(
        on_device, mesh=mesh, in_specs=placed, out_specs=P(("grp", "seq"), "tp"), check_vma=False
    )
```

profile of v0, /device:TPU:17, one launch (start us, length us, event | category | flops | bytes accessed | tf_op | source)
XLA Modules:
  0.0 233.9 jit_solution(276748390770257809)
XLA Ops:
  11.0 3.1 %collective-permute-start = (bf16[2,128,768]{1,2,0:T(8,128)(2,1)}, bf16[2,128,768]{1,2,0:T(8,128)(2,1)S(1)}, u32[]{:S(2)}, u32[]{:S(2)}) collective-permute-start(bf16[2,128,768]{1,2,0:T(8,128)(2,1)} %get-tuple-element.178), channel_id=1, source_target_pairs={{0,2},{2,4},{4,6},{6,8},{8,10},{10,12},{12,14},{1,3},{3,5},{5,7},{... | collective-permute-start | bytes 1179656 | tf_op jit(solution)/shard_map/ppermute | solution.py:22
  14.2 3.0 %collective-permute-start.1 = (bf16[2,128,768]{1,2,0:T(8,128)(2,1)}, bf16[2,128,768]{1,2,0:T(8,128)(2,1)}, u32[]{:S(2)}, u32[]{:S(2)}) collective-permute-start(bf16[2,128,768]{1,2,0:T(8,128)(2,1)} %get-tuple-element.179), channel_id=1, source_target_pairs={{2,0},{4,2},{6,4},{8,6},{10,8},{12,10},{14,12},{3,1},{5,3},{7,5},{... | collective-permute-start | bytes 1179656 | tf_op jit(solution)/shard_map/ppermute | solution.py:24
  18.6 12.0 %collective-permute-done = bf16[2,128,768]{1,2,0:T(8,128)(2,1)S(1)} collective-permute-done((bf16[2,128,768]{1,2,0:T(8,128)(2,1)}, bf16[2,128,768]{1,2,0:T(8,128)(2,1)S(1)}, u32[]{:S(2)}, u32[]{:S(2)}) %collective-permute-start) | collective-permute-done | bytes 393248 | tf_op jit(solution)/shard_map/ppermute | solution.py:22
  30.7 2.9 %collective-permute-done.1 = bf16[2,128,768]{1,2,0:T(8,128)(2,1)} collective-permute-done((bf16[2,128,768]{1,2,0:T(8,128)(2,1)}, bf16[2,128,768]{1,2,0:T(8,128)(2,1)}, u32[]{:S(2)}, u32[]{:S(2)}) %collective-permute-start.1) | collective-permute-done | bytes 393248 | tf_op jit(solution)/shard_map/ppermute | solution.py:24
  33.6 3.0 %pad_maximum_fusion = bf16[2,1280,768]{1,2,0:T(8,128)(2,1)} fusion(bf16[2,128,768]{1,2,0:T(8,128)(2,1)} %collective-permute-done.1, bf16[1,1024,768]{1,2,0:T(8,128)(2,1)S(1)} %bitcast.58, bf16[1,1024,768]{1,2,0:T(8,128)(2,1)S(1)} %bitcast.56, bf16[2,128,768]{1,2,0:T(8,128)(2,1)S(1)} %collective-permute-done), kind=kLoop, calls=%fused_computation.57 | loop fusion | flops 15728640 | bytes 7864320 | tf_op jit(solution)/shard_map/concatenate | solution.py:20
  36.6 53.7 %while.12 = (s32[]{:T(128)}, bf16[4,256,768]{2,1,0:T(8,128)(2,1)}, s32[4]{0:T(128)S(1)}, s32[1024]{0:T(1024)S(1)}, bf16[2,1280,768]{1,2,0:T(8,128)(2,1)}, /*inde...) while((s32[]{:T(128)}, bf16[4,256,768]{2,1,0:T(8,128)(2,1)}, ...), condition=%wide.region_5.6_spmd, body=%wide.region_2.5_spmd.sunk | while | flops 413601536 | bytes 23128792 | solution.py:101
  41.9 4.2 %fusion.79 = (f32[12,256]{1,0:T(8,128)S(1)}, bf16[12,256,512]{2,1,0:T(8,128)(2,1)}) fusion(pred[256,512]{1,0:T(8,128)(4,1)S(1)} %fusion.78, bf16[256,12,64]{0,2,1:T(8,128)(2,1)S(1)} %bitcast.59, bf16[512,12,64]{0,2,1:T(8,128)(2,1)S(1)} %bitcast.52), kind=kOutput, calls=%fused_computation.182.clone.1 | convolution fusion | flops 210764288 | bytes 4468736 | tf_op jit(solution)/shard_map/while/body/eval_jaxpr/sub | solution.py:57
  46.1 3.0 %fusion.80 = bf16[256,12,64]{0,2,1:T(8,128)(2,1)S(1)} fusion(bf16[512,12,64]{0,2,1:T(8,128)(2,1)S(1)} %bitcast.51, bf16[12,256,512]{2,1,0:T(8,128)(2,1)} %get-tuple-element.273, f32[256,12]{0,1:T(8,128)S(1)} %select_bitcast_fusion.2, pred[256]{0:T(512)(128)(4,1)S(1)} %get-tuple-element.271), kind=kOutput, calls=%fused_computation.12.clone.1 | convolution fusion | flops 201916416 | bytes 4337920 | tf_op jit(solution)/shard_map/while/body/eval_jaxpr/hqk,khd->qhd/dot_general | solution.py:61
  55.3 4.2 %fusion.79 = (f32[12,256]{1,0:T(8,128)S(1)}, bf16[12,256,512]{2,1,0:T(8,128)(2,1)}) fusion(pred[256,512]{1,0:T(8,128)(4,1)S(1)} %fusion.78, bf16[256,12,64]{0,2,1:T(8,128)(2,1)S(1)} %bitcast.59, bf16[512,12,64]{0,2,1:T(8,128)(2,1)S(1)} %bitcast.52), kind=kOutput, calls=%fused_computation.182.clone.1 | convolution fusion | flops 210764288 | bytes 4468736 | tf_op jit(solution)/shard_map/while/body/eval_jaxpr/sub | solution.py:57
  59.5 3.0 %fusion.80 = bf16[256,12,64]{0,2,1:T(8,128)(2,1)S(1)} fusion(bf16[512,12,64]{0,2,1:T(8,128)(2,1)S(1)} %bitcast.51, bf16[12,256,512]{2,1,0:T(8,128)(2,1)} %get-tuple-element.273, f32[256,12]{0,1:T(8,128)S(1)} %select_bitcast_fusion.2, pred[256]{0:T(512)(128)(4,1)S(1)} %get-tuple-element.271), kind=kOutput, calls=%fused_computation.12.clone.1 | convolution fusion | flops 201916416 | bytes 4337920 | tf_op jit(solution)/shard_map/while/body/eval_jaxpr/hqk,khd->qhd/dot_general | solution.py:61
  68.8 4.2 %fusion.79 = (f32[12,256]{1,0:T(8,128)S(1)}, bf16[12,256,512]{2,1,0:T(8,128)(2,1)}) fusion(pred[256,512]{1,0:T(8,128)(4,1)S(1)} %fusion.78, bf16[256,12,64]{0,2,1:T(8,128)(2,1)S(1)} %bitcast.59, bf16[512,12,64]{0,2,1:T(8,128)(2,1)S(1)} %bitcast.52), kind=kOutput, calls=%fused_computation.182.clone.1 | convolution fusion | flops 210764288 | bytes 4468736 | tf_op jit(solution)/shard_map/while/body/eval_jaxpr/sub | solution.py:57
  72.9 3.0 %fusion.80 = bf16[256,12,64]{0,2,1:T(8,128)(2,1)S(1)} fusion(bf16[512,12,64]{0,2,1:T(8,128)(2,1)S(1)} %bitcast.51, bf16[12,256,512]{2,1,0:T(8,128)(2,1)} %get-tuple-element.273, f32[256,12]{0,1:T(8,128)S(1)} %select_bitcast_fusion.2, pred[256]{0:T(512)(128)(4,1)S(1)} %get-tuple-element.271), kind=kOutput, calls=%fused_computation.12.clone.1 | convolution fusion | flops 201916416 | bytes 4337920 | tf_op jit(solution)/shard_map/while/body/eval_jaxpr/hqk,khd->qhd/dot_general | solution.py:61
  82.2 4.2 %fusion.79 = (f32[12,256]{1,0:T(8,128)S(1)}, bf16[12,256,512]{2,1,0:T(8,128)(2,1)}) fusion(pred[256,512]{1,0:T(8,128)(4,1)S(1)} %fusion.78, bf16[256,12,64]{0,2,1:T(8,128)(2,1)S(1)} %bitcast.59, bf16[512,12,64]{0,2,1:T(8,128)(2,1)S(1)} %bitcast.52), kind=kOutput, calls=%fused_computation.182.clone.1 | convolution fusion | flops 210764288 | bytes 4468736 | tf_op jit(solution)/shard_map/while/body/eval_jaxpr/sub | solution.py:57
  86.4 3.0 %fusion.80 = bf16[256,12,64]{0,2,1:T(8,128)(2,1)S(1)} fusion(bf16[512,12,64]{0,2,1:T(8,128)(2,1)S(1)} %bitcast.51, bf16[12,256,512]{2,1,0:T(8,128)(2,1)} %get-tuple-element.273, f32[256,12]{0,1:T(8,128)S(1)} %select_bitcast_fusion.2, pred[256]{0:T(512)(128)(4,1)S(1)} %get-tuple-element.271), kind=kOutput, calls=%fused_computation.12.clone.1 | convolution fusion | flops 201916416 | bytes 4337920 | tf_op jit(solution)/shard_map/while/body/eval_jaxpr/hqk,khd->qhd/dot_general | solution.py:61
  90.3 6.7 %copy.27 = bf16[768,3072]{0,1:T(8,128)(2,1)} copy(bf16[768,3072]{1,0:T(8,128)(2,1)} %param.14) | data formatting | bytes 9437184 | tf_op args[3]
  97.0 12.9 %all_to_all.19 = bf16[768,2,1536]{0,2,1:T(8,128)(2,1)} all-to-all(bf16[768,2,1536]{0,2,1:T(8,128)(2,1)} %bitcast.54), channel_id=1, replica_groups=mesh['grp'=2,'seq'=8,'tp'=2] {'tp'}, dimensions={1} | all-to-all | bytes 9437184 | tf_op jit(solution)/shard_map/all_to_all | solution.py:104
  110.0 6.9 %copy.28 = bf16[2,768,1536]{2,1,0:T(8,128)(2,1)} copy(bf16[2,768,1536]{1,2,0:T(8,128)(2,1)} %bitcast.53) | data formatting | bytes 9437184 | tf_op jit(solution)/shard_map/all_to_all | solution.py:104
  119.3 9.8 %fusion.56 = (f32[1024]{0:T(1024)S(1)}, f32[1024,1536]{1,0:T(8,128)}) fusion(bf16[1024,1536]{1,0:T(8,128)(2,1)} %all-gather.2.cloned.1.call-done, bf16[1536,1536]{1,0:T(8,128)(2,1)} %bitcast.61, bf16[1024,1536]{1,0:T(8,128)(2,1)S(1)} %copy-done.8), kind=kOutput, calls=%fused_computation.184 | convolution fusion | flops 4836555776 | bytes 17305600 | tf_op jit(solution)/shard_map/dot_general | solution.py:105
  129.2 2.6 %psum.14 = f32[1024]{0:T(1024)S(1)} all-reduce(f32[1024]{0:T(1024)S(1)} %get-tuple-element.212), channel_id=1, replica_groups=mesh['grp'=2,'seq'=8,'tp'=2] {'tp'}, use_global_device_ids=true, to_apply=%region_8.9 | all-reduce | flops 1024 | bytes 8192 | tf_op jit(solution)/shard_map/psum | solution.py:107
  131.8 3.5 %multiply_reduce_fusion = f32[1024]{0:T(1024)S(1)} fusion(f32[1024,1536]{1,0:T(8,128)} %get-tuple-element.213, f32[1024]{0:T(1024)S(1)} %broadcast_multiply_fusion), kind=kLoop, calls=%fused_computation.55 | loop fusion | flops 4717568 | bytes 6299648 | tf_op jit(solution)/shard_map/reduce_sum | solution.py:109
  135.3 2.5 %psum.15 = f32[1024]{0:T(1024)S(1)} all-reduce(f32[1024]{0:T(1024)S(1)} %multiply_reduce_fusion), channel_id=1, replica_groups=mesh['grp'=2,'seq'=8,'tp'=2] {'tp'}, use_global_device_ids=true, to_apply=%region_10.11 | all-reduce | flops 1024 | bytes 8192 | tf_op jit(solution)/shard_map/psum | solution.py:109
  137.8 3.5 %select_convert_fusion = bf16[1024,1536]{1,0:T(8,128)(2,1)S(1)} fusion(f32[1024,1536]{1,0:T(8,128)} %get-tuple-element.213, f32[1536]{0:T(1024)S(1)} %copy-done.1, f32[1024]{0:T(1024)S(1)} %add_rsqrt_fusion, f32[1024]{0:T(1024)S(1)} %broadcast_multiply_fusion, pred[1024]{0:T(1024)(128)(4,1)S(1)} %get-tuple-element.211), kind=kLoop, calls=%fused_computation.54 | loop fusion | flops 7864320 | bytes 9452544 | tf_op jit(solution)/shard_map/convert_element_type | solution.py:111
  143.5 4.2 %collective-permute-start.3 = (bf16[15,1536]{1,0:T(8,128)(2,1)S(1)}, bf16[15,1536]{1,0:T(8,128)(2,1)S(1)}, u32[]{:S(2)}, u32[]{:S(2)}) collective-permute-start(bf16[15,1536]{1,0:T(8,128)(2,1)S(1)} %get-tuple-element.177), channel_id=1, source_target_pairs={{2,0},{4,2},{6,4},{8,6},{10,8},{12,10},{14,12},{3,1},{5,3},{7,5},{... | collective-permute-start | bytes 138248 | tf_op jit(solution)/shard_map/ppermute | solution.py:24
  149.1 77.9 %add_convert_fusion = bf16[1024,1536]{1,0:T(8,128)(2,1)} fusion(f32[1024,1536]{1,0:T(8,128)} %get-tuple-element.213, bf16[1024,1536]{1,0:T(8,128)(2,1)S(1)} %select_convert_fusion, bf16[15,1536]{1,0:T(8,128)(2,1)S(1)} %collective-permute-done.3, bf16[15,1536]{1,0:T(8,128)(2,1)S(1)} %collective-permute-done.2, f32[1536]{0:T(1024)} %get-tuple-element.152, ...), kind=kLoop, calls=%fused_computation.53 | loop fusion | flops 344457216 | bytes 12897280 | tf_op jit(solution)/shard_map/convert_element_type | solution.py:125
  (93 shorter events, 34.4 us)
Async XLA Ops:
  6.5 10.7 %copy-start.2 = (s32[8]{0:T(128)S(1)}, s32[8]{0:T(128)}, u32[]{:S(2)}) copy-start(s32[8]{0:T(128)} %param.18) | copy-start | bytes 100
  6.5 10.7 %copy-start.9 = (s32[8]{0:T(128)S(1)}, s32[8]{0:T(128)}, u32[]{:S(2)}) copy-start(s32[8]{0:T(128)} %param.19) | copy-start | bytes 100
  6.5 112.8 %all-gather.2.cloned.1.call-start = ((), (), s32[]{:S(2)}) async-start(), calls=%async_computation.1 | async-start | bytes 4718592 | tf_op jit(solution)/shard_map/all_gather | solution.py:103
  11.0 19.6 %collective-permute-start = (bf16[2,128,768]{1,2,0:T(8,128)(2,1)}, bf16[2,128,768]{1,2,0:T(8,128)(2,1)S(1)}, u32[]{:S(2)}, u32[]{:S(2)}) collective-permute-start(bf16[2,128,768]{1,2,0:T(8,128)(2,1)} %get-tuple-element.178), channel_id=1, source_target_pairs={{0,2},{2,4},{4,6},{6,8},{8,10},{10,12},{12,14},{1,3},{3,5},{5,7},{... | collective-permute-start | bytes 1179656 | tf_op jit(solution)/shard_map/ppermute | solution.py:22
  14.2 19.4 %collective-permute-start.1 = (bf16[2,128,768]{1,2,0:T(8,128)(2,1)}, bf16[2,128,768]{1,2,0:T(8,128)(2,1)}, u32[]{:S(2)}, u32[]{:S(2)}) collective-permute-start(bf16[2,128,768]{1,2,0:T(8,128)(2,1)} %get-tuple-element.179), channel_id=1, source_target_pairs={{2,0},{4,2},{6,4},{8,6},{10,8},{12,10},{14,12},{3,1},{5,3},{7,5},{... | collective-permute-start | bytes 1179656 | tf_op jit(solution)/shard_map/ppermute | solution.py:24
  17.2 0.6 copy-start.4
  17.3 0.6 copy-start.6
  109.9 6.9 %copy-start.3 = (s32[8]{0:T(128)S(1)}, s32[8]{0:T(128)}, u32[]{:S(2)}) copy-start(s32[8]{0:T(128)} %param.18) | copy-start | bytes 100
  109.9 6.9 %copy-start.5 = (s32[8]{0:T(128)S(1)}, s32[8]{0:T(128)}, u32[]{:S(2)}) copy-start(s32[8]{0:T(128)} %copy-done.4) | copy-start | bytes 100
  109.9 6.9 %copy-start.7 = (s32[8]{0:T(128)S(1)}, s32[8]{0:T(128)}, u32[]{:S(2)}) copy-start(s32[8]{0:T(128)} %copy-done.6) | copy-start | bytes 100
  109.9 7.0 %copy-start = (f32[31,1536]{1,0:T(8,128)S(1)}, f32[31,1536]{1,0:T(8,128)}, u32[]{:S(2)}) copy-start(f32[31,1536]{1,0:T(8,128)} %param.17) | copy-start | bytes 571396
  109.9 9.4 %copy-start.8 = (bf16[1024,1536]{1,0:T(8,128)(2,1)S(1)}, bf16[1024,1536]{1,0:T(8,128)(2,1)}, u32[]{:S(2)}) copy-start(bf16[1024,1536]{1,0:T(8,128)(2,1)} %param.15) | copy-start | bytes 9437188
  129.2 8.7 %copy-start.1 = (f32[1536]{0:T(1024)S(1)}, f32[1536]{0:T(1024)}, u32[]{:S(2)}) copy-start(f32[1536]{0:T(1024)} %param.16) | copy-start | bytes 18436
  141.3 7.2 %collective-permute-start.2 = (bf16[15,1536]{1,0:T(8,128)(2,1)S(1)}, bf16[15,1536]{1,0:T(8,128)(2,1)S(1)}, u32[]{:S(2)}, u32[]{:S(2)}) collective-permute-start(bf16[15,1536]{1,0:T(8,128)(2,1)S(1)} %get-tuple-element.176), channel_id=1, source_target_pairs={{0,2},{2,4},{4,6},{6,8},{8,10},{10,12},{12,14},{1,3},{3,5},{5,7},{... | collective-permute-start | bytes 138248 | tf_op jit(solution)/shard_map/ppermute | solution.py:22
  143.5 5.6 %collective-permute-start.3 = (bf16[15,1536]{1,0:T(8,128)(2,1)S(1)}, bf16[15,1536]{1,0:T(8,128)(2,1)S(1)}, u32[]{:S(2)}, u32[]{:S(2)}) collective-permute-start(bf16[15,1536]{1,0:T(8,128)(2,1)S(1)} %get-tuple-element.177), channel_id=1, source_target_pairs={{2,0},{4,2},{6,4},{8,6},{10,8},{12,10},{14,12},{3,1},{5,3},{7,5},{... | collective-permute-start | bytes 138248 | tf_op jit(solution)/shard_map/ppermute | solution.py:24
Sparse Core Ops, SparseCore 0:
  90.4 12.7 all-gather.1
where the time goes:
time: 237 us; the launch traced here: 234 us
  other arithmetic  92.5 us (39%)
  local copies, waits for them, and re-layouts  40.6 us (17%)
  matrix products  38.3 us (16%)
  blocking collectives  18 us (8%)
  waiting for transfers between devices  15.6 us (7%)
  between operations  13.6 us (6%)
  starting transfers between devices  12.5 us (5%)
  loops' own time  2.78 us (1%)
    convert_element_type x1, other arithmetic, on_device(): return (hidden_sum + jax.nn.silu(conv_sum)).astype(jnp.bfloat16)  77.9 us
    sub x4, matrix products, attend(): masked - row_max  16.7 us
    all_to_all x1, blocking collectives, on_device(): lax.all_to_all(out_weight, 'tp', split_axis=1, concat_axis=0, tiled=True)  12.9 us
    ppermute x2, waiting for transfers between devices, with_halo(): lax.ppermute(tail, axis, [(i, (i + 1) % count) for i in range(ends)])  12 us
    dot_general x4, matrix products, attend(): jnp.einsum('hqk,khd->qhd', weights, value_heads, preferred_element_type=j...  11.8 us
    unnamed x23, local copies, waits for them, and re-layouts  10.7 us
    dot_general x1, matrix products, on_device(): projected = jnp.dot(all_heads, columns, preferred_element_type=jnp.float32)  9.83 us
    slice x4, local copies, waits for them, and re-layouts, one_block(): widened[0]  9.57 us
  transfers between devices with their start and end apart: 5, of which 3 were waited for; matrix products, arithmetic and copies ran while one was open for 8% of the time, Pallas kernels for 0%

commit v1 on v0

v1 whole, which is shorter than its diff:
```python
import functools

import jax
import jax.numpy as jnp
from jax import lax
from jax.experimental import pallas as pl
from jax.experimental.pallas import tpu as pltpu
from jax.sharding import PartitionSpec as P

D = 3072
HSIZE = 64
WIN = 128
KHALF = 15
REC = 8
KERNEL = 31
EDGE = 16
REACH = WIN + EDGE
SPAN = 512
LANES = 128
NEG = -1e30
EXP_SCALE = HSIZE ** (-0.5) * 1.4426950408889634
SMEM = pl.BlockSpec(memory_space=pltpu.SMEM)


def row_bounds(positions, starts_ref, lengths_ref):
    first = jnp.full(positions.shape, -1, jnp.int32)
    last = jnp.full(positions.shape, -2, jnp.int32)
    for r in range(REC):
        start = starts_ref[r]
        end = start + lengths_ref[r]
        inside = (positions >= start) & (positions < end)
        first = jnp.where(inside, start, first)
        last = jnp.where(inside, end - 1, last)
    return first, last


def as_column(row):
    return jnp.transpose(jnp.broadcast_to(row, (LANES, LANES)))


def band_bias(base, rows, key_base, keys, starts_ref, lengths_ref, store):
    for top in range(0, rows, LANES):
        count = min(LANES, rows - top)
        positions = base + top + lax.broadcasted_iota(jnp.int32, (1, LANES), 1)
        first, last = row_bounds(positions, starts_ref, lengths_ref)
        inside = first >= 0
        low = jnp.where(inside, jnp.maximum(first, positions - WIN), 0)
        high = jnp.where(inside, jnp.minimum(last, positions + WIN), -1)
        low = as_column(low.astype(jnp.float32))
        high = as_column(high.astype(jnp.float32))
        for left in range(0, keys, LANES):
            key_at = (key_base + left + lax.broadcasted_iota(jnp.int32, (LANES, LANES), 1)).astype(jnp.float32)
            bias = jnp.where((key_at >= low) & (key_at <= high), jnp.float32(0.0), jnp.float32(NEG))
            store(top, count, left, bias[:count])


def head_pair(query, keys, values, bias):
    rows = query.shape[0]
    left = lax.broadcasted_iota(jnp.int32, query.shape, 1) < HSIZE
    nothing = jnp.zeros_like(query)
    both = jnp.concatenate([jnp.where(left, query, nothing), jnp.where(left, nothing, query)], axis=0)
    scores = lax.dot_general(both, keys, (((1,), (1,)), ((), ())), preferred_element_type=jnp.float32)
    scores = scores + jnp.concatenate([bias, bias], axis=0)
    row_max = jnp.max(scores, axis=1, keepdims=True)
    weights = jnp.exp2((scores - row_max) * EXP_SCALE).astype(jnp.bfloat16)
    mixed = jnp.dot(weights, values, preferred_element_type=jnp.float32)
    mixed = mixed[:, :LANES] / mixed[:, LANES:]
    keep = bias_any(bias)
    return jnp.where(keep, jnp.where(left, mixed[:rows], mixed[rows:]), 0.0).astype(jnp.bfloat16)


def bias_any(bias):
    return jnp.max(bias, axis=1, keepdims=True) > NEG / 2


def attend_inner(frames, starts_ref, lengths_ref, q_ref, k_ref, v_ref, o_ref, bias, wide):
    blocks = frames // WIN - 2
    anchor = lax.axis_index("seq") * frames

    @pl.when(pl.program_id(0) == 0)
    def _():
        wide[:, LANES:] = jnp.ones((frames, LANES), jnp.bfloat16)
        for i in range(blocks):
            def store(top, count, left, value):
                bias[i, top : top + count, left : left + LANES] = value

            band_bias(anchor + (i + 1) * WIN, WIN, anchor + i * WIN, 3 * WIN, starts_ref, lengths_ref, store)

    wide[:, :LANES] = v_ref[...]
    for i in range(blocks):
        window = slice(i * WIN, (i + 3) * WIN)
        o_ref[i * WIN : (i + 1) * WIN, :] = head_pair(
            q_ref[(i + 1) * WIN : (i + 2) * WIN, :], k_ref[window, :], wide[window, :], bias[i]
        )


def attend_ends(frames, starts_ref, lengths_ref, q_ref, k_ref, v_ref, before_ref, after_ref, o_ref, bias):
    anchor = lax.axis_index("seq") * frames
    own = SPAN - REACH

    @pl.when(pl.program_id(0) == 0)
    def _():
        for i, (base, key_base) in enumerate(((-EDGE, -REACH), (frames - WIN, frames - own))):
            def store(top, count, left, value):
                bias[i, top : top + count, left : left + LANES] = value

            band_bias(anchor + base, REACH, anchor + key_base, SPAN, starts_ref, lengths_ref, store)

    ones = jnp.ones((SPAN, LANES), jnp.bfloat16)
    for i in range(2):
        halo = (before_ref, after_ref)[i]
        mine = slice(0, own) if i == 0 else slice(frames - own, frames)

        def joined(far, near):
            return jnp.concatenate([far, near] if i == 0 else [near, far], axis=0)

        keys = joined(halo[:REACH, :], k_ref[mine, :])
        values = joined(halo[REACH : 2 * REACH, :], v_ref[mine, :])
        query = joined(halo[2 * REACH : 2 * REACH + EDGE, :], q_ref[:WIN, :] if i == 0 else q_ref[frames - WIN :, :])
        o_ref[i * REACH : (i + 1) * REACH, :] = head_pair(
            query, keys, jnp.concatenate([values, ones], axis=1), bias[i]
        )


def project(rows, own_ref, other_ref, w_own_ref, w_other_ref, res_ref, h_ref, stats_ref):
    width = h_ref.shape[1]
    step = 512
    total = jnp.zeros((rows, LANES), jnp.float32)
    for c in range(0, width, step):
        cols = slice(c, c + step)
        part = jnp.dot(own_ref[...], w_own_ref[:, cols], preferred_element_type=jnp.float32)
        part = part + jnp.dot(other_ref[...], w_other_ref[:, cols], preferred_element_type=jnp.float32)
        part = part + res_ref[:, cols].astype(jnp.float32)
        h_ref[:, cols] = part
        for l in range(0, step, LANES):
            total = total + part[:, l : l + LANES]
    mean = jnp.sum(total, axis=1, keepdims=True) * (1.0 / width)
    square = jnp.zeros((rows, LANES), jnp.float32)
    for c in range(0, width, LANES):
        off = h_ref[:, c : c + LANES] - mean
        square = square + off * off
    square = jnp.sum(square, axis=1, keepdims=True)
    for top in range(0, rows, LANES):
        count = min(LANES, rows - top)
        for k, column in enumerate((mean, square)):
            tile = jnp.broadcast_to(column[top : top + count], (count, LANES))
            if count < LANES:
                tile = jnp.concatenate([tile, jnp.zeros((LANES - count, LANES), jnp.float32)], axis=0)
            stats_ref[8 * k : 8 * k + 8, top : top + LANES] = jnp.transpose(tile)[:8, :]


def silu_add(hidden, conv_sum):
    half = conv_sum * 0.5
    return (hidden + (half + half * jnp.tanh(half))).astype(jnp.bfloat16)


def norm_conv(
    frames, starts_ref, lengths_ref, h_in_ref, h_end_ref, s_in_ref, t_in_ref, s_end_ref, t_end_ref, gain_ref, w_ref,
    o_ref, mean, scale, parity, normed, masked, flags,
):
    anchor = lax.axis_index("seq") * frames
    total = frames + 2 * EDGE
    chunk = 128
    width = 2.0 * h_in_ref.shape[1] * pl.num_programs(0)

    @pl.when(pl.program_id(0) == 0)
    def _():
        def place(at, count, base, own, other):
            positions = base + lax.broadcasted_iota(jnp.int32, (1, LANES), 1)
            index = jnp.zeros((1, LANES), jnp.int32) - 1
            for r in range(REC):
                start = starts_ref[r]
                inside = (positions >= start) & (positions < start + lengths_ref[r])
                index = jnp.where(inside, r, index)
            gap = own[0:1, :] - other[0:1, :]
            middle = 0.5 * (own[0:1, :] + other[0:1, :])
            var = (own[8:9, :] + other[8:9, :] + gap * gap * (width * 0.25)) * (1.0 / width)
            inverse = jnp.where(index >= 0, lax.rsqrt(var + 1e-5), 0.0)
            even = jnp.where(index >= 0, (index % 2).astype(jnp.float32), -1.0)
            mean[at : at + count, :] = as_column(middle)[:count]
            scale[at : at + count, :] = as_column(inverse)[:count]
            parity[at : at + count, :] = as_column(even)[:count]

        for top in range(0, frames - 2 * WIN, LANES):
            place(REACH + top, LANES, anchor + WIN + top, s_in_ref[:, top : top + LANES], t_in_ref[:, top : top + LANES])
        for i in range(2):
            for top, count in ((0, LANES), (LANES, EDGE)):
                lane = i * 2 * LANES + top

                def piece(ref):
                    return ref[:, lane : lane + LANES]

                base = (-EDGE if i == 0 else frames - WIN) + top
                ext = base + EDGE
                place(ext, count, anchor + base, piece(s_end_ref), piece(t_end_ref))
        for c in range(frames // chunk):
            count = jnp.int32(0)
            for r in range(REC):
                start = starts_ref[r] - anchor
                meets = (start < (c + 1) * chunk + KHALF) & (start + lengths_ref[r] > c * chunk - KHALF)
                count = count + meets.astype(jnp.int32)
            flags[c] = count

    gain = gain_ref[...]
    for source, at, count in (
        (h_end_ref[:REACH, :], 0, REACH),
        (h_in_ref[...], REACH, frames - 2 * WIN),
        (h_end_ref[REACH:, :], frames - WIN + EDGE, REACH),
    ):
        value = (source - mean[at : at + count, :]) * scale[at : at + count, :] * gain
        normed[at : at + count, :] = value.astype(jnp.bfloat16).astype(jnp.float32)

    def hidden_of(top, count):
        pieces = []
        for ref, at, lo, hi in (
            (h_end_ref, 0, -EDGE, WIN),
            (h_in_ref, 0, WIN, frames - WIN),
            (h_end_ref, REACH, frames - WIN, frames + EDGE),
        ):
            a, b = max(lo, top), min(hi, top + count)
            if a < b:
                pieces.append(ref[at + a - lo : at + b - lo, :])
        return pieces[0] if len(pieces) == 1 else jnp.concatenate(pieces, axis=0)

    def taps(load):
        acc = load(0) * w_ref[0:1, :]
        for tap in range(1, KERNEL):
            acc = acc + load(tap) * w_ref[tap : tap + 1, :]
        return acc

    for c in range(frames // chunk):
        top = c * chunk
        at = top + EDGE
        conv_sum = taps(lambda tap: normed[at - KHALF + tap : at - KHALF + tap + chunk, :])
        conv_sum = jnp.where(parity[at : at + chunk, :] >= 0, conv_sum, 0.0)
        o_ref[top : top + chunk, :] = silu_add(hidden_of(top, chunk), conv_sum)

    for c in range(frames // chunk):
        top = c * chunk
        at = top + EDGE

        @pl.when(flags[c] > 1)
        def _():
            conv_sum = jnp.zeros((chunk, LANES), jnp.float32)
            for side in range(2):
                masked[...] = jnp.where(
                    parity[at - EDGE : at + chunk + EDGE, :] == side, normed[at - EDGE : at + chunk + EDGE, :], 0.0
                )
                first = EDGE - KHALF
                part = taps(lambda tap: masked[first + tap : first + tap + chunk, :])
                conv_sum = jnp.where(parity[at : at + chunk, :] == side, part, conv_sum)
            o_ref[top : top + chunk, :] = silu_add(hidden_of(top, chunk), conv_sum)


def on_device(
    queries, attn_keys, attn_values, out_weight, residual, norm_gain, conv_weight, record_starts, record_lengths
):
    frames, heads_width = queries.shape
    width = residual.shape[1]
    pairs = heads_width // LANES
    inner = frames - 2 * WIN
    ends = 2 * REACH
    count = lax.axis_size("seq")
    swap = [(0, 1), (1, 0)]
    grid_params = pltpu.CompilerParams(vmem_limit_bytes=48 * 2**20)

    def payload(lo):
        def rows(array, n):
            return array[:n] if lo else array[-n:]

        edge = rows(residual, EDGE)
        return jnp.concatenate(
            [rows(attn_keys, REACH), rows(attn_values, REACH), rows(queries, EDGE), edge[:, :heads_width], edge[:, heads_width:]],
            axis=0,
        )

    after = lax.ppermute(payload(True), "seq", [(i + 1, i) for i in range(count - 1)])
    before = lax.ppermute(payload(False), "seq", [(i, i + 1) for i in range(count - 1)])
    weight_other = lax.ppermute(out_weight, "tp", swap)

    column = pl.BlockSpec((frames, LANES), lambda p: (0, p))
    attended_in = pl.pallas_call(
        functools.partial(attend_inner, frames),
        grid=(pairs,),
        out_shape=jax.ShapeDtypeStruct((inner, heads_width), jnp.bfloat16),
        in_specs=[SMEM, SMEM, column, column, column],
        out_specs=pl.BlockSpec((inner, LANES), lambda p: (0, p)),
        scratch_shapes=[
            pltpu.VMEM((inner // WIN, WIN, 3 * WIN), jnp.float32),
            pltpu.VMEM((frames, 2 * LANES), jnp.bfloat16),
        ],
        compiler_params=grid_params,
        name="attend_inner",
    )(record_starts, record_lengths, queries, attn_keys, attn_values)

    halo = pl.BlockSpec((before.shape[0], LANES), lambda p: (0, p))
    attended_end = pl.pallas_call(
        functools.partial(attend_ends, frames),
        grid=(pairs,),
        out_shape=jax.ShapeDtypeStruct((ends, heads_width), jnp.bfloat16),
        in_specs=[SMEM, SMEM, column, column, column, halo, halo],
        out_specs=pl.BlockSpec((ends, LANES), lambda p: (0, p)),
        scratch_shapes=[pltpu.VMEM((2, REACH, SPAN), jnp.float32)],
        compiler_params=grid_params,
        name="attend_ends",
    )(record_starts, record_lengths, queries, attn_keys, attn_values, before, after)

    mine = lax.axis_index("tp").astype(jnp.int32).reshape(1)

    def projection(own, other, res, tile, name):
        rows = own.shape[0]
        padded = -(-tile // LANES) * LANES
        return pl.pallas_call(
            lambda t_ref, *refs: project(tile, *refs),
            grid_spec=pltpu.PrefetchScalarGridSpec(
                num_scalar_prefetch=1,
                grid=(rows // tile,),
                in_specs=[
                    pl.BlockSpec((tile, heads_width), lambda i, t: (i, 0)),
                    pl.BlockSpec((tile, heads_width), lambda i, t: (i, 0)),
                    pl.BlockSpec((heads_width, width), lambda i, t: (0, t[0])),
                    pl.BlockSpec((heads_width, width), lambda i, t: (0, t[0])),
                    pl.BlockSpec((tile, width), lambda i, t: (i, 0)),
                ],
                out_specs=[
                    pl.BlockSpec((tile, width), lambda i, t: (i, 0)),
                    pl.BlockSpec((16, padded), lambda i, t: (0, i)),
                ],
            ),
            out_shape=[
                jax.ShapeDtypeStruct((rows, width), jnp.float32),
                jax.ShapeDtypeStruct((16, rows // tile * padded), jnp.float32),
            ],
            compiler_params=grid_params,
            name=name,
        )(mine, own, other, out_weight, weight_other, res)

    other_in = lax.ppermute(attended_in, "tp", swap)
    hidden_in, stats_in = projection(attended_in, other_in, residual[WIN : frames - WIN], 128, "project_inner")
    other_stats_in = lax.ppermute(stats_in, "tp", swap)

    def edge_rows(received):
        tail = received[2 * REACH + EDGE :]
        return jnp.concatenate([tail[:EDGE], tail[EDGE:]], axis=1)

    residual_end = jnp.concatenate(
        [edge_rows(before), residual[:WIN], residual[frames - WIN :], edge_rows(after)], axis=0
    )
    other_end = lax.ppermute(attended_end, "tp", swap)
    hidden_end, stats_end = projection(attended_end, other_end, residual_end, REACH, "project_ends")
    other_stats_end = lax.ppermute(stats_end, "tp", swap)

    total = frames + 2 * EDGE
    whole = lambda array: pl.BlockSpec(array.shape, lambda g: (0, 0))
    lane_block = lambda n: pl.BlockSpec((n, LANES), lambda g: (0, g))
    return pl.pallas_call(
        functools.partial(norm_conv, frames),
        grid=(width // LANES,),
        out_shape=jax.ShapeDtypeStruct((frames, width), jnp.bfloat16),
        in_specs=[
            SMEM, SMEM, lane_block(inner), lane_block(ends),
            whole(stats_in), whole(stats_in), whole(stats_end), whole(stats_end),
            lane_block(1), lane_block(KERNEL),
        ],
        out_specs=lane_block(frames),
        scratch_shapes=[
            pltpu.VMEM((total, LANES), jnp.float32),
            pltpu.VMEM((total, LANES), jnp.float32),
            pltpu.VMEM((total, LANES), jnp.float32),
            pltpu.VMEM((total, LANES), jnp.float32),
            pltpu.VMEM((128 + 2 * EDGE, LANES), jnp.float32),
            pltpu.SMEM((frames // 128,), jnp.int32),
        ],
        compiler_params=grid_params,
        name="norm_conv",
    )(
        record_starts, record_lengths, hidden_in, hidden_end, stats_in, other_stats_in, stats_end, other_stats_end,
        norm_gain.reshape(1, width), conv_weight,
    )


def solution(mesh):
    placed = (
        P(("grp", "seq"), "tp"),
        P(("grp", "seq"), "tp"),
        P(("grp", "seq"), "tp"),
        P("tp", None),
        P(("grp", "seq"), "tp"),
        P("tp"),
        P(None, "tp"),
        P("grp"),
        P("grp"),
    )
    return jax.shard_map(
        on_device, mesh=mesh, in_specs=placed, out_specs=P(("grp", "seq"), "tp"), check_vma=False
    )
```

time: 237 us -> 100 us (0.42); the launches traced: 234 us -> 99.7 us
  other arithmetic: 92.5 us -> 0.06 us
  Pallas kernels: 0 us -> 55.7 us
  matrix products: 38.3 us -> 0 us
  local copies, waits for them, and re-layouts: 40.6 us -> 14.7 us
  blocking collectives: 18 us -> 0 us
  between operations: 13.6 us -> 0.14 us
  waiting for transfers between devices: 15.6 us -> 21 us
  starting transfers between devices: 12.5 us -> 8.03 us
  loops' own time: 2.78 us -> 0 us
    convert_element_type x2 -> x0, other arithmetic: 81.4 us -> none  [the longest x1 77.9 us: on_device(): return (hidden_sum + jax.nn.silu(conv_sum)).astype(jnp.bfloat16)]
    pallas_call x0 -> x5, Pallas kernels: none -> 55.7 us  [the longest x1 23.8 us: on_device(): pl.pallas_call(functools.partial(norm_conv, frames), grid=(width // LANES...]
    dot_general x5 -> x0, matrix products: 21.6 us -> none  [the longest x4 11.8 us: attend(): jnp.einsum('hqk,khd->qhd', weights, value_heads, preferred_element_type=j...]
    sub x4 -> x0, matrix products: 16.7 us -> none  [attend(): masked - row_max]
    all_to_all x1 -> x0, blocking collectives: 12.9 us -> none  [on_device(): lax.all_to_all(out_weight, 'tp', split_axis=1, concat_axis=0, tiled=True)]
    slice x7 -> x4, local copies, waits for them, and re-layouts: 11.3 us -> 2.96 us  [the longest x2 1.52 us: edge_rows(): return jnp.concatenate([tail[:EDGE], tail[EDGE:]], axis=1)]
    dynamic_slice x20 -> x0, local copies, waits for them, and re-layouts: 7.93 us -> none  [the longest x8 4.79 us: one_block(): query_block = lax.dynamic_slice_in_dim(queries, block_start, block_rows, 0)]
    all_to_all x1 -> x0, local copies, waits for them, and re-layouts: 6.87 us -> none  [on_device(): lax.all_to_all(out_weight, 'tp', split_axis=1, concat_axis=0, tiled=True)]
  transfers between devices with their start and end apart: 5 -> 7, of which waited for: 3 -> 3; matrix products, arithmetic and copies ran while one was open for 8% -> 6% of each run, Pallas kernels for 0% -> 32%
where the time goes in v1:
time: 100 us; the launch traced here: 99.7 us
  Pallas kernels  55.7 us (56%)
  waiting for transfers between devices  21 us (21%)
  local copies, waits for them, and re-layouts  14.7 us (15%)
  starting transfers between devices  8.03 us (8%)
    pallas_call x1, Pallas kernels, on_device(): pl.pallas_call(functools.partial(norm_conv, frames), grid=(width // LANES...  23.8 us
    ppermute x1, waiting for transfers between devices, on_device(): lax.ppermute(payload(False), 'seq', [(i, i + 1) for i in range(count - 1)])  17.4 us
    pallas_call x2, Pallas kernels, projection(): pl.pallas_call(lambda t_ref, *refs: project(tile, *refs), grid_spec=pltpu...  14.1 us
    unnamed x30, local copies, waits for them, and re-layouts  11.2 us
    pallas_call x1, Pallas kernels, on_device(): pl.pallas_call(functools.partial(attend_inner, frames), grid=(pairs,), ou...  11 us
    pallas_call x1, Pallas kernels, on_device(): pl.pallas_call(functools.partial(attend_ends, frames), grid=(pairs,), out...  6.8 us
    ppermute x1, starting transfers between devices, on_device(): lax.ppermute(payload(False), 'seq', [(i, i + 1) for i in range(count - 1)])  3.14 us
    ppermute x1, starting transfers between devices, on_device(): lax.ppermute(payload(True), 'seq', [(i + 1, i) for i in range(count - 1)])  3.04 us
  transfers between devices with their start and end apart: 7, of which 3 were waited for; matrix products, arithmetic and copies ran while one was open for 6% of the time, Pallas kernels for 32%

profile of v1, /device:TPU:17, one launch (start us, length us, event | category | flops | bytes accessed | tf_op | source)
XLA Modules:
  0.0 99.7 jit_solution(3481241494737455717)
XLA Ops:
  0.0 0.7 collective-permute-start.1
  0.7 1.4 %copy-done = bf16[1024,768]{1,0:T(8,128)(2,1)S(1)} copy-done((bf16[1024,768]{1,0:T(8,128)(2,1)S(1)}, bf16[1024,768]{1,0:T(8,128)(2,1)}, u32[]{:S(2)}) %copy-start) | copy-done | bytes 1572888
  2.1 1.4 %copy-done.2 = bf16[1024,768]{1,0:T(8,128)(2,1)S(1)} copy-done((bf16[1024,768]{1,0:T(8,128)(2,1)S(1)}, bf16[1024,768]{1,0:T(8,128)(2,1)}, u32[]{:S(2)}) %copy-start.2) | copy-done | bytes 1572888
  3.5 1.4 %copy-done.4 = bf16[1024,768]{1,0:T(8,128)(2,1)S(1)} copy-done((bf16[1024,768]{1,0:T(8,128)(2,1)S(1)}, bf16[1024,768]{1,0:T(8,128)(2,1)}, u32[]{:S(2)}) %copy-start.4) | copy-done | bytes 1572888
  4.9 0.7 copy-done.7
  5.6 0.7 copy-done.9
  6.2 11.0 %attend_inner.1.refs_0_ = bf16[768,768]{1,0:T(8,128)(2,1)S(1)} custom-call(s32[8]{0:T(128)S(1)} %copy-done.7, s32[8]{0:T(128)S(1)} %copy-done.9, bf16[1024,768]{1,0:T(8,128)(2,1)S(1)} %copy-done.4, bf16[1024,768]{1,0:T(8,128)(2,1)S(1)} %copy-done, bf16[1024,768]{1,0:T(8,128)(2,1)S(1)} %copy-done.2), custom_call_target="tpu_custom_call" | custom-call | tf_op jit(solution)/shard_map/attend_inner/pallas_call | solution.py:282
  17.3 0.8 slice_dynamic-update-slice_fusion.1
  18.1 0.8 slice_dynamic-update-slice_fusion
  19.5 0.6 slice_dynamic-update-slice_fusion.5
  20.7 3.1 %collective-permute-start.2 = (bf16[336,768]{1,0:T(8,128)(2,1)}, bf16[336,768]{1,0:T(8,128)(2,1)}, u32[]{:S(2)}, u32[]{:S(2)}) collective-permute-start(bf16[336,768]{1,0:T(8,128)(2,1)} %get-tuple-element.16), channel_id=1, source_target_pairs={{0,2},{2,4},{4,6},{6,8},{8,10},{10,12},{12,14},{1,3},{3,5},{5,7},{... | collective-permute-start | bytes 1548296 | tf_op jit(solution)/shard_map/ppermute | solution.py:278
  23.8 3.0 %collective-permute-start.3 = (bf16[336,768]{1,0:T(8,128)(2,1)}, bf16[336,768]{1,0:T(8,128)(2,1)}, u32[]{:S(2)}, u32[]{:S(2)}) collective-permute-start(bf16[336,768]{1,0:T(8,128)(2,1)} %get-tuple-element.15), channel_id=1, source_target_pairs={{2,0},{4,2},{6,4},{8,6},{10,8},{12,10},{14,12},{3,1},{5,3},{7,5},{... | collective-permute-start | bytes 1548296 | tf_op jit(solution)/shard_map/ppermute | solution.py:277
  27.1 1.3 %fusion = (bf16[128,1536]{1,0:T(8,128)(2,1)S(1)}, bf16[128,1536]{1,0:T(8,128)(2,1)S(1)}) fusion(bf16[1024,1536]{1,0:T(8,128)(2,1)} %param.13), kind=kLoop, calls=%fused_computation.11 | loop fusion | bytes 1572864 | tf_op jit(solution)/shard_map/slice | solution.py:347
  28.4 17.4 %collective-permute-done.2.before_ref = bf16[336,768]{1,0:T(8,128)(2,1)} collective-permute-done((bf16[336,768]{1,0:T(8,128)(2,1)}, bf16[336,768]{1,0:T(8,128)(2,1)}, u32[]{:S(2)}, u32[]{:S(2)}) %collective-permute-start.2) | collective-permute-done | bytes 516128 | tf_op jit(solution)/shard_map/ppermute | solution.py:278
  45.8 2.7 %collective-permute-done.3.after_ref = bf16[336,768]{1,0:T(8,128)(2,1)} collective-permute-done((bf16[336,768]{1,0:T(8,128)(2,1)}, bf16[336,768]{1,0:T(8,128)(2,1)}, u32[]{:S(2)}, u32[]{:S(2)}) %collective-permute-start.3) | collective-permute-done | bytes 516128 | tf_op jit(solution)/shard_map/ppermute | solution.py:277
  48.6 1.4 %copy-done.3 = bf16[1024,768]{1,0:T(8,128)(2,1)S(1)} copy-done((bf16[1024,768]{1,0:T(8,128)(2,1)S(1)}, bf16[1024,768]{1,0:T(8,128)(2,1)}, u32[]{:S(2)}) %copy-start.3) | copy-done | bytes 1572888
  50.0 1.4 %copy-done.5 = bf16[1024,768]{1,0:T(8,128)(2,1)S(1)} copy-done((bf16[1024,768]{1,0:T(8,128)(2,1)S(1)}, bf16[1024,768]{1,0:T(8,128)(2,1)}, u32[]{:S(2)}) %copy-start.5) | copy-done | bytes 1572888
  51.4 6.8 %attend_ends.1.refs_0_ = bf16[288,768]{1,0:T(8,128)(2,1)S(1)} custom-call(s32[8]{0:T(128)S(1)} %copy-done.8, s32[8]{0:T(128)S(1)} %copy-done.10, bf16[1024,768]{1,0:T(8,128)(2,1)S(1)} %copy-done.5, bf16[1024,768]{1,0:T(8,128)(2,1)S(1)} %copy-done.1, bf16[1024,768]{1,0:T(8,128)(2,1)S(1)} %copy-done.3, bf16[336,768]{1,0:T(8,128)(2,1)} %collective-permute-done.2.before_ref, ...), custom_call_target="tpu_custom_call" | custom-call | tf_op jit(solution)/shard_map/attend_ends/pallas_call | solution.py:297
  58.7 0.8 fusion.2
  59.5 0.8 fusion.1
  60.3 9.4 %project_inner.1 = (f32[768,1536]{1,0:T(8,128)}, f32[16,768]{1,0:T(8,128)S(1)}) custom-call(s32[1]{0:T(128)} %bitcast.t_ref, bf16[768,768]{1,0:T(8,128)(2,1)S(1)} %attend_inner.1.refs_0_, bf16[768,768]{1,0:T(8,128)(2,1)} %collective-permute-done.refs_1_, bf16[768,3072]{1,0:T(8,128)(2,1)} %refs_2_.3, bf16[768,3072]{1,0:T(8,128)(2,1)} %collective-permute-done.1.refs_3_, ...), custom_call_target="tpu_custom_call" | custom-call | tf_op jit(solution)/shard_map/project_inner/pallas_call | solution.py:313
  69.8 4.7 %project_ends.1 = (f32[288,1536]{1,0:T(8,128)S(1)}, f32[16,512]{1,0:T(8,128)S(1)}) custom-call(s32[1]{0:T(128)} %bitcast.t_ref, bf16[288,768]{1,0:T(8,128)(2,1)S(1)} %attend_ends.1.refs_0_, bf16[288,768]{1,0:T(8,128)(2,1)S(1)} %collective-permute-done.4.refs_1_, bf16[768,3072]{1,0:T(8,128)(2,1)} %refs_2_.3, ...), custom_call_target="tpu_custom_call" | custom-call | tf_op jit(solution)/shard_map/project_ends/pallas_call | solution.py:313
  75.0 0.8 collective-permute-done.6.t_end_ref
  75.9 23.8 %norm_conv.1 = bf16[1024,1536]{1,0:T(8,128)(2,1)} custom-call(s32[8]{0:T(128)S(1)} %copy-done.8, s32[8]{0:T(128)S(1)} %copy-done.10, f32[768,1536]{1,0:T(8,128)} %get-tuple-element.9.h_in_ref, f32[288,1536]{1,0:T(8,128)S(1)} %get-tuple-element.10.h_end_ref, f32[16,768]{1,0:T(8,128)S(1)} %get-tuple-element.11.s_in_ref, ...), custom_call_target="tpu_custom_call" | custom-call | tf_op jit(solution)/shard_map/norm_conv/pallas_call | solution.py:356
  (32 shorter events, 2.7 us)
Async XLA Ops:
  0.0 60.3 %collective-permute-start.1 = (bf16[768,3072]{1,0:T(8,128)(2,1)}, bf16[768,3072]{1,0:T(8,128)(2,1)}, u32[]{:S(2)}, u32[]{:S(2)}) collective-permute-start(bf16[768,3072]{1,0:T(8,128)(2,1)} %refs_2_.3), channel_id=1, source_target_pairs={{0,1},{1,0},{2,3},{3,2},{4,5},{5,4},{6,7},{7,6},{8,9},{9,8},{10,11... | collective-permute-start | bytes 14155784 | tf_op jit(solution)/shard_map/ppermute | solution.py:279
  0.7 1.4 %copy-start = (bf16[1024,768]{1,0:T(8,128)(2,1)S(1)}, bf16[1024,768]{1,0:T(8,128)(2,1)}, u32[]{:S(2)}) copy-start(bf16[1024,768]{1,0:T(8,128)(2,1)} %k_ref.3) | copy-start | bytes 4718596
  2.1 1.4 %copy-start.2 = (bf16[1024,768]{1,0:T(8,128)(2,1)S(1)}, bf16[1024,768]{1,0:T(8,128)(2,1)}, u32[]{:S(2)}) copy-start(bf16[1024,768]{1,0:T(8,128)(2,1)} %v_ref.3) | copy-start | bytes 4718596
  3.5 1.4 %copy-start.4 = (bf16[1024,768]{1,0:T(8,128)(2,1)S(1)}, bf16[1024,768]{1,0:T(8,128)(2,1)}, u32[]{:S(2)}) copy-start(bf16[1024,768]{1,0:T(8,128)(2,1)} %q_ref.3) | copy-start | bytes 4718596
  4.9 0.7 copy-start.7
  5.6 0.7 copy-start.9
  6.2 13.3 %copy-start.11 = (bf16[1024,1536]{1,0:T(8,128)(2,1)S(1)}, bf16[1024,1536]{1,0:T(8,128)(2,1)}, u32[]{:S(2)}) copy-start(bf16[1024,1536]{1,0:T(8,128)(2,1)} %param.13) | copy-start | bytes 9437188
  17.2 43.0 %collective-permute-start = (bf16[768,768]{1,0:T(8,128)(2,1)S(1)}, bf16[768,768]{1,0:T(8,128)(2,1)}, u32[]{:S(2)}, u32[]{:S(2)}) collective-permute-start(bf16[768,768]{1,0:T(8,128)(2,1)S(1)} %attend_inner.1.refs_0_), channel_id=1, source_target_pairs={{0,1},{1,0},{2,3},{3,2},{4,5},{5,4},{6,7},{7,6},{8,9},{9,8},{10,11... | collective-permute-start | bytes 3538952 | tf_op jit(solution)/shard_map/ppermute | solution.py:338
  20.7 25.1 %collective-permute-start.2 = (bf16[336,768]{1,0:T(8,128)(2,1)}, bf16[336,768]{1,0:T(8,128)(2,1)}, u32[]{:S(2)}, u32[]{:S(2)}) collective-permute-start(bf16[336,768]{1,0:T(8,128)(2,1)} %get-tuple-element.16), channel_id=1, source_target_pairs={{0,2},{2,4},{4,6},{6,8},{8,10},{10,12},{12,14},{1,3},{3,5},{5,7},{... | collective-permute-start | bytes 1548296 | tf_op jit(solution)/shard_map/ppermute | solution.py:278
  23.8 24.7 %collective-permute-start.3 = (bf16[336,768]{1,0:T(8,128)(2,1)}, bf16[336,768]{1,0:T(8,128)(2,1)}, u32[]{:S(2)}, u32[]{:S(2)}) collective-permute-start(bf16[336,768]{1,0:T(8,128)(2,1)} %get-tuple-element.15), channel_id=1, source_target_pairs={{2,0},{4,2},{6,4},{8,6},{10,8},{12,10},{14,12},{3,1},{5,3},{7,5},{... | collective-permute-start | bytes 1548296 | tf_op jit(solution)/shard_map/ppermute | solution.py:277
  26.9 21.6 %copy-start.8 = (s32[8]{0:T(128)S(1)}, s32[8]{0:T(128)}, u32[]{:S(2)}) copy-start(s32[8]{0:T(128)} %starts_ref.5) | copy-start | bytes 100
  26.9 21.6 %copy-start.10 = (s32[8]{0:T(128)S(1)}, s32[8]{0:T(128)}, u32[]{:S(2)}) copy-start(s32[8]{0:T(128)} %lengths_ref.5) | copy-start | bytes 100
  27.1 21.5 %copy-start.1 = (bf16[1024,768]{1,0:T(8,128)(2,1)S(1)}, bf16[1024,768]{1,0:T(8,128)(2,1)}, u32[]{:S(2)}) copy-start(bf16[1024,768]{1,0:T(8,128)(2,1)} %k_ref.3) | copy-start | bytes 4718596
  48.5 1.4 %copy-start.3 = (bf16[1024,768]{1,0:T(8,128)(2,1)S(1)}, bf16[1024,768]{1,0:T(8,128)(2,1)}, u32[]{:S(2)}) copy-start(bf16[1024,768]{1,0:T(8,128)(2,1)} %v_ref.3) | copy-start | bytes 4718596
  50.0 1.4 %copy-start.5 = (bf16[1024,768]{1,0:T(8,128)(2,1)S(1)}, bf16[1024,768]{1,0:T(8,128)(2,1)}, u32[]{:S(2)}) copy-start(bf16[1024,768]{1,0:T(8,128)(2,1)} %q_ref.3) | copy-start | bytes 4718596
  58.2 11.6 %collective-permute-start.4 = (bf16[288,768]{1,0:T(8,128)(2,1)S(1)}, bf16[288,768]{1,0:T(8,128)(2,1)S(1)}, u32[]{:S(2)}, u32[]{:S(2)}) collective-permute-start(bf16[288,768]{1,0:T(8,128)(2,1)S(1)} %attend_ends.1.refs_0_), channel_id=1, source_target_pairs={{0,1},{1,0},{2,3},{3,2},{4,5},{5,4},{6,7},{7,6},{8,9},{9,8},{10,11... | collective-permute-start | bytes 1327112 | tf_op jit(solution)/shard_map/ppermute | solution.py:349
  69.6 6.2 %collective-permute-start.5 = (f32[16,768]{1,0:T(8,128)S(1)}, f32[16,768]{1,0:T(8,128)S(1)}, u32[]{:S(2)}, u32[]{:S(2)}) collective-permute-start(f32[16,768]{1,0:T(8,128)S(1)} %get-tuple-element.11.s_in_ref), channel_id=1, source_target_pairs={{0,1},{1,0},{2,3},{3,2},{4,5},{5,4},{6,7},{7,6},{8,9},{9,8},{10,11... | collective-permute-start | bytes 147464 | tf_op jit(solution)/shard_map/ppermute | solution.py:340
  69.7 5.3 %copy-start.12 = (f32[1536]{0:T(1024)S(1)}, f32[1536]{0:T(1024)}, u32[]{:S(2)}) copy-start(f32[1536]{0:T(1024)} %param.14) | copy-start | bytes 18436
  69.7 6.2 %copy-start.6 = (f32[31,1536]{1,0:T(8,128)S(1)}, f32[31,1536]{1,0:T(8,128)}, u32[]{:S(2)}) copy-start(f32[31,1536]{1,0:T(8,128)} %w_ref.1) | copy-start | bytes 571396
  74.5 1.4 %collective-permute-start.6 = (f32[16,512]{1,0:T(8,128)S(1)}, f32[16,512]{1,0:T(8,128)S(1)}, u32[]{:S(2)}, u32[]{:S(2)}) collective-permute-start(f32[16,512]{1,0:T(8,128)S(1)} %get-tuple-element.12.s_end_ref), channel_id=1, source_target_pairs={{0,1},{1,0},{2,3},{3,2},{4,5},{5,4},{6,7},{7,6},{8,9},{9,8},{10,11... | collective-permute-start | bytes 98312 | tf_op jit(solution)/shard_map/ppermute | solution.py:351

commit v2 on v1

v2 whole, which is shorter than its diff:
```python
import functools

import jax
import jax.numpy as jnp
from jax import lax
from jax.experimental import pallas as pl
from jax.experimental.pallas import tpu as pltpu
from jax.sharding import PartitionSpec as P

D = 3072
HSIZE = 64
WIN = 128
KHALF = 15
REC = 8
KERNEL = 31
EDGE = 16
REACH = WIN + EDGE
SPAN = 512
LANES = 128
NEG = -1e30
EXP_SCALE = HSIZE ** (-0.5) * 1.4426950408889634
SMEM = pl.BlockSpec(memory_space=pltpu.SMEM)


def row_bounds(positions, starts_ref, lengths_ref):
    first = jnp.full(positions.shape, -1, jnp.int32)
    last = jnp.full(positions.shape, -2, jnp.int32)
    for r in range(REC):
        start = starts_ref[r]
        end = start + lengths_ref[r]
        inside = (positions >= start) & (positions < end)
        first = jnp.where(inside, start, first)
        last = jnp.where(inside, end - 1, last)
    return first, last


def as_column(row):
    return jnp.transpose(jnp.broadcast_to(row, (LANES, LANES)))


def band_bias(base, rows, key_base, keys, starts_ref, lengths_ref, store):
    for top in range(0, rows, LANES):
        count = min(LANES, rows - top)
        positions = base + top + lax.broadcasted_iota(jnp.int32, (1, LANES), 1)
        first, last = row_bounds(positions, starts_ref, lengths_ref)
        inside = first >= 0
        low = jnp.where(inside, jnp.maximum(first, positions - WIN), 0)
        high = jnp.where(inside, jnp.minimum(last, positions + WIN), -1)
        low = as_column(low.astype(jnp.float32))
        high = as_column(high.astype(jnp.float32))
        for left in range(0, keys, LANES):
            key_at = (key_base + left + lax.broadcasted_iota(jnp.int32, (LANES, LANES), 1)).astype(jnp.float32)
            bias = jnp.where((key_at >= low) & (key_at <= high), jnp.float32(0.0), jnp.float32(NEG))
            store(top, count, left, bias[:count])


def head_pair(query, keys, values, bias):
    rows = query.shape[0]
    left = lax.broadcasted_iota(jnp.int32, query.shape, 1) < HSIZE
    nothing = jnp.zeros_like(query)
    both = jnp.concatenate([jnp.where(left, query, nothing), jnp.where(left, nothing, query)], axis=0)
    scores = lax.dot_general(both, keys, (((1,), (1,)), ((), ())), preferred_element_type=jnp.float32)
    scores = scores + jnp.concatenate([bias, bias], axis=0)
    row_max = jnp.max(scores, axis=1, keepdims=True)
    weights = jnp.exp2((scores - row_max) * EXP_SCALE).astype(jnp.bfloat16)
    mixed = jnp.dot(weights, values, preferred_element_type=jnp.float32)
    mixed = mixed[:, :LANES] / mixed[:, LANES:]
    keep = bias_any(bias)
    return jnp.where(keep, jnp.where(left, mixed[:rows], mixed[rows:]), 0.0).astype(jnp.bfloat16)


def bias_any(bias):
    return jnp.max(bias, axis=1, keepdims=True) > NEG / 2


def attend_inner(frames, starts_ref, lengths_ref, q_ref, k_ref, v_ref, o_ref, bias, wide):
    blocks = frames // WIN - 2
    anchor = lax.axis_index("seq") * frames

    @pl.when(pl.program_id(0) == 0)
    def _():
        wide[:, LANES:] = jnp.ones((frames, LANES), jnp.bfloat16)
        for i in range(blocks):
            def store(top, count, left, value):
                bias[i, top : top + count, left : left + LANES] = value

            band_bias(anchor + (i + 1) * WIN, WIN, anchor + i * WIN, 3 * WIN, starts_ref, lengths_ref, store)

    wide[:, :LANES] = v_ref[...]
    for i in range(blocks):
        window = slice(i * WIN, (i + 3) * WIN)
        o_ref[i * WIN : (i + 1) * WIN, :] = head_pair(
            q_ref[(i + 1) * WIN : (i + 2) * WIN, :], k_ref[window, :], wide[window, :], bias[i]
        )


def attend_ends(frames, starts_ref, lengths_ref, q_ref, k_ref, v_ref, before_ref, after_ref, o_ref, bias):
    anchor = lax.axis_index("seq") * frames
    own = SPAN - REACH

    @pl.when(pl.program_id(0) == 0)
    def _():
        for i, (base, key_base) in enumerate(((-EDGE, -REACH), (frames - WIN, frames - own))):
            def store(top, count, left, value):
                bias[i, top : top + count, left : left + LANES] = value

            band_bias(anchor + base, REACH, anchor + key_base, SPAN, starts_ref, lengths_ref, store)

    ones = jnp.ones((SPAN, LANES), jnp.bfloat16)
    for i in range(2):
        halo = (before_ref, after_ref)[i]
        mine = slice(0, own) if i == 0 else slice(frames - own, frames)

        def joined(far, near):
            return jnp.concatenate([far, near] if i == 0 else [near, far], axis=0)

        keys = joined(halo[3 * EDGE : 3 * EDGE + REACH, :], k_ref[mine, :])
        values = joined(halo[3 * EDGE + REACH :, :], v_ref[mine, :])
        query = joined(halo[2 * EDGE : 3 * EDGE, :], q_ref[:WIN, :] if i == 0 else q_ref[frames - WIN :, :])
        o_ref[i * REACH : (i + 1) * REACH, :] = head_pair(
            query, keys, jnp.concatenate([values, ones], axis=1), bias[i]
        )


def pack_edges(frames, q_ref, k_ref, v_ref, r_ref, top_ref, bottom_ref, sems):
    half = q_ref.shape[1]
    copies = []
    for i, out in enumerate((top_ref, bottom_ref)):
        def rows(ref, n):
            return ref.at[pl.ds(0 if i == 0 else frames - n, n), :]

        moves = [
            (r_ref.at[pl.ds(0 if i == 0 else frames - EDGE, EDGE), pl.ds(0, half)], 0, EDGE),
            (r_ref.at[pl.ds(0 if i == 0 else frames - EDGE, EDGE), pl.ds(half, half)], EDGE, EDGE),
            (rows(q_ref, EDGE), 2 * EDGE, EDGE),
            (rows(k_ref, REACH), 3 * EDGE, REACH),
            (rows(v_ref, REACH), 3 * EDGE + REACH, REACH),
        ]
        for n, (source, at, count) in enumerate(moves):
            copies.append(pltpu.make_async_copy(source, out.at[pl.ds(at, count), :], sems.at[i, n]))
    for copy in copies:
        copy.start()
    for copy in copies:
        copy.wait()


def project(own_ref, other_ref, w_own_ref, w_other_ref, residual, h_ref, stats_ref, shift, first, second, tiles, total_width):
    step = pl.program_id(tiles[0])
    rows, width = h_ref.shape
    part = jnp.dot(own_ref[...], w_own_ref[...], preferred_element_type=jnp.float32)
    part = part + jnp.dot(other_ref[...], w_other_ref[...], preferred_element_type=jnp.float32)
    part = part + residual
    h_ref[...] = part

    @pl.when(step == 0)
    def _():
        mean = jnp.sum(part, axis=1, keepdims=True) * (1.0 / width)
        shift[...] = jnp.broadcast_to(mean, (rows, LANES))
        first[...] = jnp.zeros_like(first)
        second[...] = jnp.zeros_like(second)

    one, two = first[...], second[...]
    for l in range(0, width, LANES):
        off = part[:, l : l + LANES] - shift[...]
        one = one + off
        two = two + off * off
    first[...] = one
    second[...] = two

    @pl.when(step == tiles[1] - 1)
    def _():
        moved = jnp.sum(first[...], axis=1, keepdims=True) * (1.0 / total_width)
        mean = shift[...] + moved
        square = jnp.sum(second[...], axis=1, keepdims=True) - moved * moved * total_width
        for top in range(0, rows, LANES):
            count = min(LANES, rows - top)
            for k, column in enumerate((mean, jnp.broadcast_to(square, (rows, LANES)))):
                tile = column[top : top + count]
                if count < LANES:
                    tile = jnp.concatenate([tile, jnp.zeros((LANES - count, LANES), jnp.float32)], axis=0)
                stats_ref[8 * k : 8 * k + 8, top : top + LANES] = jnp.transpose(tile)[:8, :]


def project_inner(tiles, t_ref, own, other, w_own, w_other, res, h_ref, stats, shift, first, second):
    top = WIN
    project(
        own, other, w_own, w_other, res[top : top + h_ref.shape[0], :].astype(jnp.float32),
        h_ref, stats, shift, first, second, (0, tiles), float(tiles * h_ref.shape[1]),
    )


def project_ends(tiles, t_ref, own, other, w_own, w_other, res, before, after, h_ref, stats, shift, first, second):
    frames = res.shape[0]
    residual = jnp.concatenate([before[...], res[:WIN, :], res[frames - WIN :, :], after[...]], axis=0)
    project(
        own, other, w_own, w_other, residual.astype(jnp.float32),
        h_ref, stats, shift, first, second, (0, tiles), float(tiles * h_ref.shape[1]),
    )


def stat_columns(base, own, other, width, starts_ref, lengths_ref):
    positions = base + lax.broadcasted_iota(jnp.int32, (1, LANES), 1)
    index = jnp.zeros((1, LANES), jnp.int32) - 1
    for r in range(REC):
        start = starts_ref[r]
        inside = (positions >= start) & (positions < start + lengths_ref[r])
        index = jnp.where(inside, r, index)
    gap = own[0:1, :] - other[0:1, :]
    middle = 0.5 * (own[0:1, :] + other[0:1, :])
    var = (own[8:9, :] + other[8:9, :] + gap * gap * (width * 0.25)) * (1.0 / width)
    inverse = jnp.where(index >= 0, lax.rsqrt(var + 1e-5), 0.0)
    parity = jnp.where(index >= 0, (index % 2).astype(jnp.float32), -1.0)
    return as_column(middle), as_column(inverse), as_column(parity)


def mark_mixed(base, chunks, flags, at, starts_ref, lengths_ref):
    flags[at] = jnp.int32(0)
    for r in range(REC - 1):
        end, start = starts_ref[r] + lengths_ref[r], starts_ref[r + 1]
        low = jnp.maximum((end - KHALF - base) >> 4, 0)
        high = jnp.minimum((start + KHALF - base + EDGE - 1) >> 4, chunks)

        @pl.when(start - end < KHALF)
        def _():
            def add(c, carry):
                known = flags[at]
                flags[at + 1 + known] = c
                flags[at] = known + 1
                return carry

            lax.fori_loop(low, high, add, 0)


def convolve(load, w_ref):
    acc = load(0) * w_ref[0:1, :]
    for tap in range(1, KERNEL):
        acc = acc + load(tap) * w_ref[tap : tap + 1, :]
    return acc


def differences(x_ref, diffs):
    rows = x_ref.shape[0]
    x = x_ref[...]
    near = x[: rows - 8] - x[8:]
    diffs[0, : rows - 8, :] = near
    diffs[1, : rows - 16, :] = x[: rows - 16] - x[16:]
    diffs[2, : rows - 24, :] = near[: rows - 24] - near[16:]


def tap_sums(w_ref, wq):
    padded = jnp.concatenate([jnp.zeros((1, LANES), jnp.float32), w_ref[...]], axis=0)
    w0, w1, w2, w3 = (padded[8 * j : 8 * j + 8] for j in range(4))
    for n, value in enumerate((w0, w0 + w1, -w1, w0 + w2, w0 + w1 + w2 + w3, -(w1 + w3), -w2, -(w2 + w3), w3)):
        wq[n] = value


def conv_group(x_ref, diffs, wq, at):
    sources = (
        (diffs.at[2], 0), (diffs.at[1], 8), (diffs.at[2], 8),
        (diffs.at[0], 16), (x_ref, 24), (diffs.at[0], 24),
        (diffs.at[2], 16), (diffs.at[1], 24), (diffs.at[2], 24),
    )
    sums = [None] * 9
    for s in range(8):
        for n, (ref, off) in enumerate(sources):
            first = at - EDGE + s + off
            term = ref[first : first + 8, :] * wq[n, s : s + 1, :]
            sums[n] = term if sums[n] is None else sums[n] + term
    a0, a1 = sums[1] + sums[0], sums[1] + sums[2]
    p0, p1 = sums[4] + sums[3], sums[4] + sums[5]
    c0, c1 = sums[7] + sums[6], sums[7] + sums[8]
    return jnp.concatenate([a0 + p0, a1 + p1, p0 + c0, p1 + c1], axis=0)


def silu_add(hidden, conv_sum):
    half = conv_sum * 0.5
    return (hidden + (half + half * jnp.tanh(half))).astype(jnp.bfloat16)


def conv_rows(rows, hidden, normed, parity, diffs, wq, masked, flags, flag_at, w_ref, out):
    differences(normed, diffs)
    group = 2 * EDGE
    for top in list(range(0, rows - group, group)) + [rows - group]:
        at = top + EDGE
        conv_sum = conv_group(normed, diffs, wq, at)
        conv_sum = jnp.where(parity[at : at + group, :] >= 0, conv_sum, 0.0)
        out[top : top + group, :] = silu_add(hidden[at : at + group, :], conv_sum)

    def again(c, carry):
        top = pl.multiple_of(flags[flag_at + 1 + c] * EDGE, EDGE)
        around, here = pl.ds(top, 3 * EDGE), pl.ds(top + EDGE, EDGE)
        conv_sum = jnp.zeros((EDGE, LANES), jnp.float32)
        for side in range(2):
            masked[...] = jnp.where(parity[around, :] == side, normed[around, :], 0.0)
            first = EDGE - KHALF
            part = convolve(lambda tap: masked[first + tap : first + tap + EDGE, :], w_ref)
            conv_sum = jnp.where(parity[here, :] == side, part, conv_sum)
        out[pl.ds(top, EDGE), :] = silu_add(hidden[here, :], conv_sum)
        return carry

    lax.fori_loop(0, flags[flag_at], again, 0)


def norm_conv_inner(
    frames, starts_ref, lengths_ref, h_ref, own_ref, other_ref, gain_ref, w_ref, o_ref,
    mean, scale, parity, normed, diffs, wq, masked, out, flags, sems,
):
    step, steps = pl.program_id(0), pl.num_programs(0)
    rows = frames - 2 * WIN
    kept = rows - 2 * EDGE
    base = lax.axis_index("seq") * frames + WIN

    @pl.when(step == 0)
    def _():
        width = 2.0 * LANES * steps
        for top in range(0, rows, LANES):
            here = slice(top, top + LANES)
            mean[here, :], scale[here, :], parity[here, :] = stat_columns(
                base + top, own_ref[:, here], other_ref[:, here], width, starts_ref, lengths_ref
            )
        mark_mixed(base + EDGE, kept // EDGE, flags, 0, starts_ref, lengths_ref)

    value = (h_ref[...] - mean[...]) * scale[...] * gain_ref[...]
    normed[...] = value.astype(jnp.bfloat16).astype(jnp.float32)
    slot = step % 2

    def copy(at, which):
        return pltpu.make_async_copy(
            out.at[which], o_ref.at[pl.ds(WIN + EDGE, kept), pl.ds(pl.multiple_of(at * LANES, LANES), LANES)], sems.at[which]
        )

    @pl.when(step >= 2)
    def _():
        copy(step - 2, slot).wait()

    tap_sums(w_ref, wq)
    conv_rows(kept, h_ref, normed, parity, diffs, wq, masked, flags, 0, w_ref, out.at[slot])
    copy(step, slot).start()

    @pl.when(step == steps - 1)
    def _():
        copy(step - 1, 1 - slot).wait()
        copy(step, slot).wait()


def norm_conv_ends(
    frames, starts_ref, lengths_ref, h_end_ref, h_low_ref, h_high_ref, s_end_ref, t_end_ref, s_in_ref, t_in_ref,
    gain_ref, w_ref, done_ref, o_ref, mean, scale, parity, hidden, normed, diffs, wq, masked, out, flags, sems,
):
    step, steps = pl.program_id(0), pl.num_programs(0)
    inner = frames - 2 * WIN
    anchor = lax.axis_index("seq") * frames
    more = 2 * EDGE
    rows = REACH + more

    @pl.when(step == 0)
    def _():
        width = 2.0 * LANES * steps

        def place(i, at, count, base, lane, own, other, skip):
            values = stat_columns(
                base, own[:, lane : lane + LANES], other[:, lane : lane + LANES], width, starts_ref, lengths_ref
            )
            for ref, value in zip((mean, scale, parity), values):
                ref[i, at : at + count, :] = value[skip : skip + count]

        for top, count in ((0, LANES), (LANES, EDGE)):
            place(0, top, count, anchor - EDGE + top, top, s_end_ref, t_end_ref, 0)
        place(0, REACH, more, anchor + WIN, 0, s_in_ref, t_in_ref, 0)
        place(1, 0, more, anchor + frames - 2 * WIN, inner - LANES, s_in_ref, t_in_ref, LANES - more)
        own = jnp.concatenate([s_end_ref[:, LANES : 2 * LANES], s_end_ref[:, 2 * LANES :]], axis=1)[:, EDGE : EDGE + 2 * LANES - EDGE]
        other = jnp.concatenate([t_end_ref[:, LANES : 2 * LANES], t_end_ref[:, 2 * LANES :]], axis=1)[:, EDGE : EDGE + 2 * LANES - EDGE]
        place(1, more, LANES, anchor + frames - WIN, 0, own, other, 0)
        tail = jnp.concatenate([s_end_ref[:, 2 * LANES + EDGE :], jnp.zeros((16, LANES), jnp.float32)], axis=1)
        tail2 = jnp.concatenate([t_end_ref[:, 2 * LANES + EDGE :], jnp.zeros((16, LANES), jnp.float32)], axis=1)
        place(1, more + LANES, EDGE, anchor + frames, 0, tail, tail2, 0)
        for i in range(2):
            mark_mixed(anchor + i * (frames - REACH), REACH // EDGE, flags, i * 64, starts_ref, lengths_ref)

    hidden[0, :REACH, :] = h_end_ref[:REACH, :]
    hidden[0, REACH:, :] = h_low_ref[...]
    hidden[1, :more, :] = h_high_ref[...]
    hidden[1, more:, :] = h_end_ref[REACH:, :]
    slot = step % 2

    def copies(at, which):
        lanes = pl.ds(pl.multiple_of(at * LANES, LANES), LANES)
        return [
            pltpu.make_async_copy(
                out.at[which, i], o_ref.at[pl.ds(i * (frames - REACH), REACH), lanes], sems.at[which, i]
            )
            for i in range(2)
        ]

    @pl.when(step >= 2)
    def _():
        for copy in copies(step - 2, slot):
            copy.wait()

    tap_sums(w_ref, wq)
    for i in range(2):
        value = (hidden[i] - mean[i]) * scale[i] * gain_ref[...]
        normed[i] = value.astype(jnp.bfloat16).astype(jnp.float32)
        conv_rows(
            REACH, hidden.at[i], normed.at[i], parity.at[i], diffs.at[i], wq, masked, flags, i * 64, w_ref, out.at[slot, i]
        )
    for copy in copies(step, slot):
        copy.start()

    @pl.when(step == steps - 1)
    def _():
        for copy in copies(step - 1, 1 - slot) + copies(step, slot):
            copy.wait()


def cost(microseconds):
    return pl.CostEstimate(flops=int(microseconds * 4e8), bytes_accessed=1000, transcendentals=0)


def params(mebibytes):
    return pltpu.CompilerParams(vmem_limit_bytes=mebibytes * 2**20)


def on_device(
    queries, attn_keys, attn_values, out_weight, residual, norm_gain, conv_weight, record_starts, record_lengths
):
    frames, heads_width = queries.shape
    width = residual.shape[1]
    pairs = heads_width // LANES
    inner = frames - 2 * WIN
    ends = 2 * REACH
    count = lax.axis_size("seq")
    swap = [(0, 1), (1, 0)]
    anywhere = pl.BlockSpec(memory_space=pl.ANY)

    edges = jax.ShapeDtypeStruct((3 * EDGE + 2 * REACH, heads_width), jnp.bfloat16)
    top_edge, bottom_edge = pl.pallas_call(
        functools.partial(pack_edges, frames),
        out_shape=[edges, edges],
        in_specs=[pl.BlockSpec(memory_space=pltpu.HBM)] * 4,
        out_specs=[pl.BlockSpec(memory_space=pltpu.VMEM)] * 2,
        scratch_shapes=[pltpu.SemaphoreType.DMA((2, 5))],
        compiler_params=params(60),
        name="pack_edges",
    )(queries, attn_keys, attn_values, residual)
    top_edge, bottom_edge, queries = lax.optimization_barrier((top_edge, bottom_edge, queries))
    after = lax.ppermute(top_edge, "seq", [(i + 1, i) for i in range(count - 1)])
    before = lax.ppermute(bottom_edge, "seq", [(i, i + 1) for i in range(count - 1)])
    weight_other = lax.ppermute(out_weight, "tp", swap)

    column = pl.BlockSpec((frames, LANES), lambda p: (0, p))
    attended_in = pl.pallas_call(
        functools.partial(attend_inner, frames),
        grid=(pairs,),
        out_shape=jax.ShapeDtypeStruct((inner, heads_width), jnp.bfloat16),
        in_specs=[SMEM, SMEM, column, column, column],
        out_specs=pl.BlockSpec((inner, LANES), lambda p: (0, p)),
        scratch_shapes=[
            pltpu.VMEM((inner // WIN, WIN, 3 * WIN), jnp.float32),
            pltpu.VMEM((frames, 2 * LANES), jnp.bfloat16),
        ],
        compiler_params=params(16),
        cost_estimate=cost(0.2),
        name="attend_inner",
    )(record_starts, record_lengths, queries, attn_keys, attn_values)

    mine = lax.axis_index("tp").astype(jnp.int32).reshape(1)
    step = 256
    tiles = width // step

    def projection(body, own, other, extra, extra_specs, microseconds, name):
        rows = own.shape[0]
        padded = -(-rows // LANES) * LANES
        return pl.pallas_call(
            functools.partial(body, tiles),
            grid_spec=pltpu.PrefetchScalarGridSpec(
                num_scalar_prefetch=1,
                grid=(tiles,),
                in_specs=[
                    pl.BlockSpec((rows, heads_width), lambda j, t: (0, 0)),
                    pl.BlockSpec((rows, heads_width), lambda j, t: (0, 0)),
                    pl.BlockSpec((heads_width, step), lambda j, t: (0, t[0] * tiles + j)),
                    pl.BlockSpec((heads_width, step), lambda j, t: (0, t[0] * tiles + j)),
                    pl.BlockSpec((frames, step), lambda j, t: (0, j)),
                ]
                + extra_specs,
                out_specs=[
                    pl.BlockSpec((rows, step), lambda j, t: (0, j)),
                    pl.BlockSpec((16, padded), lambda j, t: (0, 0)),
                ],
                scratch_shapes=[pltpu.VMEM((rows, LANES), jnp.float32)] * 3,
            ),
            out_shape=[
                jax.ShapeDtypeStruct((rows, width), jnp.float32),
                jax.ShapeDtypeStruct((16, padded), jnp.float32),
            ],
            compiler_params=params(20),
            cost_estimate=cost(microseconds),
            name=name,
        )(mine, own, other, out_weight, weight_other, residual, *extra)

    other_in = lax.ppermute(attended_in, "tp", swap)
    hidden_in, stats_in = projection(project_inner, attended_in, other_in, [], [], 0.2, "project_inner")
    other_stats_in = lax.ppermute(stats_in, "tp", swap)

    whole = lambda array: pl.BlockSpec(array.shape, lambda g: (0, 0))
    lane_block = lambda n, i=0: pl.BlockSpec((n, LANES), lambda g: (i, g))
    gain = norm_gain.reshape(1, width)
    shared = lambda n: pltpu.VMEM(n + (LANES,), jnp.float32)
    kept = inner - 2 * EDGE
    result = jax.ShapeDtypeStruct((frames, width), jnp.bfloat16)
    partly = pl.pallas_call(
        functools.partial(norm_conv_inner, frames),
        grid=(width // LANES,),
        out_shape=result,
        in_specs=[SMEM, SMEM, lane_block(inner), whole(stats_in), whole(stats_in), lane_block(1), lane_block(KERNEL)],
        out_specs=anywhere,
        scratch_shapes=[
            shared((inner,)), shared((inner,)), shared((inner,)), shared((inner,)), shared((3, inner)), shared((9, 8)),
            shared((3 * EDGE,)),
            pltpu.VMEM((2, kept, LANES), jnp.bfloat16),
            pltpu.SMEM((64,), jnp.int32),
            pltpu.SemaphoreType.DMA((2,)),
        ],
        compiler_params=params(16),
        cost_estimate=cost(0.2),
        name="norm_conv_inner",
    )(record_starts, record_lengths, hidden_in, stats_in, other_stats_in, gain, conv_weight)

    before, after, partly = lax.optimization_barrier((before, after, partly))
    halo = pl.BlockSpec((before.shape[0], LANES), lambda p: (0, p))
    attended_end = pl.pallas_call(
        functools.partial(attend_ends, frames),
        grid=(pairs,),
        out_shape=jax.ShapeDtypeStruct((ends, heads_width), jnp.bfloat16),
        in_specs=[SMEM, SMEM, column, column, column, halo, halo],
        out_specs=pl.BlockSpec((ends, LANES), lambda p: (0, p)),
        scratch_shapes=[pltpu.VMEM((2, REACH, SPAN), jnp.float32)],
        compiler_params=params(16),
        cost_estimate=cost(5),
        name="attend_ends",
    )(record_starts, record_lengths, queries, attn_keys, attn_values, before, after)

    def edge_rows(received):
        return jnp.concatenate([received[:EDGE], received[EDGE : 2 * EDGE]], axis=1)

    other_end = lax.ppermute(attended_end, "tp", swap)
    sliver = pl.BlockSpec((EDGE, step), lambda j, t: (0, j))
    hidden_end, stats_end = projection(
        project_ends, attended_end, other_end, [edge_rows(before), edge_rows(after)], [sliver, sliver], 4, "project_ends"
    )
    other_stats_end = lax.ppermute(stats_end, "tp", swap)

    more = 2 * EDGE
    rows = REACH + more
    return pl.pallas_call(
        functools.partial(norm_conv_ends, frames),
        grid=(width // LANES,),
        out_shape=result,
        in_specs=[
            SMEM, SMEM, lane_block(ends), lane_block(more), lane_block(more, inner // more - 1),
            whole(stats_end), whole(stats_end), whole(stats_in), whole(stats_in), lane_block(1), lane_block(KERNEL),
            anywhere,
        ],
        out_specs=anywhere,
        scratch_shapes=[
            shared((2, rows)), shared((2, rows)), shared((2, rows)), shared((2, rows)), shared((2, rows)),
            shared((2, 3, rows)), shared((9, 8)), shared((3 * EDGE,)),
            pltpu.VMEM((2, 2, REACH, LANES), jnp.bfloat16),
            pltpu.SMEM((128,), jnp.int32),
            pltpu.SemaphoreType.DMA((2, 2)),
        ],
        input_output_aliases={11: 0},
        compiler_params=params(16),
        cost_estimate=cost(5),
        name="norm_conv_ends",
    )(
        record_starts, record_lengths, hidden_end, hidden_in, hidden_in, stats_end, other_stats_end, stats_in,
        other_stats_in, gain, conv_weight, partly,
    )


def solution(mesh):
    placed = (
        P(("grp", "seq"), "tp"),
        P(("grp", "seq"), "tp"),
        P(("grp", "seq"), "tp"),
        P("tp", None),
        P(("grp", "seq"), "tp"),
        P("tp"),
        P(None, "tp"),
        P("grp"),
        P("grp"),
    )
    return jax.shard_map(
        on_device, mesh=mesh, in_specs=placed, out_specs=P(("grp", "seq"), "tp"), check_vma=False
    )
```

time: 100 us -> 75.1 us (0.75)
  waiting for transfers between devices: 21 us -> 3.16 us
  local copies, waits for them, and re-layouts: 14.7 us -> 7.55 us
    ppermute x2, waiting for transfers between devices: 20.1 us -> 0.01 us  [the longest x1 0.01 us: on_device(): lax.ppermute(top_edge, 'seq', [(i + 1, i) for i in range(count - 1)])]
    unnamed x30 -> x28, local copies, waits for them, and re-layouts: 11.2 us -> 6.74 us
    slice x4 -> x1, local copies, waits for them, and re-layouts: 2.96 us -> 0.8 us  [edge_rows(): return jnp.concatenate([received[:EDGE], received[EDGE:2 * EDGE]], axis=1)]
    pallas_call x3 -> x5, Pallas kernels: 37.9 us -> 36.4 us  [the longest x2 14.7 us: projection(): pl.pallas_call(functools.partial(body, tiles), grid_spec=pltpu.PrefetchSc...]
    ppermute x1, waiting for transfers between devices: 0.01 us -> 1.43 us  [on_device(): other_end = lax.ppermute(attended_end, 'tp', swap)]
    ppermute x1, starting transfers between devices: 0.01 us -> 1.11 us  [on_device(): other_stats_in = lax.ppermute(stats_in, 'tp', swap)]
  transfers between devices with their start and end apart: 7 -> 7, of which waited for: 3 -> 3; matrix products, arithmetic and copies ran while one was open for 6% -> 0% of each run, Pallas kernels for 32% -> 47%
where the time goes in v2:
time: 75.1 us; the launch traced here: 74.5 us
  Pallas kernels  54.8 us (73%)
  starting transfers between devices  8.82 us (12%)
  local copies, waits for them, and re-layouts  7.55 us (10%)
  waiting for transfers between devices  3.16 us (4%)
    pallas_call x2, Pallas kernels, projection(): pl.pallas_call(functools.partial(body, tiles), grid_spec=pltpu.PrefetchSc...  14.7 us
    pallas_call x1, Pallas kernels, on_device(): pl.pallas_call(functools.partial(norm_conv_inner, frames), grid=(width //...  11.9 us
    pallas_call x1, Pallas kernels, on_device(): pl.pallas_call(functools.partial(attend_inner, frames), grid=(pairs,), ou...  11.6 us
    pallas_call x1, Pallas kernels, on_device(): pl.pallas_call(functools.partial(norm_conv_ends, frames), grid=(width //...  7.39 us
    pallas_call x1, Pallas kernels, on_device(): pl.pallas_call(functools.partial(attend_ends, frames), grid=(pairs,), out...  6.83 us
    unnamed x28, local copies, waits for them, and re-layouts  6.74 us
    ppermute x1, starting transfers between devices, on_device(): lax.ppermute(bottom_edge, 'seq', [(i, i + 1) for i in range(count - 1)])  3.14 us
    ppermute x1, starting transfers between devices, on_device(): lax.ppermute(top_edge, 'seq', [(i + 1, i) for i in range(count - 1)])  3.04 us
  transfers between devices with their start and end apart: 7, of which 3 were waited for; matrix products, arithmetic and copies ran while one was open for 0% of the time, Pallas kernels for 47%

profile of v2, /device:TPU:17, one launch (start us, length us, event | category | flops | bytes accessed | tf_op | source)
XLA Modules:
  0.0 74.5 jit_solution(2001984605972201909)
XLA Ops:
  0.0 0.7 collective-permute-start.3
  0.7 2.4 %pack_edges.1 = (bf16[336,768]{1,0:T(8,128)(2,1)}, bf16[336,768]{1,0:T(8,128)(2,1)}) custom-call(bf16[1024,768]{1,0:T(8,128)(2,1)} %q_ref.3, bf16[1024,768]{1,0:T(8,128)(2,1)} %k_ref.5, bf16[1024,768]{1,0:T(8,128)(2,1)} %v_ref.5, bf16[1024,1536]{1,0:T(8,128)(2,1)} %res.3), custom_call_target="tpu_custom_call" | custom-call | tf_op jit(solution)/shard_map/pack_edges/pallas_call | solution.py:437
  3.1 0.0 copy-start
  3.1 0.0 copy-start.2
  3.1 1.5 %copy-done.2 = bf16[1024,768]{1,0:T(8,128)(2,1)S(1)} copy-done((bf16[1024,768]{1,0:T(8,128)(2,1)S(1)}, bf16[1024,768]{1,0:T(8,128)(2,1)}, u32[]{:S(2)}) %copy-start.2) | copy-done | bytes 1572888
  4.7 1.4 %copy-done.4 = bf16[1024,768]{1,0:T(8,128)(2,1)S(1)} copy-done((bf16[1024,768]{1,0:T(8,128)(2,1)S(1)}, bf16[1024,768]{1,0:T(8,128)(2,1)}, u32[]{:S(2)}) %copy-start.4) | copy-done | bytes 1572888
  6.1 1.4 %copy-done.6 = bf16[1024,768]{1,0:T(8,128)(2,1)S(1)} copy-done((bf16[1024,768]{1,0:T(8,128)(2,1)S(1)}, bf16[1024,768]{1,0:T(8,128)(2,1)}, u32[]{:S(2)}) %copy-start.6) | copy-done | bytes 1572888
  7.5 11.6 %attend_inner.1.own = bf16[768,768]{1,0:T(8,128)(2,1)} custom-call(s32[8]{0:T(128)S(1)} %copy-done.9, s32[8]{0:T(128)S(1)} %copy-done.10, bf16[1024,768]{1,0:T(8,128)(2,1)S(1)} %copy-done.2, bf16[1024,768]{1,0:T(8,128)(2,1)S(1)} %copy-done.4, bf16[1024,768]{1,0:T(8,128)(2,1)S(1)} %copy-done.6), custom_call_target="tpu_custom_call" | custom-call | flops 80000000 | bytes 1000 | tf_op jit(solution)/shard_map/attend_inner/pallas_call | solution.py:452
  19.0 0.0 collective-permute-start.2
  19.1 3.1 %collective-permute-start = (bf16[336,768]{1,0:T(8,128)(2,1)}, bf16[336,768]{1,0:T(8,128)(2,1)}, u32[]{:S(2)}, u32[]{:S(2)}) collective-permute-start(bf16[336,768]{1,0:T(8,128)(2,1)} %get-tuple-element.20), channel_id=1, source_target_pairs={{0,2},{2,4},{4,6},{6,8},{8,10},{10,12},{12,14},{1,3},{3,5},{5,7},{... | collective-permute-start | bytes 1548296 | tf_op jit(solution)/shard_map/ppermute | solution.py:448
  22.2 3.0 %collective-permute-start.1 = (bf16[336,768]{1,0:T(8,128)(2,1)}, bf16[336,768]{1,0:T(8,128)(2,1)}, u32[]{:S(2)}, u32[]{:S(2)}) collective-permute-start(bf16[336,768]{1,0:T(8,128)(2,1)} %get-tuple-element.21), channel_id=1, source_target_pairs={{2,0},{4,2},{6,4},{8,6},{10,8},{12,10},{14,12},{3,1},{5,3},{7,5},{... | collective-permute-start | bytes 1548296 | tf_op jit(solution)/shard_map/ppermute | solution.py:447
  25.3 2.3 %copy-done.1 = bf16[768,3072]{1,0:T(8,128)(2,1)S(1)} copy-done((bf16[768,3072]{1,0:T(8,128)(2,1)S(1)}, bf16[768,3072]{1,0:T(8,128)(2,1)}, u32[]{:S(2)}) %copy-start.1) | copy-done | bytes 4718616
  27.6 9.1 %project_inner.1 = (f32[768,1536]{1,0:T(8,128)S(1)}, f32[16,768]{1,0:T(8,128)S(1)}) custom-call(s32[1]{0:T(128)} %bitcast.t_ref, bf16[768,768]{1,0:T(8,128)(2,1)} %attend_inner.1.own, bf16[768,768]{1,0:T(8,128)(2,1)} %collective-permute-done.2.other, bf16[768,3072]{1,0:T(8,128)(2,1)S(1)} %copy-done.1, bf16[768,3072]{1,0:T(8,128)(2,1)} %collective-permute-done.3.w_other, ...), custom_call_target="tpu_custom_call" | custom-call | flops 80000000 | bytes 1000 | tf_op jit(solution)/shard_map/project_inner/pallas_call | solution.py:474
  36.7 1.1 %collective-permute-start.4 = (f32[16,768]{1,0:T(8,128)S(1)}, f32[16,768]{1,0:T(8,128)S(1)}, u32[]{:S(2)}, u32[]{:S(2)}) collective-permute-start(f32[16,768]{1,0:T(8,128)S(1)} %get-tuple-element.23.own_ref.s_in_ref), channel_id=1, source_target_pairs={{0,1},{1,0},{2,3},{3,2},{4,5},{5,4},{6,7},{7,6},{8,9},{9,8},{10,11... | collective-permute-start | bytes 147464 | tf_op jit(solution)/shard_map/ppermute | solution.py:504
  37.9 0.9 %collective-permute-done.4.other_ref.t_in_ref = f32[16,768]{1,0:T(8,128)S(1)} collective-permute-done((f32[16,768]{1,0:T(8,128)S(1)}, f32[16,768]{1,0:T(8,128)S(1)}, u32[]{:S(2)}, u32[]{:S(2)}) %collective-permute-start.4) | collective-permute-done | bytes 49184 | tf_op jit(solution)/shard_map/ppermute | solution.py:504
  38.7 11.9 %norm_conv_inner.1.done_ref = bf16[1024,1536]{1,0:T(8,128)(2,1)} custom-call(s32[8]{0:T(128)S(1)} %copy-done.9, s32[8]{0:T(128)S(1)} %copy-done.10, f32[768,1536]{1,0:T(8,128)S(1)} %get-tuple-element.22.h_ref.h_low_ref.h_high_ref, f32[16,768]{1,0:T(8,128)S(1)} %get-tuple-element.23.own_ref.s_in_ref, f32[16,768]{1,0:T(8,128)S(1)} %collective-permute-done.4.other_ref.t_in_ref, ...), custom_call_target="tpu_custom_call" | custom-call | flops 80000000 | bytes 1000 | tf_op jit(solution)/shard_map/norm_conv_inner/pallas_call | solution.py:512
  50.7 0.8 %fusion = (bf16[16,768]{1,0:T(8,128)(2,1)S(1)}, bf16[16,768]{1,0:T(8,128)(2,1)S(1)}, bf16[16,768]{1,0:T(8,128)(2,1)S(1)}, bf16[16,768]{1,0:T(8,128)(2,1)S(1)}) fusion(bf16[336,768]{1,0:T(8,128)(2,1)} %collective-permute-done.1.after_ref, bf16[336,768]{1,0:T(8,128)(2,1)} %collective-permute-done.before_ref), kind=kLoop, calls=%fused_computation.2 | loop fusion | bytes 196608 | tf_op jit(solution)/shard_map/slice | solution.py:545
  51.5 6.8 %attend_ends.1.own = bf16[288,768]{1,0:T(8,128)(2,1)S(1)} custom-call(s32[8]{0:T(128)S(1)} %copy-done.9, s32[8]{0:T(128)S(1)} %copy-done.10, bf16[1024,768]{1,0:T(8,128)(2,1)S(1)} %copy-done.3, bf16[1024,768]{1,0:T(8,128)(2,1)S(1)} %copy-done.5, bf16[1024,768]{1,0:T(8,128)(2,1)S(1)} %copy-done.7, bf16[336,768]{1,0:T(8,128)(2,1)} %collective-permute-done.before_ref, ...), custom_call_target="tpu_custom_call" | custom-call | flops 2000000000 | bytes 1000 | tf_op jit(solution)/shard_map/attend_ends/pallas_call | solution.py:532
  58.3 0.4 collective-permute-start.5
  58.8 1.4 %collective-permute-done.5.other = bf16[288,768]{1,0:T(8,128)(2,1)S(1)} collective-permute-done((bf16[288,768]{1,0:T(8,128)(2,1)S(1)}, bf16[288,768]{1,0:T(8,128)(2,1)S(1)}, u32[]{:S(2)}, u32[]{:S(2)}) %collective-permute-start.5) | collective-permute-done | bytes 442400 | tf_op jit(solution)/shard_map/ppermute | solution.py:547
  60.2 5.7 %project_ends.1 = (f32[288,1536]{1,0:T(8,128)S(1)}, f32[16,384]{1,0:T(8,128)S(1)}) custom-call(s32[1]{0:T(128)} %bitcast.t_ref, bf16[288,768]{1,0:T(8,128)(2,1)S(1)} %attend_ends.1.own, bf16[288,768]{1,0:T(8,128)(2,1)S(1)} %collective-permute-done.5.other, bf16[768,3072]{1,0:T(8,128)(2,1)S(1)} %bitcast.2, bf16[768,3072]{1,0:T(8,128)(2,1)} %collective-permute-done.3.w_other, ...), custom_call_target="tpu_custom_call" | custom-call | flops 1600000000 | bytes 1000 | tf_op jit(solution)/shard_map/project_ends/pallas_call | solution.py:474
  65.9 0.4 collective-permute-start.6
  66.3 0.8 %collective-permute-done.6.t_end_ref = f32[16,384]{1,0:T(8,128)S(1)} collective-permute-done((f32[16,384]{1,0:T(8,128)S(1)}, f32[16,384]{1,0:T(8,128)S(1)}, u32[]{:S(2)}, u32[]{:S(2)}) %collective-permute-start.6) | collective-permute-done | bytes 24608 | tf_op jit(solution)/shard_map/ppermute | solution.py:552
  67.1 7.4 %norm_conv_ends.1 = bf16[1024,1536]{1,0:T(8,128)(2,1)} custom-call(s32[8]{0:T(128)S(1)} %copy-done.9, s32[8]{0:T(128)S(1)} %copy-done.10, f32[288,1536]{1,0:T(8,128)S(1)} %get-tuple-element.26.h_end_ref, f32[768,1536]{1,0:T(8,128)S(1)} %get-tuple-element.22.h_ref.h_low_ref.h_high_ref, ...), custom_call_target="tpu_custom_call", output_to_operand_aliasing={{}: (11, {})} | custom-call | flops 2000000000 | bytes 1000 | tf_op jit(solution)/shard_map/norm_conv_ends/pallas_call | solution.py:556
  (30 shorter events, 0.1 us)
Async XLA Ops:
  0.0 3.1 %copy-start.10 = (s32[8]{0:T(128)S(1)}, s32[8]{0:T(128)}, u32[]{:S(2)}) copy-start(s32[8]{0:T(128)} %lengths_ref.7) | copy-start | bytes 100
  0.0 3.1 %copy-start.9 = (s32[8]{0:T(128)S(1)}, s32[8]{0:T(128)}, u32[]{:S(2)}) copy-start(s32[8]{0:T(128)} %starts_ref.7) | copy-start | bytes 100
  0.0 25.3 %collective-permute-start.3 = (bf16[768,3072]{1,0:T(8,128)(2,1)}, bf16[768,3072]{1,0:T(8,128)(2,1)}, u32[]{:S(2)}, u32[]{:S(2)}) collective-permute-start(bf16[768,3072]{1,0:T(8,128)(2,1)} %w_own.3), channel_id=1, source_target_pairs={{0,1},{1,0},{2,3},{3,2},{4,5},{5,4},{6,7},{7,6},{8,9},{9,8},{10,11... | collective-permute-start | bytes 14155784 | tf_op jit(solution)/shard_map/ppermute | solution.py:449
  3.1 22.2 %copy-start = (bf16[1024,1536]{1,0:T(8,128)(2,1)S(1)}, bf16[1024,1536]{1,0:T(8,128)(2,1)}, u32[]{:S(2)}) copy-start(bf16[1024,1536]{1,0:T(8,128)(2,1)} %res.3) | copy-start | bytes 9437188
  3.1 1.6 %copy-start.2 = (bf16[1024,768]{1,0:T(8,128)(2,1)S(1)}, bf16[1024,768]{1,0:T(8,128)(2,1)}, u32[]{:S(2)}) copy-start(bf16[1024,768]{1,0:T(8,128)(2,1)} %q_ref.3) | copy-start | bytes 4718596
  4.7 1.4 %copy-start.4 = (bf16[1024,768]{1,0:T(8,128)(2,1)S(1)}, bf16[1024,768]{1,0:T(8,128)(2,1)}, u32[]{:S(2)}) copy-start(bf16[1024,768]{1,0:T(8,128)(2,1)} %k_ref.5) | copy-start | bytes 4718596
  6.1 1.4 %copy-start.6 = (bf16[1024,768]{1,0:T(8,128)(2,1)S(1)}, bf16[1024,768]{1,0:T(8,128)(2,1)}, u32[]{:S(2)}) copy-start(bf16[1024,768]{1,0:T(8,128)(2,1)} %v_ref.5) | copy-start | bytes 4718596
  19.0 6.2 %collective-permute-start.2 = (bf16[768,768]{1,0:T(8,128)(2,1)}, bf16[768,768]{1,0:T(8,128)(2,1)}, u32[]{:S(2)}, u32[]{:S(2)}) collective-permute-start(bf16[768,768]{1,0:T(8,128)(2,1)} %attend_inner.1.own), channel_id=1, source_target_pairs={{0,1},{1,0},{2,3},{3,2},{4,5},{5,4},{6,7},{7,6},{8,9},{9,8},{10,11... | collective-permute-start | bytes 3538952 | tf_op jit(solution)/shard_map/ppermute | solution.py:502
  19.1 31.6 %collective-permute-start = (bf16[336,768]{1,0:T(8,128)(2,1)}, bf16[336,768]{1,0:T(8,128)(2,1)}, u32[]{:S(2)}, u32[]{:S(2)}) collective-permute-start(bf16[336,768]{1,0:T(8,128)(2,1)} %get-tuple-element.20), channel_id=1, source_target_pairs={{0,2},{2,4},{4,6},{6,8},{8,10},{10,12},{12,14},{1,3},{3,5},{5,7},{... | collective-permute-start | bytes 1548296 | tf_op jit(solution)/shard_map/ppermute | solution.py:448
  22.2 28.5 %collective-permute-start.1 = (bf16[336,768]{1,0:T(8,128)(2,1)}, bf16[336,768]{1,0:T(8,128)(2,1)}, u32[]{:S(2)}, u32[]{:S(2)}) collective-permute-start(bf16[336,768]{1,0:T(8,128)(2,1)} %get-tuple-element.21), channel_id=1, source_target_pairs={{2,0},{4,2},{6,4},{8,6},{10,8},{12,10},{14,12},{3,1},{5,3},{7,5},{... | collective-permute-start | bytes 1548296 | tf_op jit(solution)/shard_map/ppermute | solution.py:447
  25.3 2.3 %copy-start.1 = (bf16[768,3072]{1,0:T(8,128)(2,1)S(1)}, bf16[768,3072]{1,0:T(8,128)(2,1)}, u32[]{:S(2)}) copy-start(bf16[768,3072]{1,0:T(8,128)(2,1)} %w_own.3) | copy-start | bytes 14155780
  27.6 10.2 %copy-start.11 = (f32[1536]{0:T(1024)S(1)}, f32[1536]{0:T(1024)}, u32[]{:S(2)}) copy-start(f32[1536]{0:T(1024)} %param.14) | copy-start | bytes 18436
  27.6 11.1 %copy-start.8 = (f32[31,1536]{1,0:T(8,128)S(1)}, f32[31,1536]{1,0:T(8,128)}, u32[]{:S(2)}) copy-start(f32[31,1536]{1,0:T(8,128)} %w_ref.3) | copy-start | bytes 571396
  27.6 23.8 %copy-start.7 = (bf16[1024,768]{1,0:T(8,128)(2,1)S(1)}, bf16[1024,768]{1,0:T(8,128)(2,1)}, u32[]{:S(2)}) copy-start(bf16[1024,768]{1,0:T(8,128)(2,1)} %v_ref.5) | copy-start | bytes 4718596
  36.7 2.0 %collective-permute-start.4 = (f32[16,768]{1,0:T(8,128)S(1)}, f32[16,768]{1,0:T(8,128)S(1)}, u32[]{:S(2)}, u32[]{:S(2)}) collective-permute-start(f32[16,768]{1,0:T(8,128)S(1)} %get-tuple-element.23.own_ref.s_in_ref), channel_id=1, source_target_pairs={{0,1},{1,0},{2,3},{3,2},{4,5},{5,4},{6,7},{7,6},{8,9},{9,8},{10,11... | collective-permute-start | bytes 147464 | tf_op jit(solution)/shard_map/ppermute | solution.py:504
  38.7 21.5 %slice-start = ((s8[4718592]{0:T(1024)(128)(4,1)}), s8[4194304]{0:T(1024)(128)(4,1)S(1)}, s32[]{:S(2)}) async-start(s8[4718592]{0:T(1024)(128)(4,1)} %bitcast.1), calls=%async_computation | async-start | bytes 8388608
  38.7 12.8 %copy-start.3 = (bf16[1024,768]{1,0:T(8,128)(2,1)S(1)}, bf16[1024,768]{1,0:T(8,128)(2,1)}, u32[]{:S(2)}) copy-start(bf16[1024,768]{1,0:T(8,128)(2,1)} %q_ref.3) | copy-start | bytes 4718596
  38.7 12.8 %copy-start.5 = (bf16[1024,768]{1,0:T(8,128)(2,1)S(1)}, bf16[1024,768]{1,0:T(8,128)(2,1)}, u32[]{:S(2)}) copy-start(bf16[1024,768]{1,0:T(8,128)(2,1)} %k_ref.5) | copy-start | bytes 4718596
  38.7 21.5 %slice-start.1 = ((s8[4718592]{0:T(1024)(128)(4,1)}), s8[524288]{0:T(1024)(128)(4,1)S(1)}, s32[]{:S(2)}) async-start(s8[4718592]{0:T(1024)(128)(4,1)} %bitcast.1), calls=%async_computation.1 | async-start | bytes 1048576
  58.3 1.9 %collective-permute-start.5 = (bf16[288,768]{1,0:T(8,128)(2,1)S(1)}, bf16[288,768]{1,0:T(8,128)(2,1)S(1)}, u32[]{:S(2)}, u32[]{:S(2)}) collective-permute-start(bf16[288,768]{1,0:T(8,128)(2,1)S(1)} %attend_ends.1.own), channel_id=1, source_target_pairs={{0,1},{1,0},{2,3},{3,2},{4,5},{5,4},{6,7},{7,6},{8,9},{9,8},{10,11... | collective-permute-start | bytes 1327112 | tf_op jit(solution)/shard_map/ppermute | solution.py:547
  65.9 1.3 %collective-permute-start.6 = (f32[16,384]{1,0:T(8,128)S(1)}, f32[16,384]{1,0:T(8,128)S(1)}, u32[]{:S(2)}, u32[]{:S(2)}) collective-permute-start(f32[16,384]{1,0:T(8,128)S(1)} %get-tuple-element.27.s_end_ref), channel_id=1, source_target_pairs={{0,1},{1,0},{2,3},{3,2},{4,5},{5,4},{6,7},{7,6},{8,9},{9,8},{10,11... | collective-permute-start | bytes 73736 | tf_op jit(solution)/shard_map/ppermute | solution.py:552

commit v3 on v2

v3 whole, which is shorter than its diff:
```python
import functools

import jax
import jax.numpy as jnp
from jax import lax
from jax.experimental import pallas as pl
from jax.experimental.pallas import tpu as pltpu
from jax.sharding import PartitionSpec as P

D = 3072
HSIZE = 64
WIN = 128
KHALF = 15
REC = 8
KERNEL = 31
EDGE = 16
REACH = WIN + EDGE
SPAN = 512
LANES = 128
NEG = -1e30
SHARE = 4
EXP_SCALE = HSIZE ** (-0.5) * 1.4426950408889634
SMEM = pl.BlockSpec(memory_space=pltpu.SMEM)


def row_bounds(positions, starts_ref, lengths_ref):
    first = jnp.full(positions.shape, -1, jnp.int32)
    last = jnp.full(positions.shape, -2, jnp.int32)
    for r in range(REC):
        start = starts_ref[r]
        end = start + lengths_ref[r]
        inside = (positions >= start) & (positions < end)
        first = jnp.where(inside, start, first)
        last = jnp.where(inside, end - 1, last)
    return first, last


def as_column(row):
    return jnp.transpose(jnp.broadcast_to(row, (LANES, LANES)))


def band_bias(base, rows, key_base, keys, starts_ref, lengths_ref, store):
    for top in range(0, rows, LANES):
        count = min(LANES, rows - top)
        positions = base + top + lax.broadcasted_iota(jnp.int32, (1, LANES), 1)
        first, last = row_bounds(positions, starts_ref, lengths_ref)
        inside = first >= 0
        low = jnp.where(inside, jnp.maximum(first, positions - WIN), 0)
        high = jnp.where(inside, jnp.minimum(last, positions + WIN), -1)
        low = as_column(low.astype(jnp.float32))
        high = as_column(high.astype(jnp.float32))
        for left in range(0, keys, LANES):
            key_at = (key_base + left + lax.broadcasted_iota(jnp.int32, (LANES, LANES), 1)).astype(jnp.float32)
            bias = jnp.where((key_at >= low) & (key_at <= high), jnp.float32(0.0), jnp.float32(NEG))
            store(top, count, left, bias[:count])


def head_pair(query, keys, values, bias):
    rows = query.shape[0]
    left = lax.broadcasted_iota(jnp.int32, query.shape, 1) < HSIZE
    nothing = jnp.zeros_like(query)
    both = jnp.concatenate([jnp.where(left, query, nothing), jnp.where(left, nothing, query)], axis=0)
    scores = lax.dot_general(both, keys, (((1,), (1,)), ((), ())), preferred_element_type=jnp.float32)
    scores = scores + jnp.concatenate([bias, bias], axis=0)
    row_max = jnp.max(scores, axis=1, keepdims=True)
    weights = jnp.exp2((scores - row_max) * EXP_SCALE).astype(jnp.bfloat16)
    mixed = jnp.dot(weights, values, preferred_element_type=jnp.float32)
    mixed = mixed[:, :LANES] / mixed[:, LANES:]
    keep = bias_any(bias)
    return jnp.where(keep, jnp.where(left, mixed[:rows], mixed[rows:]), 0.0).astype(jnp.bfloat16)


def bias_any(bias):
    return jnp.max(bias, axis=1, keepdims=True) > NEG / 2


def split_heads(array):
    left = lax.broadcasted_iota(jnp.int32, array.shape, 1) < HSIZE
    nothing = jnp.zeros_like(array)
    return jnp.where(left, array, nothing), jnp.where(left, nothing, array)


def start_all(copies):
    for copy in copies:
        copy.start()
    return copies


def wait_all(copies):
    for copy in copies:
        copy.wait()


def attend_inner(
    frames, starts_ref, lengths_ref, q_hbm, k_hbm, v_hbm, w_hbm, r_hbm, o_ref, w_own_ref, r_in_ref,
    columns, bias, keys, values, sems, more_sems
):
    blocks = frames // WIN - 2
    span = 3 * WIN
    pairs = q_hbm.shape[1] // LANES
    anchor = lax.axis_index("seq") * frames

    def fetch(p):
        lanes = pl.ds(p * LANES, LANES)
        return [
            pltpu.make_async_copy(ref.at[:, lanes], columns.at[p, n], sems.at[p, n])
            for n, ref in enumerate((q_hbm, k_hbm, v_hbm))
        ]

    for p in range(pairs):
        start_all(fetch(p))
    width = w_own_ref.shape[1]
    mine = pl.multiple_of(lax.axis_index("tp") * width, LANES)
    later = start_all([
        pltpu.make_async_copy(w_hbm.at[:, pl.ds(mine, width)], w_own_ref, more_sems.at[0]),
        pltpu.make_async_copy(r_hbm.at[pl.ds(WIN, blocks * WIN), :], r_in_ref, more_sems.at[1]),
    ])
    values[0, :, LANES:], values[1, :, LANES:] = split_heads(jnp.ones((frames, LANES), jnp.bfloat16))
    for i in range(blocks):
        def store(top, count, left, value):
            bias[i, top : top + count, left : left + LANES] = value

        band_bias(anchor + (i + 1) * WIN, WIN, anchor + i * WIN, span, starts_ref, lengths_ref, store)

    def one_pair(p, carry):
        lanes = pl.ds(pl.multiple_of(p * LANES, LANES), LANES)
        for n, ref in enumerate((q_hbm, k_hbm, v_hbm)):
            pltpu.make_async_copy(ref.at[:, lanes], columns.at[p, n], sems.at[p, n]).wait()
        keys[0], keys[1] = split_heads(columns[p, 1])
        values[0, :, :LANES], values[1, :, :LANES] = split_heads(columns[p, 2])
        for i in range(blocks):
            window = slice(i * WIN, i * WIN + span)
            both = jnp.concatenate([keys[0, window, :], keys[1, window, :]], axis=0)
            scores = lax.dot_general(
                columns[p, 0, (i + 1) * WIN : (i + 2) * WIN, :], both, (((1,), (1,)), ((), ())),
                preferred_element_type=jnp.float32,
            )
            weights = []
            for h in range(2):
                part = scores[:, h * span : (h + 1) * span] + bias[i]
                row_max = jnp.max(part, axis=1, keepdims=True)
                weights.append(jnp.exp2((part - row_max) * EXP_SCALE).astype(jnp.bfloat16))
            mixed = jnp.dot(
                jnp.concatenate(weights, axis=1),
                jnp.concatenate([values[0, window, :], values[1, window, :]], axis=0),
                preferred_element_type=jnp.float32,
            )
            mixed = jnp.where(bias_any(bias[i]), mixed[:, :LANES] / mixed[:, LANES:], 0.0)
            o_ref[i * WIN : (i + 1) * WIN, lanes] = mixed.astype(jnp.bfloat16)
        return carry

    lax.fori_loop(0, pairs, one_pair, 0)
    wait_all(later)


def halo_side():
    return 1 - lax.axis_index("seq") % 2


def attend_ends(
    frames, starts_ref, lengths_ref, q_hbm, k_hbm, v_hbm, first_hbm, second_hbm, o_ref, bias, query, keys, values, sems
):
    anchor = lax.axis_index("seq") * frames
    own = SPAN - REACH
    pairs = q_hbm.shape[1] // LANES
    side = halo_side()
    copies = []

    def move(source, target):
        copies.append(pltpu.make_async_copy(source, target, sems.at[len(copies)]))

    for target, ref, at, rows, mine in (
        (query, q_hbm, 2 * EDGE, EDGE, WIN), (keys, k_hbm, 3 * EDGE, REACH, own), (values, v_hbm, 3 * EDGE + REACH, REACH, own)
    ):
        move(ref.at[pl.ds(0, mine), :], target.at[0, pl.ds(rows, mine), :])
        move(ref.at[pl.ds(frames - mine, mine), :], target.at[1, pl.ds(0, mine), :])
        for halo, which in ((first_hbm, side), (second_hbm, 1 - side)):
            top = pl.multiple_of(which * mine, EDGE)
            move(halo.at[pl.ds(at, rows), :], target.at[which, pl.ds(top, rows), :])
    start_all(copies)
    for i, (base, key_base) in enumerate(((-EDGE, -REACH), (frames - WIN, frames - own))):
        def store(top, count, left, value):
            bias[i, top : top + count, left : left + LANES] = value

        band_bias(anchor + base, REACH, anchor + key_base, SPAN, starts_ref, lengths_ref, store)
    wait_all(copies)
    ones = jnp.ones((SPAN, LANES), jnp.bfloat16)

    def one_pair(p, carry):
        lanes = pl.ds(pl.multiple_of(p * LANES, LANES), LANES)
        for i in range(2):
            o_ref[i * REACH : (i + 1) * REACH, lanes] = head_pair(
                query[i, :, lanes], keys[i, :, lanes], jnp.concatenate([values[i, :, lanes], ones], axis=1), bias[i]
            )
        return carry

    lax.fori_loop(0, pairs, one_pair, 0, unroll=2)


def pack_edges(frames, q_ref, k_ref, v_ref, r_ref, w_ref, first_ref, second_ref, w_send_ref, sems):
    half = q_ref.shape[1]
    odd = lax.axis_index("seq") % 2
    copies = []
    for i, out in enumerate((first_ref, second_ref)):
        bottom = (1 - odd) if i == 0 else odd

        def rows(ref, n, left=0):
            return ref.at[pl.ds(pl.multiple_of(bottom * (frames - n), EDGE), n), pl.ds(left, half)]

        moves = [
            (rows(r_ref, EDGE), 0, EDGE),
            (rows(r_ref, EDGE, half), EDGE, EDGE),
            (rows(q_ref, EDGE), 2 * EDGE, EDGE),
            (rows(k_ref, REACH), 3 * EDGE, REACH),
            (rows(v_ref, REACH), 3 * EDGE + REACH, REACH),
        ]
        for n, (source, at, count) in enumerate(moves):
            copies.append(pltpu.make_async_copy(source, out.at[pl.ds(at, count), :], sems.at[i, n]))
    width = w_send_ref.shape[1]
    left = pl.multiple_of((1 - lax.axis_index("tp")) * width, LANES)
    copies.append(pltpu.make_async_copy(w_ref.at[:, pl.ds(left, width)], w_send_ref, sems.at[2, 0]))
    wait_all(start_all(copies))


def project(
    inner, own_hbm, other_hbm, w_own_hbm, w_other_hbm, r_hbm, first_hbm, second_hbm,
    h_ref, stats_ref, left, right, residual, shift, first, second, sems,
):
    rows, width = h_ref.shape
    half = own_hbm.shape[1]
    step = 256
    copies = []

    def move(source, target):
        copies.append(pltpu.make_async_copy(source, target, sems.at[len(copies)]))

    move(own_hbm, left.at[:, pl.ds(0, half)])
    move(w_own_hbm, right.at[pl.ds(0, half), :])
    move(other_hbm, left.at[:, pl.ds(half, half)])
    move(w_other_hbm, right.at[pl.ds(half, half), :])
    if inner:
        move(r_hbm, residual)
    else:
        frames = r_hbm.shape[0]
        move(r_hbm.at[pl.ds(0, WIN), :], residual.at[pl.ds(EDGE, WIN), :])
        move(r_hbm.at[pl.ds(frames - WIN, WIN), :], residual.at[pl.ds(REACH, WIN), :])
        side = halo_side()
        for halo, which in ((first_hbm, side), (second_hbm, 1 - side)):
            at = pl.ds(pl.multiple_of(which * (REACH + WIN), EDGE), EDGE)
            for n in range(2):
                move(halo.at[pl.ds(n * EDGE, EDGE), :], residual.at[at, pl.ds(n * half, half)])
    wait_all(start_all(copies))

    def gather(j):
        first_sum, second_sum = first[...], second[...]
        for l in range(j * step, (j + 1) * step, LANES):
            off = h_ref[:, l : l + LANES] - shift[...]
            first_sum = first_sum + off
            second_sum = second_sum + off * off
        first[...] = first_sum
        second[...] = second_sum

    first[...] = jnp.zeros_like(first)
    second[...] = jnp.zeros_like(second)
    for j in range(width // step):
        cols = slice(j * step, (j + 1) * step)
        part = jnp.dot(left[...], right[:, cols], preferred_element_type=jnp.float32)
        h_ref[:, cols] = part + residual[:, cols].astype(jnp.float32)
        if j == 0:
            mean = jnp.sum(h_ref[:, cols], axis=1, keepdims=True) * (1.0 / step)
            shift[...] = jnp.broadcast_to(mean, (rows, LANES))
        else:
            gather(j - 1)
    gather(width // step - 1)
    moved = jnp.sum(first[...], axis=1, keepdims=True) * (1.0 / width)
    mean = shift[...] + moved
    square = jnp.sum(second[...], axis=1, keepdims=True) - moved * moved * float(width)
    for top in range(0, rows, LANES):
        count = min(LANES, rows - top)
        for k, column in enumerate((mean, jnp.broadcast_to(square, (rows, LANES)))):
            tile = column[top : top + count]
            if count < LANES:
                tile = jnp.concatenate([tile, jnp.zeros((LANES - count, LANES), jnp.float32)], axis=0)
            stats_ref[8 * k : 8 * k + 8, top : top + LANES] = jnp.transpose(tile)[:8, :]


def stat_columns(base, own, other, width, starts_ref, lengths_ref):
    positions = base + lax.broadcasted_iota(jnp.int32, (1, LANES), 1)
    index = jnp.zeros((1, LANES), jnp.int32) - 1
    for r in range(REC):
        start = starts_ref[r]
        inside = (positions >= start) & (positions < start + lengths_ref[r])
        index = jnp.where(inside, r, index)
    gap = own[0:1, :] - other[0:1, :]
    middle = 0.5 * (own[0:1, :] + other[0:1, :])
    var = (own[8:9, :] + other[8:9, :] + gap * gap * (width * 0.25)) * (1.0 / width)
    inverse = jnp.where(index >= 0, lax.rsqrt(var + 1e-5), 0.0)
    parity = jnp.where(index >= 0, (index % 2).astype(jnp.float32), -1.0)
    halves = jnp.where(index >= 0, 0.5, 0.0)
    return as_column(middle), as_column(inverse), as_column(parity), as_column(halves)


def mark_mixed(base, chunks, flags, at, starts_ref, lengths_ref):
    flags[at] = jnp.int32(0)
    for r in range(REC - 1):
        end, start = starts_ref[r] + lengths_ref[r], starts_ref[r + 1]
        low = jnp.maximum((end - KHALF - base) >> 4, 0)
        high = jnp.minimum((start + KHALF - base + EDGE - 1) >> 4, chunks)

        @pl.when(start - end < KHALF)
        def _():
            def add(c, carry):
                known = flags[at]
                flags[at + 1 + known] = c
                flags[at] = known + 1
                return carry

            lax.fori_loop(low, high, add, 0)


def convolve(load, w_ref):
    acc = load(0) * w_ref[0:1, :]
    for tap in range(1, KERNEL):
        acc = acc + load(tap) * w_ref[tap : tap + 1, :]
    return acc


def differences(x_ref, diffs):
    rows = x_ref.shape[0]
    x = x_ref[...]
    near = x[: rows - 8] - x[8:]
    diffs[0, : rows - 8, :] = near
    diffs[1, : rows - 16, :] = x[: rows - 16] - x[16:]
    diffs[2, : rows - 24, :] = near[: rows - 24] - near[16:]


def tap_sums(w_ref, wq):
    padded = jnp.concatenate([jnp.zeros((1, LANES), jnp.float32), w_ref[...]], axis=0)
    w0, w1, w2, w3 = (padded[8 * j : 8 * j + 8] for j in range(4))
    for n, value in enumerate((w0, w0 + w1, -w1, w0 + w2, w0 + w1 + w2 + w3, -(w1 + w3), -w2, -(w2 + w3), w3)):
        wq[n] = value


def conv_groups(x_ref, diffs, wq, ats):
    sources = (
        (diffs.at[2], 0), (diffs.at[1], 8), (diffs.at[2], 8),
        (diffs.at[0], 16), (x_ref, 24), (diffs.at[0], 24),
        (diffs.at[2], 16), (diffs.at[1], 24), (diffs.at[2], 24),
    )
    sums = [[None] * 9 for _ in ats]
    for s in range(8):
        for n, (ref, off) in enumerate(sources):
            weight = jnp.broadcast_to(wq[n, s : s + 1, :], (8, LANES))
            for group, at in zip(sums, ats):
                first = at - EDGE + s + off
                term = ref[first : first + 8, :] * weight
                group[n] = term if group[n] is None else group[n] + term
    results = []
    for t in sums:
        a0, a1 = t[1] + t[0], t[1] + t[2]
        p0, p1 = t[4] + t[3], t[4] + t[5]
        c0, c1 = t[7] + t[6], t[7] + t[8]
        results.append(jnp.concatenate([a0 + p0, a1 + p1, p0 + c0, p1 + c1], axis=0))
    return results


def silu_add(hidden, half):
    return (hidden + (half + half * jnp.tanh(half))).astype(jnp.bfloat16)


def conv_rows(rows, hidden, normed, parity, halves, diffs, wq, masked, flags, flag_at, w_ref, out):
    differences(normed, diffs)
    group = 2 * EDGE
    tops = list(range(0, rows - group, group)) + [rows - group]
    for start in range(0, len(tops), SHARE):
        some = tops[start : start + SHARE]
        for top, conv_sum in zip(some, conv_groups(normed, diffs, wq, [top + EDGE for top in some])):
            at = top + EDGE
            here = slice(at, at + group)
            out[top : top + group, :] = silu_add(hidden[here, :], conv_sum * halves[here, :])

    def again(c, carry):
        top = pl.multiple_of(flags[flag_at + 1 + c] * EDGE, EDGE)
        around, here = pl.ds(top, 3 * EDGE), pl.ds(top + EDGE, EDGE)
        conv_sum = jnp.zeros((EDGE, LANES), jnp.float32)
        for side in range(2):
            masked[...] = jnp.where(parity[around, :] == side, normed[around, :], 0.0)
            first = EDGE - KHALF
            part = convolve(lambda tap: masked[first + tap : first + tap + EDGE, :], w_ref)
            conv_sum = jnp.where(parity[here, :] == side, part, conv_sum)
        out[pl.ds(top, EDGE), :] = silu_add(hidden[here, :], conv_sum * 0.5)
        return carry

    lax.fori_loop(0, flags[flag_at], again, 0)


def norm_conv_inner(
    frames, starts_ref, lengths_ref, h_ref, own_ref, other_ref, gain_ref, w_ref, o_ref,
    mean, scale, parity, halves, normed, diffs, wq, masked, out, flags, sems,
):
    step, steps = pl.program_id(0), pl.num_programs(0)
    rows = frames - 2 * WIN
    kept = rows - 2 * EDGE
    base = lax.axis_index("seq") * frames + WIN

    @pl.when(step == 0)
    def _():
        width = 2.0 * LANES * steps
        for top in range(0, rows, LANES):
            here = slice(top, top + LANES)
            mean[here, :], scale[here, :], parity[here, :], halves[here, :] = stat_columns(
                base + top, own_ref[:, here], other_ref[:, here], width, starts_ref, lengths_ref
            )
        mark_mixed(base + EDGE, kept // EDGE, flags, 0, starts_ref, lengths_ref)

    value = (h_ref[...] - mean[...]) * scale[...] * gain_ref[...]
    normed[...] = value.astype(jnp.bfloat16).astype(jnp.float32)
    slot = step % 2

    def copy(at, which):
        return pltpu.make_async_copy(
            out.at[which], o_ref.at[pl.ds(WIN + EDGE, kept), pl.ds(pl.multiple_of(at * LANES, LANES), LANES)], sems.at[which]
        )

    @pl.when(step >= 2)
    def _():
        copy(step - 2, slot).wait()

    tap_sums(w_ref, wq)
    conv_rows(kept, h_ref, normed, parity, halves, diffs, wq, masked, flags, 0, w_ref, out.at[slot])
    copy(step, slot).start()

    @pl.when(step == steps - 1)
    def _():
        copy(step - 1, 1 - slot).wait()
        copy(step, slot).wait()


def norm_conv_ends(
    frames, starts_ref, lengths_ref, h_end_ref, h_low_ref, h_high_ref, s_end_ref, t_end_ref, s_in_ref, t_in_ref,
    gain_ref, w_ref, done_ref, o_ref, mean, scale, parity, halves, hidden, normed, diffs, wq, masked, out, flags, sems,
):
    step, steps = pl.program_id(0), pl.num_programs(0)
    inner = frames - 2 * WIN
    anchor = lax.axis_index("seq") * frames
    more = 2 * EDGE
    rows = REACH + more

    @pl.when(step == 0)
    def _():
        width = 2.0 * LANES * steps

        def place(i, at, count, base, lane, own, other, skip):
            values = stat_columns(
                base, own[:, lane : lane + LANES], other[:, lane : lane + LANES], width, starts_ref, lengths_ref
            )
            for ref, value in zip((mean, scale, parity, halves), values):
                ref[i, at : at + count, :] = value[skip : skip + count]

        for top, count in ((0, LANES), (LANES, EDGE)):
            place(0, top, count, anchor - EDGE + top, top, s_end_ref, t_end_ref, 0)
        place(0, REACH, more, anchor + WIN, 0, s_in_ref, t_in_ref, 0)
        place(1, 0, more, anchor + frames - 2 * WIN, inner - LANES, s_in_ref, t_in_ref, LANES - more)
        own = jnp.concatenate([s_end_ref[:, LANES : 2 * LANES], s_end_ref[:, 2 * LANES :]], axis=1)[:, EDGE : EDGE + 2 * LANES - EDGE]
        other = jnp.concatenate([t_end_ref[:, LANES : 2 * LANES], t_end_ref[:, 2 * LANES :]], axis=1)[:, EDGE : EDGE + 2 * LANES - EDGE]
        place(1, more, LANES, anchor + frames - WIN, 0, own, other, 0)
        tail = jnp.concatenate([s_end_ref[:, 2 * LANES + EDGE :], jnp.zeros((16, LANES), jnp.float32)], axis=1)
        tail2 = jnp.concatenate([t_end_ref[:, 2 * LANES + EDGE :], jnp.zeros((16, LANES), jnp.float32)], axis=1)
        place(1, more + LANES, EDGE, anchor + frames, 0, tail, tail2, 0)
        for i in range(2):
            mark_mixed(anchor + i * (frames - REACH), REACH // EDGE, flags, i * 64, starts_ref, lengths_ref)

    hidden[0, :REACH, :] = h_end_ref[:REACH, :]
    hidden[0, REACH:, :] = h_low_ref[...]
    hidden[1, :more, :] = h_high_ref[...]
    hidden[1, more:, :] = h_end_ref[REACH:, :]
    slot = step % 2

    def copies(at, which):
        lanes = pl.ds(pl.multiple_of(at * LANES, LANES), LANES)
        return [
            pltpu.make_async_copy(
                out.at[which, i], o_ref.at[pl.ds(i * (frames - REACH), REACH), lanes], sems.at[which, i]
            )
            for i in range(2)
        ]

    @pl.when(step >= 2)
    def _():
        for copy in copies(step - 2, slot):
            copy.wait()

    tap_sums(w_ref, wq)
    for i in range(2):
        value = (hidden[i] - mean[i]) * scale[i] * gain_ref[...]
        normed[i] = value.astype(jnp.bfloat16).astype(jnp.float32)
        conv_rows(
            REACH, hidden.at[i], normed.at[i], parity.at[i], halves.at[i], diffs.at[i], wq, masked, flags, i * 64, w_ref,
            out.at[slot, i],
        )
    for copy in copies(step, slot):
        copy.start()

    @pl.when(step == steps - 1)
    def _():
        for copy in copies(step - 1, 1 - slot) + copies(step, slot):
            copy.wait()


def cost(microseconds):
    return pl.CostEstimate(flops=int(microseconds * 4e8), bytes_accessed=1000, transcendentals=0)


def params(mebibytes):
    return pltpu.CompilerParams(vmem_limit_bytes=mebibytes * 2**20)


def on_device(
    queries, attn_keys, attn_values, out_weight, residual, norm_gain, conv_weight, record_starts, record_lengths
):
    frames, heads_width = queries.shape
    width = residual.shape[1]
    pairs = heads_width // LANES
    inner = frames - 2 * WIN
    ends = 2 * REACH
    count = lax.axis_size("seq")
    swap = [(0, 1), (1, 0)]
    anywhere = pl.BlockSpec(memory_space=pl.ANY)

    edges = jax.ShapeDtypeStruct((3 * EDGE + 2 * REACH, heads_width), jnp.bfloat16)
    halved = jax.ShapeDtypeStruct((heads_width, width), jnp.bfloat16)
    first_edge, second_edge, weight_send = pl.pallas_call(
        functools.partial(pack_edges, frames),
        out_shape=[edges, edges, halved],
        in_specs=[pl.BlockSpec(memory_space=pltpu.HBM)] * 5,
        out_specs=[pl.BlockSpec(memory_space=pltpu.VMEM)] * 3,
        scratch_shapes=[pltpu.SemaphoreType.DMA((3, 5))],
        compiler_params=params(52),
        name="pack_edges",
    )(queries, attn_keys, attn_values, residual, out_weight)
    first_edge, second_edge, queries = lax.optimization_barrier((first_edge, second_edge, queries))
    first = lax.ppermute(first_edge, "seq", [(i, i ^ 1) for i in range(count)])
    second = lax.ppermute(second_edge, "seq", [(i, ((i + 1) ^ 1) - 1) for i in range(1, count - 1)])
    weight_other = lax.ppermute(weight_send, "tp", swap)

    hbm = pl.BlockSpec(memory_space=pltpu.HBM)
    vmem = pl.BlockSpec(memory_space=pltpu.VMEM)
    attended_in, weight_own, residual_in = pl.pallas_call(
        functools.partial(attend_inner, frames),
        out_shape=[
            jax.ShapeDtypeStruct((inner, heads_width), jnp.bfloat16), halved,
            jax.ShapeDtypeStruct((inner, width), jnp.bfloat16),
        ],
        in_specs=[SMEM, SMEM, hbm, hbm, hbm, hbm, hbm],
        out_specs=[vmem, vmem, vmem],
        scratch_shapes=[
            pltpu.VMEM((pairs, 3, frames, LANES), jnp.bfloat16),
            pltpu.VMEM((inner // WIN, WIN, 3 * WIN), jnp.float32),
            pltpu.VMEM((2, frames, LANES), jnp.bfloat16),
            pltpu.VMEM((2, frames, 2 * LANES), jnp.bfloat16),
            pltpu.SemaphoreType.DMA((pairs, 3)),
            pltpu.SemaphoreType.DMA((2,)),
        ],
        compiler_params=params(42),
        cost_estimate=cost(0.2),
        name="attend_inner",
    )(record_starts, record_lengths, queries, attn_keys, attn_values, out_weight, residual)

    def projection(inside, own, other, microseconds, name):
        rows = own.shape[0]
        padded = -(-rows // LANES) * LANES
        shared = pltpu.VMEM((rows, LANES), jnp.float32)
        halos = [first_edge, second_edge] if inside else [first, second]
        return pl.pallas_call(
            functools.partial(project, inside),
            in_specs=[anywhere] * 7,
            out_specs=[vmem, vmem],
            scratch_shapes=[
                pltpu.VMEM((rows, 2 * heads_width), jnp.bfloat16),
                pltpu.VMEM((2 * heads_width, width), jnp.bfloat16),
                pltpu.VMEM((rows, width), jnp.bfloat16),
                shared, shared, shared,
                pltpu.SemaphoreType.DMA((10,)),
            ],
            out_shape=[
                jax.ShapeDtypeStruct((rows, width), jnp.float32),
                jax.ShapeDtypeStruct((16, padded), jnp.float32),
            ],
            compiler_params=params(24),
            cost_estimate=cost(microseconds),
            name=name,
        )(own, other, weight_own, weight_other, residual_in if inside else residual, *halos)

    other_in = lax.ppermute(attended_in, "tp", swap)
    hidden_in, stats_in = projection(True, attended_in, other_in, 0.2, "project_inner")
    other_stats_in = lax.ppermute(stats_in, "tp", swap)

    whole = lambda array: pl.BlockSpec(array.shape, lambda g: (0, 0))
    lane_block = lambda n, i=0: pl.BlockSpec((n, LANES), lambda g: (i, g))
    gain = norm_gain.reshape(1, width)
    shared = lambda n: pltpu.VMEM(n + (LANES,), jnp.float32)
    kept = inner - 2 * EDGE
    result = jax.ShapeDtypeStruct((frames, width), jnp.bfloat16)
    partly = pl.pallas_call(
        functools.partial(norm_conv_inner, frames),
        grid=(width // LANES,),
        out_shape=result,
        in_specs=[SMEM, SMEM, lane_block(inner), whole(stats_in), whole(stats_in), lane_block(1), lane_block(KERNEL)],
        out_specs=anywhere,
        scratch_shapes=[
            shared((inner,)), shared((inner,)), shared((inner,)), shared((inner,)), shared((inner,)), shared((3, inner)), shared((9, 8)),
            shared((3 * EDGE,)),
            pltpu.VMEM((2, kept, LANES), jnp.bfloat16),
            pltpu.SMEM((64,), jnp.int32),
            pltpu.SemaphoreType.DMA((2,)),
        ],
        compiler_params=params(16),
        cost_estimate=cost(0.2),
        name="norm_conv_inner",
    )(record_starts, record_lengths, hidden_in, stats_in, other_stats_in, gain, conv_weight)

    first, second, partly = lax.optimization_barrier((first, second, partly))
    wide = lambda n: pltpu.VMEM((2, n, heads_width), jnp.bfloat16)
    attended_end = pl.pallas_call(
        functools.partial(attend_ends, frames),
        out_shape=jax.ShapeDtypeStruct((ends, heads_width), jnp.bfloat16),
        in_specs=[SMEM, SMEM, hbm, hbm, hbm, anywhere, anywhere],
        out_specs=vmem,
        scratch_shapes=[
            pltpu.VMEM((2, REACH, SPAN), jnp.float32), wide(REACH), wide(SPAN), wide(SPAN), pltpu.SemaphoreType.DMA((12,)),
        ],
        compiler_params=params(16),
        cost_estimate=cost(5),
        name="attend_ends",
    )(record_starts, record_lengths, queries, attn_keys, attn_values, first, second)

    other_end = lax.ppermute(attended_end, "tp", swap)
    hidden_end, stats_end = projection(False, attended_end, other_end, 4, "project_ends")
    other_stats_end = lax.ppermute(stats_end, "tp", swap)

    more = 2 * EDGE
    rows = REACH + more
    return pl.pallas_call(
        functools.partial(norm_conv_ends, frames),
        grid=(width // LANES,),
        out_shape=result,
        in_specs=[
            SMEM, SMEM, lane_block(ends), lane_block(more), lane_block(more, inner // more - 1),
            whole(stats_end), whole(stats_end), whole(stats_in), whole(stats_in), lane_block(1), lane_block(KERNEL),
            anywhere,
        ],
        out_specs=anywhere,
        scratch_shapes=[
            shared((2, rows)), shared((2, rows)), shared((2, rows)), shared((2, rows)), shared((2, rows)), shared((2, rows)),
            shared((2, 3, rows)), shared((9, 8)), shared((3 * EDGE,)),
            pltpu.VMEM((2, 2, REACH, LANES), jnp.bfloat16),
            pltpu.SMEM((128,), jnp.int32),
            pltpu.SemaphoreType.DMA((2, 2)),
        ],
        input_output_aliases={11: 0},
        compiler_params=params(16),
        cost_estimate=cost(5),
        name="norm_conv_ends",
    )(
        record_starts, record_lengths, hidden_end, hidden_in, hidden_in, stats_end, other_stats_end, stats_in,
        other_stats_in, gain, conv_weight, partly,
    )


def solution(mesh):
    placed = (
        P(("grp", "seq"), "tp"),
        P(("grp", "seq"), "tp"),
        P(("grp", "seq"), "tp"),
        P("tp", None),
        P(("grp", "seq"), "tp"),
        P("tp"),
        P(None, "tp"),
        P("grp"),
        P("grp"),
    )
    return jax.shard_map(
        on_device, mesh=mesh, in_specs=placed, out_specs=P(("grp", "seq"), "tp"), check_vma=False
    )
```

time: 75.1 us -> 57.6 us (0.77)
  Pallas kernels: 54.8 us -> 44.5 us
  local copies, waits for them, and re-layouts: 7.55 us -> 0.04 us
  waiting for transfers between devices: 3.16 us -> 5.81 us
  starting transfers between devices: 8.82 us -> 6.88 us
    pallas_call x4, Pallas kernels: 33.1 us -> 22.5 us  [the longest x1 8.3 us: on_device(): pl.pallas_call(functools.partial(attend_inner, frames), out_shape=[jax.Sh...]
    unnamed x28 -> x16, local copies, waits for them, and re-layouts: 6.74 us -> 0.04 us
    ppermute x3, starting transfers between devices: 6.85 us -> 3.99 us  [the longest x1 2.01 us: on_device(): lax.ppermute(second_edge, 'seq', [(i, (i + 1 ^ 1) - 1) for i in range(1,...]
    ppermute x3, waiting for transfers between devices: 0.01 us -> 2.67 us  [the longest x1 2.66 us: on_device(): first = lax.ppermute(first_edge, 'seq', [(i, i ^ 1) for i in range(count)])]
    pallas_call x1, Pallas kernels: 2.39 us -> 3.79 us  [on_device(): pl.pallas_call(functools.partial(pack_edges, frames), out_shape=[edges, e...]
    pallas_call x1, Pallas kernels: 11.9 us -> 11 us  [on_device(): pl.pallas_call(functools.partial(norm_conv_inner, frames), grid=(width //...]
    ppermute x1, starting transfers between devices: 0.42 us -> 1.25 us  [on_device(): other_end = lax.ppermute(attended_end, 'tp', swap)]
    slice x1 -> x0, local copies, waits for them, and re-layouts: 0.8 us -> none  [edge_rows(): return jnp.concatenate([received[:EDGE], received[EDGE:2 * EDGE]], axis=1)]
  transfers between devices with their start and end apart: 7 -> 7, of which waited for: 3 -> 4; matrix products, arithmetic and copies ran while one was open for 0% -> 0% of each run, Pallas kernels for 47% -> 43%
where the time goes in v3:
time: 57.6 us; the launch traced here: 57.3 us
  Pallas kernels  44.5 us (77%)
  starting transfers between devices  6.88 us (12%)
  waiting for transfers between devices  5.81 us (10%)
    pallas_call x1, Pallas kernels, on_device(): pl.pallas_call(functools.partial(norm_conv_inner, frames), grid=(width //...  11 us
    pallas_call x1, Pallas kernels, on_device(): pl.pallas_call(functools.partial(attend_inner, frames), out_shape=[jax.Sh...  8.3 us
    pallas_call x2, Pallas kernels, projection(): pl.pallas_call(functools.partial(project, inside), in_specs=[anywhere] *...  7.87 us
    pallas_call x1, Pallas kernels, on_device(): pl.pallas_call(functools.partial(norm_conv_ends, frames), grid=(width //...  7.18 us
    pallas_call x1, Pallas kernels, on_device(): pl.pallas_call(functools.partial(attend_ends, frames), out_shape=jax.Shap...  6.29 us
    pallas_call x1, Pallas kernels, on_device(): pl.pallas_call(functools.partial(pack_edges, frames), out_shape=[edges, e...  3.79 us
    ppermute x1, waiting for transfers between devices, on_device(): first = lax.ppermute(first_edge, 'seq', [(i, i ^ 1) for i in range(count)])  2.66 us
    ppermute x1, starting transfers between devices, on_device(): lax.ppermute(second_edge, 'seq', [(i, (i + 1 ^ 1) - 1) for i in range(1,...  2.01 us
  transfers between devices with their start and end apart: 7, of which 4 were waited for; matrix products, arithmetic and copies ran while one was open for 0% of the time, Pallas kernels for 43%

profile of v3, /device:TPU:17, one launch (start us, length us, event | category | flops | bytes accessed | tf_op | source)
XLA Modules:
  0.0 57.3 jit_solution(524402625226040953)
XLA Ops:
  0.0 3.8 %pack_edges.1 = (bf16[336,768]{1,0:T(8,128)(2,1)S(1)}, bf16[336,768]{1,0:T(8,128)(2,1)S(1)}, bf16[768,1536]{1,0:T(8,128)(2,1)}) custom-call(bf16[1024,768]{1,0:T(8,128)(2,1)} %q_hbm.1, bf16[1024,768]{1,0:T(8,128)(2,1)} %k_hbm.3, bf16[1024,768]{1,0:T(8,128)(2,1)} %v_hbm.3, bf16[1024,1536]{1,0:T(8,128)(2,1)} %r_hbm.3, bf16[768,3072]{1,0:T(8,128)(2,1)} %w_hbm.1), custom_call_target="tpu_custom_call" | custom-call | tf_op jit(solution)/shard_map/pack_edges/pallas_call | solution.py:532
  3.8 0.7 %collective-permute-start.3 = (bf16[768,1536]{1,0:T(8,128)(2,1)}, bf16[768,1536]{1,0:T(8,128)(2,1)S(1)}, u32[]{:S(2)}, u32[]{:S(2)}) collective-permute-start(bf16[768,1536]{1,0:T(8,128)(2,1)} %get-tuple-element.28), channel_id=1, source_target_pairs={{0,1},{1,0},{2,3},{3,2},{4,5},{5,4},{6,7},{7,6},{8,9},{9,8},{10,11... | collective-permute-start | bytes 7077896 | tf_op jit(solution)/shard_map/ppermute | solution.py:544
  4.6 8.3 %attend_inner.1 = (bf16[768,768]{1,0:T(8,128)(2,1)S(1)}, bf16[768,1536]{1,0:T(8,128)(2,1)S(1)}, bf16[768,1536]{1,0:T(8,128)(2,1)S(1)}) custom-call(s32[8]{0:T(128)S(1)} %copy-done.5, s32[8]{0:T(128)S(1)} %copy-done.6, bf16[1024,768]{1,0:T(8,128)(2,1)S(1)} %copy-done.1, bf16[1024,768]{1,0:T(8,128)(2,1)S(1)} %copy-done.2, bf16[1024,768]{1,0:T(8,128)(2,1)S(1)} %copy-done.3, ...), custom_call_target="tpu_custom_call" | custom-call | flops 80000000 | bytes 1000 | tf_op jit(solution)/shard_map/attend_inner/pallas_call | solution.py:548
  12.9 0.2 collective-permute-start.2
  13.1 1.2 %collective-permute-start = (bf16[336,768]{1,0:T(8,128)(2,1)S(1)}, bf16[336,768]{1,0:T(8,128)(2,1)S(1)}, u32[]{:S(2)}, u32[]{:S(2)}) collective-permute-start(bf16[336,768]{1,0:T(8,128)(2,1)S(1)} %get-tuple-element.24.first_hbm), channel_id=1, source_target_pairs={{0,2},{2,0},{4,6},{6,4},{8,10},{10,8},{12,14},{14,12},{1,3},{3,1},... | collective-permute-start | bytes 1548296 | tf_op jit(solution)/shard_map/ppermute | solution.py:542
  14.4 2.0 %collective-permute-start.1 = (bf16[336,768]{1,0:T(8,128)(2,1)S(1)}, bf16[336,768]{1,0:T(8,128)(2,1)S(1)}, u32[]{:S(2)}, u32[]{:S(2)}) collective-permute-start(bf16[336,768]{1,0:T(8,128)(2,1)S(1)} %get-tuple-element.25.second_hbm), channel_id=1, source_target_pairs={{2,4},{4,2},{6,8},{8,6},{10,12},{12,10},{3,5},{5,3},{7,9},{9,7},{1... | collective-permute-start | bytes 1548296 | tf_op jit(solution)/shard_map/ppermute | solution.py:543
  16.4 0.0 collective-permute-done.2.other_hbm
  16.4 0.0 collective-permute-done.3.w_other_hbm
  16.4 0.0 copy-start.7
  16.4 0.0 copy-start.4
  16.4 5.2 %project_inner.1 = (f32[768,1536]{1,0:T(8,128)S(1)}, f32[16,768]{1,0:T(8,128)S(1)}) custom-call(bf16[768,768]{1,0:T(8,128)(2,1)S(1)} %get-tuple-element.26.own_hbm, bf16[768,768]{1,0:T(8,128)(2,1)S(1)} %collective-permute-done.2.other_hbm, bf16[768,1536]{1,0:T(8,128)(2,1)S(1)} %get-tuple-element.27.w_own_hbm, ...), custom_call_target="tpu_custom_call" | custom-call | flops 80000000 | bytes 1000 | tf_op jit(solution)/shard_map/project_inner/pallas_call | solution.py:574
  21.6 1.0 %collective-permute-start.4 = (f32[16,768]{1,0:T(8,128)S(1)}, f32[16,768]{1,0:T(8,128)S(1)}, u32[]{:S(2)}, u32[]{:S(2)}) collective-permute-start(f32[16,768]{1,0:T(8,128)S(1)} %get-tuple-element.31.own_ref.s_in_ref), channel_id=1, source_target_pairs={{0,1},{1,0},{2,3},{3,2},{4,5},{5,4},{6,7},{7,6},{8,9},{9,8},{10,11... | collective-permute-start | bytes 147464 | tf_op jit(solution)/shard_map/ppermute | solution.py:596
  22.6 0.9 %collective-permute-done.4.other_ref.t_in_ref = f32[16,768]{1,0:T(8,128)S(1)} collective-permute-done((f32[16,768]{1,0:T(8,128)S(1)}, f32[16,768]{1,0:T(8,128)S(1)}, u32[]{:S(2)}, u32[]{:S(2)}) %collective-permute-start.4) | collective-permute-done | bytes 49184 | tf_op jit(solution)/shard_map/ppermute | solution.py:596
  23.5 11.0 %norm_conv_inner.1.done_ref = bf16[1024,1536]{1,0:T(8,128)(2,1)} custom-call(s32[8]{0:T(128)S(1)} %copy-done.5, s32[8]{0:T(128)S(1)} %copy-done.6, f32[768,1536]{1,0:T(8,128)S(1)} %get-tuple-element.30.h_ref.h_low_ref.h_high_ref, f32[16,768]{1,0:T(8,128)S(1)} %get-tuple-element.31.own_ref.s_in_ref, f32[16,768]{1,0:T(8,128)S(1)} %collective-permute-done.4.other_ref.t_in_ref, ...), custom_call_target="tpu_custom_call" | custom-call | flops 80000000 | bytes 1000 | tf_op jit(solution)/shard_map/norm_conv_inner/pallas_call | solution.py:604
  34.5 0.0 copy-start
  34.5 2.7 %collective-permute-done.first_hbm = bf16[336,768]{1,0:T(8,128)(2,1)S(1)} collective-permute-done((bf16[336,768]{1,0:T(8,128)(2,1)S(1)}, bf16[336,768]{1,0:T(8,128)(2,1)S(1)}, u32[]{:S(2)}, u32[]{:S(2)}) %collective-permute-start) | collective-permute-done | bytes 516128 | tf_op jit(solution)/shard_map/ppermute | solution.py:542
  37.2 0.0 collective-permute-done.1.second_hbm
  37.2 6.3 %attend_ends.1.own_hbm = bf16[288,768]{1,0:T(8,128)(2,1)S(1)} custom-call(s32[8]{0:T(128)S(1)} %copy-done.5, s32[8]{0:T(128)S(1)} %copy-done.6, bf16[1024,768]{1,0:T(8,128)(2,1)S(1)} %copy-done.1, bf16[1024,768]{1,0:T(8,128)(2,1)S(1)} %copy-done.2, bf16[1024,768]{1,0:T(8,128)(2,1)S(1)} %copy-done.3, bf16[336,768]{1,0:T(8,128)(2,1)S(1)} %collective-permute-done.first_hbm, ...), custom_call_target="tpu_custom_call" | custom-call | flops 2000000000 | bytes 1000 | tf_op jit(solution)/shard_map/attend_ends/pallas_call | solution.py:624
  43.5 1.3 %collective-permute-start.5 = (bf16[288,768]{1,0:T(8,128)(2,1)S(1)}, bf16[288,768]{1,0:T(8,128)(2,1)S(1)}, u32[]{:S(2)}, u32[]{:S(2)}) collective-permute-start(bf16[288,768]{1,0:T(8,128)(2,1)S(1)} %attend_ends.1.own_hbm), channel_id=1, source_target_pairs={{0,1},{1,0},{2,3},{3,2},{4,5},{5,4},{6,7},{7,6},{8,9},{9,8},{10,11... | collective-permute-start | bytes 1327112 | tf_op jit(solution)/shard_map/ppermute | solution.py:637
  44.7 1.4 %collective-permute-done.5.other_hbm = bf16[288,768]{1,0:T(8,128)(2,1)S(1)} collective-permute-done((bf16[288,768]{1,0:T(8,128)(2,1)S(1)}, bf16[288,768]{1,0:T(8,128)(2,1)S(1)}, u32[]{:S(2)}, u32[]{:S(2)}) %collective-permute-start.5) | collective-permute-done | bytes 442400 | tf_op jit(solution)/shard_map/ppermute | solution.py:637
  46.1 2.7 %project_ends.1 = (f32[288,1536]{1,0:T(8,128)S(1)}, f32[16,384]{1,0:T(8,128)S(1)}) custom-call(bf16[288,768]{1,0:T(8,128)(2,1)S(1)} %attend_ends.1.own_hbm, bf16[288,768]{1,0:T(8,128)(2,1)S(1)} %collective-permute-done.5.other_hbm, bf16[768,1536]{1,0:T(8,128)(2,1)S(1)} %get-tuple-element.27.w_own_hbm, ...), custom_call_target="tpu_custom_call" | custom-call | flops 1600000000 | bytes 1000 | tf_op jit(solution)/shard_map/project_ends/pallas_call | solution.py:574
  48.8 0.4 collective-permute-start.6
  49.3 0.8 %collective-permute-done.6.t_end_ref = f32[16,384]{1,0:T(8,128)S(1)} collective-permute-done((f32[16,384]{1,0:T(8,128)S(1)}, f32[16,384]{1,0:T(8,128)S(1)}, u32[]{:S(2)}, u32[]{:S(2)}) %collective-permute-start.6) | collective-permute-done | bytes 24608 | tf_op jit(solution)/shard_map/ppermute | solution.py:639
  50.1 7.2 %norm_conv_ends.1 = bf16[1024,1536]{1,0:T(8,128)(2,1)} custom-call(s32[8]{0:T(128)S(1)} %copy-done.5, s32[8]{0:T(128)S(1)} %copy-done.6, f32[288,1536]{1,0:T(8,128)S(1)} %get-tuple-element.34.h_end_ref, f32[768,1536]{1,0:T(8,128)S(1)} %get-tuple-element.30.h_ref.h_low_ref.h_high_ref, ...), custom_call_target="tpu_custom_call", output_to_operand_aliasing={{}: (11, {})} | custom-call | flops 2000000000 | bytes 1000 | tf_op jit(solution)/shard_map/norm_conv_ends/pallas_call | solution.py:643
  (14 shorter events, 0.0 us)
Async XLA Ops:
  0.0 4.6 %copy-start.3 = (bf16[1024,768]{1,0:T(8,128)(2,1)S(1)}, bf16[1024,768]{1,0:T(8,128)(2,1)}, u32[]{:S(2)}) copy-start(bf16[1024,768]{1,0:T(8,128)(2,1)} %v_hbm.3) | copy-start | bytes 4718596
  0.0 4.6 %copy-start.2 = (bf16[1024,768]{1,0:T(8,128)(2,1)S(1)}, bf16[1024,768]{1,0:T(8,128)(2,1)}, u32[]{:S(2)}) copy-start(bf16[1024,768]{1,0:T(8,128)(2,1)} %k_hbm.3) | copy-start | bytes 4718596
  0.0 4.6 %copy-start.1 = (bf16[1024,768]{1,0:T(8,128)(2,1)S(1)}, bf16[1024,768]{1,0:T(8,128)(2,1)}, u32[]{:S(2)}) copy-start(bf16[1024,768]{1,0:T(8,128)(2,1)} %q_hbm.1) | copy-start | bytes 4718596
  0.0 4.6 %copy-start.6 = (s32[8]{0:T(128)S(1)}, s32[8]{0:T(128)}, u32[]{:S(2)}) copy-start(s32[8]{0:T(128)} %lengths_ref.7) | copy-start | bytes 100
  0.0 4.6 %copy-start.5 = (s32[8]{0:T(128)S(1)}, s32[8]{0:T(128)}, u32[]{:S(2)}) copy-start(s32[8]{0:T(128)} %starts_ref.7) | copy-start | bytes 100
  3.8 12.6 %collective-permute-start.3 = (bf16[768,1536]{1,0:T(8,128)(2,1)}, bf16[768,1536]{1,0:T(8,128)(2,1)S(1)}, u32[]{:S(2)}, u32[]{:S(2)}) collective-permute-start(bf16[768,1536]{1,0:T(8,128)(2,1)} %get-tuple-element.28), channel_id=1, source_target_pairs={{0,1},{1,0},{2,3},{3,2},{4,5},{5,4},{6,7},{7,6},{8,9},{9,8},{10,11... | collective-permute-start | bytes 7077896 | tf_op jit(solution)/shard_map/ppermute | solution.py:544
  12.9 3.5 %collective-permute-start.2 = (bf16[768,768]{1,0:T(8,128)(2,1)S(1)}, bf16[768,768]{1,0:T(8,128)(2,1)S(1)}, u32[]{:S(2)}, u32[]{:S(2)}) collective-permute-start(bf16[768,768]{1,0:T(8,128)(2,1)S(1)} %get-tuple-element.26.own_hbm), channel_id=1, source_target_pairs={{0,1},{1,0},{2,3},{3,2},{4,5},{5,4},{6,7},{7,6},{8,9},{9,8},{10,11... | collective-permute-start | bytes 3538952 | tf_op jit(solution)/shard_map/ppermute | solution.py:594
  13.1 24.0 %collective-permute-start = (bf16[336,768]{1,0:T(8,128)(2,1)S(1)}, bf16[336,768]{1,0:T(8,128)(2,1)S(1)}, u32[]{:S(2)}, u32[]{:S(2)}) collective-permute-start(bf16[336,768]{1,0:T(8,128)(2,1)S(1)} %get-tuple-element.24.first_hbm), channel_id=1, source_target_pairs={{0,2},{2,0},{4,6},{6,4},{8,10},{10,8},{12,14},{14,12},{1,3},{3,1},... | collective-permute-start | bytes 1548296 | tf_op jit(solution)/shard_map/ppermute | solution.py:542
  14.4 22.8 %collective-permute-start.1 = (bf16[336,768]{1,0:T(8,128)(2,1)S(1)}, bf16[336,768]{1,0:T(8,128)(2,1)S(1)}, u32[]{:S(2)}, u32[]{:S(2)}) collective-permute-start(bf16[336,768]{1,0:T(8,128)(2,1)S(1)} %get-tuple-element.25.second_hbm), channel_id=1, source_target_pairs={{2,4},{4,2},{6,8},{8,6},{10,12},{12,10},{3,5},{5,3},{7,9},{9,7},{1... | collective-permute-start | bytes 1548296 | tf_op jit(solution)/shard_map/ppermute | solution.py:543
  16.4 6.2 %copy-start.7 = (f32[1536]{0:T(1024)S(1)}, f32[1536]{0:T(1024)}, u32[]{:S(2)}) copy-start(f32[1536]{0:T(1024)} %param.14) | copy-start | bytes 18436
  16.4 7.1 %copy-start.4 = (f32[31,1536]{1,0:T(8,128)S(1)}, f32[31,1536]{1,0:T(8,128)}, u32[]{:S(2)}) copy-start(f32[31,1536]{1,0:T(8,128)} %w_ref.5) | copy-start | bytes 571396
  21.6 1.9 %collective-permute-start.4 = (f32[16,768]{1,0:T(8,128)S(1)}, f32[16,768]{1,0:T(8,128)S(1)}, u32[]{:S(2)}, u32[]{:S(2)}) collective-permute-start(f32[16,768]{1,0:T(8,128)S(1)} %get-tuple-element.31.own_ref.s_in_ref), channel_id=1, source_target_pairs={{0,1},{1,0},{2,3},{3,2},{4,5},{5,4},{6,7},{7,6},{8,9},{9,8},{10,11... | collective-permute-start | bytes 147464 | tf_op jit(solution)/shard_map/ppermute | solution.py:596
  34.5 11.7 %copy-start = (bf16[1024,1536]{1,0:T(8,128)(2,1)S(1)}, bf16[1024,1536]{1,0:T(8,128)(2,1)}, u32[]{:S(2)}) copy-start(bf16[1024,1536]{1,0:T(8,128)(2,1)} %r_hbm.3) | copy-start | bytes 9437188
  43.5 2.7 %collective-permute-start.5 = (bf16[288,768]{1,0:T(8,128)(2,1)S(1)}, bf16[288,768]{1,0:T(8,128)(2,1)S(1)}, u32[]{:S(2)}, u32[]{:S(2)}) collective-permute-start(bf16[288,768]{1,0:T(8,128)(2,1)S(1)} %attend_ends.1.own_hbm), channel_id=1, source_target_pairs={{0,1},{1,0},{2,3},{3,2},{4,5},{5,4},{6,7},{7,6},{8,9},{9,8},{10,11... | collective-permute-start | bytes 1327112 | tf_op jit(solution)/shard_map/ppermute | solution.py:637
  48.8 1.3 %collective-permute-start.6 = (f32[16,384]{1,0:T(8,128)S(1)}, f32[16,384]{1,0:T(8,128)S(1)}, u32[]{:S(2)}, u32[]{:S(2)}) collective-permute-start(f32[16,384]{1,0:T(8,128)S(1)} %get-tuple-element.35.s_end_ref), channel_id=1, source_target_pairs={{0,1},{1,0},{2,3},{3,2},{4,5},{5,4},{6,7},{7,6},{8,9},{9,8},{10,11... | collective-permute-start | bytes 73736 | tf_op jit(solution)/shard_map/ppermute | solution.py:639

commit v4 on v3

--- a/solution.py
+++ b/solution.py
@@ -56,18 +56,15 @@
 
 
 def head_pair(query, keys, values, bias):
-    rows = query.shape[0]
-    left = lax.broadcasted_iota(jnp.int32, query.shape, 1) < HSIZE
-    nothing = jnp.zeros_like(query)
-    both = jnp.concatenate([jnp.where(left, query, nothing), jnp.where(left, nothing, query)], axis=0)
-    scores = lax.dot_general(both, keys, (((1,), (1,)), ((), ())), preferred_element_type=jnp.float32)
-    scores = scores + jnp.concatenate([bias, bias], axis=0)
-    row_max = jnp.max(scores, axis=1, keepdims=True)
-    weights = jnp.exp2((scores - row_max) * EXP_SCALE).astype(jnp.bfloat16)
-    mixed = jnp.dot(weights, values, preferred_element_type=jnp.float32)
-    mixed = mixed[:, :LANES] / mixed[:, LANES:]
-    keep = bias_any(bias)
-    return jnp.where(keep, jnp.where(left, mixed[:rows], mixed[rows:]), 0.0).astype(jnp.bfloat16)
+    span = bias.shape[1]
+    scores = lax.dot_general(query, keys, (((1,), (1,)), ((), ())), preferred_element_type=jnp.float32)
+    weights = []
+    for h in range(2):
+        part = scores[:, h * span : (h + 1) * span] + bias
+        row_max = jnp.max(part, axis=1, keepdims=True)
+        weights.append(jnp.exp2((part - row_max) * EXP_SCALE).astype(jnp.bfloat16))
+    mixed = jnp.dot(jnp.concatenate(weights, axis=1), values, preferred_element_type=jnp.float32)
+    return jnp.where(bias_any(bias), mixed[:, :LANES] / mixed[:, LANES:], 0.0).astype(jnp.bfloat16)
 
 
 def bias_any(bias):
@@ -130,23 +127,12 @@
         values[0, :, :LANES], values[1, :, :LANES] = split_heads(columns[p, 2])
         for i in range(blocks):
             window = slice(i * WIN, i * WIN + span)
-            both = jnp.concatenate([keys[0, window, :], keys[1, window, :]], axis=0)
-            scores = lax.dot_general(
-                columns[p, 0, (i + 1) * WIN : (i + 2) * WIN, :], both, (((1,), (1,)), ((), ())),
-                preferred_element_type=jnp.float32,
+            o_ref[i * WIN : (i + 1) * WIN, lanes] = head_pair(
+                columns[p, 0, (i + 1) * WIN : (i + 2) * WIN, :],
+                jnp.concatenate([keys[0, window, :], keys[1, window, :]], axis=0),
+                jnp.concatenate([values[0, window, :], values[1, window, :]], axis=0),
+                bias[i],
             )
-            weights = []
-            for h in range(2):
-                part = scores[:, h * span : (h + 1) * span] + bias[i]
-                row_max = jnp.max(part, axis=1, keepdims=True)
-                weights.append(jnp.exp2((part - row_max) * EXP_SCALE).astype(jnp.bfloat16))
-            mixed = jnp.dot(
-                jnp.concatenate(weights, axis=1),
-                jnp.concatenate([values[0, window, :], values[1, window, :]], axis=0),
-                preferred_element_type=jnp.float32,
-            )
-            mixed = jnp.where(bias_any(bias[i]), mixed[:, :LANES] / mixed[:, LANES:], 0.0)
-            o_ref[i * WIN : (i + 1) * WIN, lanes] = mixed.astype(jnp.bfloat16)
         return carry
 
     lax.fori_loop(0, pairs, one_pair, 0)
@@ -184,20 +170,20 @@
 
         band_bias(anchor + base, REACH, anchor + key_base, SPAN, starts_ref, lengths_ref, store)
     wait_all(copies)
-    ones = jnp.ones((SPAN, LANES), jnp.bfloat16)
-
-    def one_pair(p, carry):
-        lanes = pl.ds(pl.multiple_of(p * LANES, LANES), LANES)
+    ones = split_heads(jnp.ones((SPAN, LANES), jnp.bfloat16))
+    for p in range(pairs):
+        lanes = slice(p * LANES, (p + 1) * LANES)
         for i in range(2):
+            sides = [jnp.concatenate([v, one], axis=1) for v, one in zip(split_heads(values[i, :, lanes]), ones)]
             o_ref[i * REACH : (i + 1) * REACH, lanes] = head_pair(
-                query[i, :, lanes], keys[i, :, lanes], jnp.concatenate([values[i, :, lanes], ones], axis=1), bias[i]
+                query[i, :, lanes],
+                jnp.concatenate(split_heads(keys[i, :, lanes]), axis=0),
+                jnp.concatenate(sides, axis=0),
+                bias[i],
             )
-        return carry
-
-    lax.fori_loop(0, pairs, one_pair, 0, unroll=2)
-
-
-def pack_edges(frames, q_ref, k_ref, v_ref, r_ref, w_ref, first_ref, second_ref, w_send_ref, sems):
+
+
+def pack_edges(frames, q_ref, k_ref, v_ref, r_ref, first_ref, second_ref, sems):
     half = q_ref.shape[1]
     odd = lax.axis_index("seq") % 2
     copies = []
@@ -216,39 +202,50 @@
         ]
         for n, (source, at, count) in enumerate(moves):
             copies.append(pltpu.make_async_copy(source, out.at[pl.ds(at, count), :], sems.at[i, n]))
-    width = w_send_ref.shape[1]
-    left = pl.multiple_of((1 - lax.axis_index("tp")) * width, LANES)
-    copies.append(pltpu.make_async_copy(w_ref.at[:, pl.ds(left, width)], w_send_ref, sems.at[2, 0]))
     wait_all(start_all(copies))
 
 
-def project(
-    inner, own_hbm, other_hbm, w_own_hbm, w_other_hbm, r_hbm, first_hbm, second_hbm,
-    h_ref, stats_ref, left, right, residual, shift, first, second, sems,
-):
+def project_own(own_ref, w_ref, r_ref, more_hbm, o_ref, more_ref, sem):
+    step = 256
+    width = more_ref.shape[1]
+    left = pl.multiple_of(lax.axis_index("tp") * width, LANES)
+    later = pltpu.make_async_copy(more_hbm.at[:, pl.ds(left, width)], more_ref, sem)
+    later.start()
+    for left in range(0, o_ref.shape[1], step):
+        cols = slice(left, left + step)
+        part = jnp.dot(own_ref[...], w_ref[:, cols], preferred_element_type=jnp.float32)
+        o_ref[:, cols] = part + r_ref[:, cols].astype(jnp.float32)
+    later.wait()
+
+
+def project(inner, *refs):
+    if inner:
+        other_hbm, w_other_hbm, base, h_ref, stats_ref, left, right, shift, first, second, sems = refs
+    else:
+        (own_hbm, other_hbm, w_own_hbm, w_other_hbm, r_hbm, first_hbm, second_hbm,
+         h_ref, stats_ref, left, right, base, shift, first, second, sems) = refs
     rows, width = h_ref.shape
-    half = own_hbm.shape[1]
+    half = other_hbm.shape[1]
     step = 256
     copies = []
 
     def move(source, target):
         copies.append(pltpu.make_async_copy(source, target, sems.at[len(copies)]))
 
-    move(own_hbm, left.at[:, pl.ds(0, half)])
-    move(w_own_hbm, right.at[pl.ds(0, half), :])
-    move(other_hbm, left.at[:, pl.ds(half, half)])
-    move(w_other_hbm, right.at[pl.ds(half, half), :])
-    if inner:
-        move(r_hbm, residual)
-    else:
+    at = left.shape[1] - half
+    move(other_hbm, left.at[:, pl.ds(at, half)])
+    move(w_other_hbm, right.at[pl.ds(at, half), :])
+    if not inner:
+        move(own_hbm, left.at[:, pl.ds(0, half)])
+        move(w_own_hbm, right.at[pl.ds(0, half), :])
         frames = r_hbm.shape[0]
-        move(r_hbm.at[pl.ds(0, WIN), :], residual.at[pl.ds(EDGE, WIN), :])
-        move(r_hbm.at[pl.ds(frames - WIN, WIN), :], residual.at[pl.ds(REACH, WIN), :])
+        move(r_hbm.at[pl.ds(0, WIN), :], base.at[pl.ds(EDGE, WIN), :])
+        move(r_hbm.at[pl.ds(frames - WIN, WIN), :], base.at[pl.ds(REACH, WIN), :])
         side = halo_side()
         for halo, which in ((first_hbm, side), (second_hbm, 1 - side)):
-            at = pl.ds(pl.multiple_of(which * (REACH + WIN), EDGE), EDGE)
+            target = pl.ds(pl.multiple_of(which * (REACH + WIN), EDGE), EDGE)
             for n in range(2):
-                move(halo.at[pl.ds(n * EDGE, EDGE), :], residual.at[at, pl.ds(n * half, half)])
+                move(halo.at[pl.ds(n * EDGE, EDGE), :], base.at[target, pl.ds(n * half, half)])
     wait_all(start_all(copies))
 
     def gather(j):
@@ -265,7 +262,7 @@
     for j in range(width // step):
         cols = slice(j * step, (j + 1) * step)
         part = jnp.dot(left[...], right[:, cols], preferred_element_type=jnp.float32)
-        h_ref[:, cols] = part + residual[:, cols].astype(jnp.float32)
+        h_ref[:, cols] = part + base[:, cols].astype(jnp.float32)
         if j == 0:
             mean = jnp.sum(h_ref[:, cols], axis=1, keepdims=True) * (1.0 / step)
             shift[...] = jnp.broadcast_to(mean, (rows, LANES))
@@ -284,20 +281,29 @@
             stats_ref[8 * k : 8 * k + 8, top : top + LANES] = jnp.transpose(tile)[:8, :]
 
 
-def stat_columns(base, own, other, width, starts_ref, lengths_ref):
+def recording_of(base, starts_ref, lengths_ref):
     positions = base + lax.broadcasted_iota(jnp.int32, (1, LANES), 1)
     index = jnp.zeros((1, LANES), jnp.int32) - 1
     for r in range(REC):
         start = starts_ref[r]
         inside = (positions >= start) & (positions < start + lengths_ref[r])
         index = jnp.where(inside, r, index)
+    return index
+
+
+def stat_columns(base, own, other, width, starts_ref, lengths_ref):
+    inside = recording_of(base, starts_ref, lengths_ref) >= 0
     gap = own[0:1, :] - other[0:1, :]
     middle = 0.5 * (own[0:1, :] + other[0:1, :])
     var = (own[8:9, :] + other[8:9, :] + gap * gap * (width * 0.25)) * (1.0 / width)
-    inverse = jnp.where(index >= 0, lax.rsqrt(var + 1e-5), 0.0)
-    parity = jnp.where(index >= 0, (index % 2).astype(jnp.float32), -1.0)
-    halves = jnp.where(index >= 0, 0.5, 0.0)
-    return as_column(middle), as_column(inverse), as_column(parity), as_column(halves)
+    inverse = jnp.where(inside, lax.rsqrt(var + 1e-5), 0.0)
+    deviation = as_column(inverse)
+    return as_column(middle), deviation, jnp.where(deviation > 0, 0.5, 0.0)
+
+
+def parity_column(base, starts_ref, lengths_ref):
+    index = recording_of(base, starts_ref, lengths_ref)
+    return as_column(jnp.where(index >= 0, (index % 2).astype(jnp.float32), -1.0))
 
 
 def mark_mixed(base, chunks, flags, at, starts_ref, lengths_ref):
@@ -370,6 +376,7 @@
 
 def conv_rows(rows, hidden, normed, parity, halves, diffs, wq, masked, flags, flag_at, w_ref, out):
     differences(normed, diffs)
+    tap_sums(w_ref, wq)
     group = 2 * EDGE
     tops = list(range(0, rows - group, group)) + [rows - group]
     for start in range(0, len(tops), SHARE):
@@ -399,35 +406,43 @@
     mean, scale, parity, halves, normed, diffs, wq, masked, out, flags, sems,
 ):
     step, steps = pl.program_id(0), pl.num_programs(0)
-    rows = frames - 2 * WIN
+    rows, wide = h_ref.shape
     kept = rows - 2 * EDGE
     base = lax.axis_index("seq") * frames + WIN
 
     @pl.when(step == 0)
     def _():
-        width = 2.0 * LANES * steps
+        width = 2.0 * wide * steps
+        mark_mixed(base + EDGE, kept // EDGE, flags, 0, starts_ref, lengths_ref)
         for top in range(0, rows, LANES):
             here = slice(top, top + LANES)
-            mean[here, :], scale[here, :], parity[here, :], halves[here, :] = stat_columns(
+            mean[here, :], scale[here, :], halves[here, :] = stat_columns(
                 base + top, own_ref[:, here], other_ref[:, here], width, starts_ref, lengths_ref
             )
-        mark_mixed(base + EDGE, kept // EDGE, flags, 0, starts_ref, lengths_ref)
-
-    value = (h_ref[...] - mean[...]) * scale[...] * gain_ref[...]
-    normed[...] = value.astype(jnp.bfloat16).astype(jnp.float32)
+
+        @pl.when(flags[0] > 0)
+        def _():
+            for top in range(0, rows, LANES):
+                parity[top : top + LANES, :] = parity_column(base + top, starts_ref, lengths_ref)
+
     slot = step % 2
 
     def copy(at, which):
-        return pltpu.make_async_copy(
-            out.at[which], o_ref.at[pl.ds(WIN + EDGE, kept), pl.ds(pl.multiple_of(at * LANES, LANES), LANES)], sems.at[which]
-        )
+        lanes = pl.ds(pl.multiple_of(at * wide, LANES), wide)
+        return pltpu.make_async_copy(out.at[which], o_ref.at[pl.ds(WIN + EDGE, kept), lanes], sems.at[which])
 
     @pl.when(step >= 2)
     def _():
         copy(step - 2, slot).wait()
 
-    tap_sums(w_ref, wq)
-    conv_rows(kept, h_ref, normed, parity, halves, diffs, wq, masked, flags, 0, w_ref, out.at[slot])
+    for u in range(wide // LANES):
+        lanes = slice(u * LANES, (u + 1) * LANES)
+        value = (h_ref[:, lanes] - mean[...]) * scale[...] * gain_ref[:, lanes]
+        normed[u] = value.astype(jnp.bfloat16).astype(jnp.float32)
+        conv_rows(
+            kept, h_ref.at[:, lanes], normed.at[u], parity, halves, diffs.at[u], wq.at[u], masked, flags, 0,
+            w_ref.at[:, lanes], out.at[slot, :, lanes],
+        )
     copy(step, slot).start()
 
     @pl.when(step == steps - 1)
@@ -445,39 +460,35 @@
     anchor = lax.axis_index("seq") * frames
     more = 2 * EDGE
     rows = REACH + more
+    wide = h_end_ref.shape[1]
 
     @pl.when(step == 0)
     def _():
-        width = 2.0 * LANES * steps
-
-        def place(i, at, count, base, lane, own, other, skip):
-            values = stat_columns(
-                base, own[:, lane : lane + LANES], other[:, lane : lane + LANES], width, starts_ref, lengths_ref
-            )
-            for ref, value in zip((mean, scale, parity, halves), values):
-                ref[i, at : at + count, :] = value[skip : skip + count]
-
-        for top, count in ((0, LANES), (LANES, EDGE)):
-            place(0, top, count, anchor - EDGE + top, top, s_end_ref, t_end_ref, 0)
-        place(0, REACH, more, anchor + WIN, 0, s_in_ref, t_in_ref, 0)
-        place(1, 0, more, anchor + frames - 2 * WIN, inner - LANES, s_in_ref, t_in_ref, LANES - more)
-        own = jnp.concatenate([s_end_ref[:, LANES : 2 * LANES], s_end_ref[:, 2 * LANES :]], axis=1)[:, EDGE : EDGE + 2 * LANES - EDGE]
-        other = jnp.concatenate([t_end_ref[:, LANES : 2 * LANES], t_end_ref[:, 2 * LANES :]], axis=1)[:, EDGE : EDGE + 2 * LANES - EDGE]
-        place(1, more, LANES, anchor + frames - WIN, 0, own, other, 0)
-        tail = jnp.concatenate([s_end_ref[:, 2 * LANES + EDGE :], jnp.zeros((16, LANES), jnp.float32)], axis=1)
-        tail2 = jnp.concatenate([t_end_ref[:, 2 * LANES + EDGE :], jnp.zeros((16, LANES), jnp.float32)], axis=1)
-        place(1, more + LANES, EDGE, anchor + frames, 0, tail, tail2, 0)
+        width = 2.0 * wide * steps
         for i in range(2):
             mark_mixed(anchor + i * (frames - REACH), REACH // EDGE, flags, i * 64, starts_ref, lengths_ref)
 
-    hidden[0, :REACH, :] = h_end_ref[:REACH, :]
-    hidden[0, REACH:, :] = h_low_ref[...]
-    hidden[1, :more, :] = h_high_ref[...]
-    hidden[1, more:, :] = h_end_ref[REACH:, :]
+        def joined(ends, ins, i):
+            if i == 0:
+                return jnp.concatenate([ends[:, :REACH], ins[:, : 2 * LANES - REACH]], axis=1)
+            return jnp.concatenate([ins[:, inner - more :], ends[:, REACH : REACH + 2 * LANES - more]], axis=1)
+
+        for i, first in enumerate((anchor - EDGE, anchor + frames - WIN - more)):
+            own, other = joined(s_end_ref, s_in_ref, i), joined(t_end_ref, t_in_ref, i)
+            for top, count in ((0, LANES), (LANES, rows - LANES)):
+                here, lanes = slice(top, top + count), slice(top, top + LANES)
+                values = stat_columns(first + top, own[:, lanes], other[:, lanes], width, starts_ref, lengths_ref)
+                for ref, value in zip((mean, scale, halves), values):
+                    ref[i, here, :] = value[:count]
+
+                @pl.when(flags[0] + flags[64] > 0)
+                def _():
+                    parity[i, here, :] = parity_column(first + top, starts_ref, lengths_ref)[:count]
+
     slot = step % 2
 
     def copies(at, which):
-        lanes = pl.ds(pl.multiple_of(at * LANES, LANES), LANES)
+        lanes = pl.ds(pl.multiple_of(at * wide, LANES), wide)
         return [
             pltpu.make_async_copy(
                 out.at[which, i], o_ref.at[pl.ds(i * (frames - REACH), REACH), lanes], sems.at[which, i]
@@ -490,14 +501,19 @@
         for copy in copies(step - 2, slot):
             copy.wait()
 
-    tap_sums(w_ref, wq)
-    for i in range(2):
-        value = (hidden[i] - mean[i]) * scale[i] * gain_ref[...]
-        normed[i] = value.astype(jnp.bfloat16).astype(jnp.float32)
-        conv_rows(
-            REACH, hidden.at[i], normed.at[i], parity.at[i], halves.at[i], diffs.at[i], wq, masked, flags, i * 64, w_ref,
-            out.at[slot, i],
-        )
+    for u in range(wide // LANES):
+        lanes = slice(u * LANES, (u + 1) * LANES)
+        hidden[u, 0, :REACH, :] = h_end_ref[:REACH, lanes]
+        hidden[u, 0, REACH:, :] = h_low_ref[:, lanes]
+        hidden[u, 1, :more, :] = h_high_ref[:, lanes]
+        hidden[u, 1, more:, :] = h_end_ref[REACH:, lanes]
+        for i in range(2):
+            value = (hidden[u, i] - mean[i]) * scale[i] * gain_ref[:, lanes]
+            normed[u, i] = value.astype(jnp.bfloat16).astype(jnp.float32)
+            conv_rows(
+                REACH, hidden.at[u, i], normed.at[u, i], parity.at[i], halves.at[i], diffs.at[u, i], wq.at[u], masked,
+                flags, i * 64, w_ref.at[:, lanes], out.at[slot, i, :, lanes],
+            )
     for copy in copies(step, slot):
         copy.start()
 
@@ -529,19 +545,19 @@
 
     edges = jax.ShapeDtypeStruct((3 * EDGE + 2 * REACH, heads_width), jnp.bfloat16)
     halved = jax.ShapeDtypeStruct((heads_width, width), jnp.bfloat16)
-    first_edge, second_edge, weight_send = pl.pallas_call(
+    first_edge, second_edge = pl.pallas_call(
         functools.partial(pack_edges, frames),
-        out_shape=[edges, edges, halved],
-        in_specs=[pl.BlockSpec(memory_space=pltpu.HBM)] * 5,
-        out_specs=[pl.BlockSpec(memory_space=pltpu.VMEM)] * 3,
-        scratch_shapes=[pltpu.SemaphoreType.DMA((3, 5))],
+        out_shape=[edges, edges],
+        in_specs=[pl.BlockSpec(memory_space=pltpu.HBM)] * 4,
+        out_specs=[pl.BlockSpec(memory_space=pltpu.VMEM)] * 2,
+        scratch_shapes=[pltpu.SemaphoreType.DMA((2, 5))],
         compiler_params=params(52),
         name="pack_edges",
-    )(queries, attn_keys, attn_values, residual, out_weight)
+    )(queries, attn_keys, attn_values, residual)
     first_edge, second_edge, queries = lax.optimization_barrier((first_edge, second_edge, queries))
     first = lax.ppermute(first_edge, "seq", [(i, i ^ 1) for i in range(count)])
     second = lax.ppermute(second_edge, "seq", [(i, ((i + 1) ^ 1) - 1) for i in range(1, count - 1)])
-    weight_other = lax.ppermute(weight_send, "tp", swap)
+    weight_both = lax.ppermute(out_weight, "tp", swap)
 
     hbm = pl.BlockSpec(memory_space=pltpu.HBM)
     vmem = pl.BlockSpec(memory_space=pltpu.VMEM)
@@ -562,26 +578,21 @@
             pltpu.SemaphoreType.DMA((2,)),
         ],
         compiler_params=params(42),
-        cost_estimate=cost(0.2),
+        cost_estimate=cost(0.001),
         name="attend_inner",
     )(record_starts, record_lengths, queries, attn_keys, attn_values, out_weight, residual)
 
-    def projection(inside, own, other, microseconds, name):
-        rows = own.shape[0]
+    def projection(inside, operands, rows, microseconds, name):
         padded = -(-rows // LANES) * LANES
         shared = pltpu.VMEM((rows, LANES), jnp.float32)
-        halos = [first_edge, second_edge] if inside else [first, second]
+        depth = heads_width if inside else 2 * heads_width
         return pl.pallas_call(
             functools.partial(project, inside),
-            in_specs=[anywhere] * 7,
+            in_specs=[anywhere, anywhere, vmem] if inside else [anywhere] * 7,
             out_specs=[vmem, vmem],
-            scratch_shapes=[
-                pltpu.VMEM((rows, 2 * heads_width), jnp.bfloat16),
-                pltpu.VMEM((2 * heads_width, width), jnp.bfloat16),
-                pltpu.VMEM((rows, width), jnp.bfloat16),
-                shared, shared, shared,
-                pltpu.SemaphoreType.DMA((10,)),
-            ],
+            scratch_shapes=[pltpu.VMEM((rows, depth), jnp.bfloat16), pltpu.VMEM((depth, width), jnp.bfloat16)]
+            + ([] if inside else [pltpu.VMEM((rows, width), jnp.bfloat16)])
+            + [shared, shared, shared, pltpu.SemaphoreType.DMA((10,))],
             out_shape=[
                 jax.ShapeDtypeStruct((rows, width), jnp.float32),
                 jax.ShapeDtypeStruct((16, padded), jnp.float32),
@@ -589,33 +600,45 @@
             compiler_params=params(24),
             cost_estimate=cost(microseconds),
             name=name,
-        )(own, other, weight_own, weight_other, residual_in if inside else residual, *halos)
+        )(*operands)
 
     other_in = lax.ppermute(attended_in, "tp", swap)
-    hidden_in, stats_in = projection(True, attended_in, other_in, 0.2, "project_inner")
+    base_in, weight_other = pl.pallas_call(
+        project_own,
+        in_specs=[vmem, vmem, vmem, hbm],
+        out_specs=[vmem, vmem],
+        out_shape=[jax.ShapeDtypeStruct((inner, width), jnp.float32), halved],
+        scratch_shapes=[pltpu.SemaphoreType.DMA],
+        compiler_params=params(8),
+        cost_estimate=cost(10),
+        name="project_own",
+    )(attended_in, weight_own, residual_in, weight_both)
+    hidden_in, stats_in = projection(True, [other_in, weight_other, base_in], inner, 0.001, "project_inner")
     other_stats_in = lax.ppermute(stats_in, "tp", swap)
 
     whole = lambda array: pl.BlockSpec(array.shape, lambda g: (0, 0))
-    lane_block = lambda n, i=0: pl.BlockSpec((n, LANES), lambda g: (i, g))
+    lane_block = lambda n, i=0: pl.BlockSpec((n, step), lambda g: (i, g))
+    step = 2 * LANES
     gain = norm_gain.reshape(1, width)
     shared = lambda n: pltpu.VMEM(n + (LANES,), jnp.float32)
     kept = inner - 2 * EDGE
     result = jax.ShapeDtypeStruct((frames, width), jnp.bfloat16)
     partly = pl.pallas_call(
         functools.partial(norm_conv_inner, frames),
-        grid=(width // LANES,),
+        grid=(width // step,),
         out_shape=result,
         in_specs=[SMEM, SMEM, lane_block(inner), whole(stats_in), whole(stats_in), lane_block(1), lane_block(KERNEL)],
         out_specs=anywhere,
         scratch_shapes=[
-            shared((inner,)), shared((inner,)), shared((inner,)), shared((inner,)), shared((inner,)), shared((3, inner)), shared((9, 8)),
+            shared((inner,)), shared((inner,)), shared((inner,)), shared((inner,)), shared((2, inner)), shared((2, 3, inner)),
+            shared((2, 9, 8)),
             shared((3 * EDGE,)),
-            pltpu.VMEM((2, kept, LANES), jnp.bfloat16),
+            pltpu.VMEM((2, kept, step), jnp.bfloat16),
             pltpu.SMEM((64,), jnp.int32),
             pltpu.SemaphoreType.DMA((2,)),
         ],
         compiler_params=params(16),
-        cost_estimate=cost(0.2),
+        cost_estimate=cost(0.001),
         name="norm_conv_inner",
     )(record_starts, record_lengths, hidden_in, stats_in, other_stats_in, gain, conv_weight)
 
@@ -635,14 +658,16 @@
     )(record_starts, record_lengths, queries, attn_keys, attn_values, first, second)
 
     other_end = lax.ppermute(attended_end, "tp", swap)
-    hidden_end, stats_end = projection(False, attended_end, other_end, 4, "project_ends")
+    hidden_end, stats_end = projection(
+        False, [attended_end, other_end, weight_own, weight_other, residual, first, second], ends, 4, "project_ends"
+    )
     other_stats_end = lax.ppermute(stats_end, "tp", swap)
 
     more = 2 * EDGE
     rows = REACH + more
     return pl.pallas_call(
         functools.partial(norm_conv_ends, frames),
-        grid=(width // LANES,),
+        grid=(width // step,),
         out_shape=result,
         in_specs=[
             SMEM, SMEM, lane_block(ends), lane_block(more), lane_block(more, inner // more - 1),
@@ -651,9 +676,9 @@
         ],
         out_specs=anywhere,
         scratch_shapes=[
-            shared((2, rows)), shared((2, rows)), shared((2, rows)), shared((2, rows)), shared((2, rows)), shared((2, rows)),
-            shared((2, 3, rows)), shared((9, 8)), shared((3 * EDGE,)),
-            pltpu.VMEM((2, 2, REACH, LANES), jnp.bfloat16),
+            shared((2, rows)), shared((2, rows)), shared((2, rows)), shared((2, rows)), shared((2, 2, rows)),
+            shared((2, 2, rows)), shared((2, 2, 3, rows)), shared((2, 9, 8)), shared((3 * EDGE,)),
+            pltpu.VMEM((2, 2, REACH, step), jnp.bfloat16),
             pltpu.SMEM((128,), jnp.int32),
             pltpu.SemaphoreType.DMA((2, 2)),
         ],

time: 57.6 us -> 55.1 us (0.957)
  Pallas kernels: 44.5 us -> 41.7 us
    pallas_call x1, Pallas kernels: 3.79 us -> 1.74 us  [on_device(): pl.pallas_call(functools.partial(pack_edges, frames), out_shape=[edges, e...]
    pallas_call x1, Pallas kernels: 6.29 us -> 5.51 us  [on_device(): pl.pallas_call(functools.partial(attend_ends, frames), out_shape=jax.Shap...]
    pallas_call x1, Pallas kernels: 7.18 us -> 6.53 us  [on_device(): pl.pallas_call(functools.partial(norm_conv_ends, frames), grid=(width //...]
    pallas_call x2 -> x3, Pallas kernels: 7.87 us -> 8.1 us  [the longest x2 5.77 us: projection(): pl.pallas_call(functools.partial(project, inside), in_specs=[anywhere, an...]
  transfers between devices with their start and end apart: 7 -> 7, of which waited for: 4 -> 4; matrix products, arithmetic and copies ran while one was open for 0% -> 0% of each run, Pallas kernels for 43% -> 49%
where the time goes in v4:
time: 55.1 us; the launch traced here: 54.8 us
  Pallas kernels  41.7 us (76%)
  starting transfers between devices  6.96 us (13%)
  waiting for transfers between devices  5.56 us (10%)
    pallas_call x1, Pallas kernels, on_device(): pl.pallas_call(functools.partial(norm_conv_inner, frames), grid=(width //...  11.5 us
    pallas_call x1, Pallas kernels, on_device(): pl.pallas_call(functools.partial(attend_inner, frames), out_shape=[jax.Sh...  8.31 us
    pallas_call x1, Pallas kernels, on_device(): pl.pallas_call(functools.partial(norm_conv_ends, frames), grid=(width //...  6.53 us
    pallas_call x2, Pallas kernels, projection(): pl.pallas_call(functools.partial(project, inside), in_specs=[anywhere, an...  5.77 us
    pallas_call x1, Pallas kernels, on_device(): pl.pallas_call(functools.partial(attend_ends, frames), out_shape=jax.Shap...  5.51 us
    ppermute x1, waiting for transfers between devices, on_device(): first = lax.ppermute(first_edge, 'seq', [(i, i ^ 1) for i in range(count)])  2.41 us
    pallas_call x1, Pallas kernels, on_device(): pl.pallas_call(project_own, in_specs=[vmem, vmem, vmem, hbm], out_specs=[...  2.33 us
    ppermute x1, starting transfers between devices, on_device(): lax.ppermute(second_edge, 'seq', [(i, (i + 1 ^ 1) - 1) for i in range(1,...  2.19 us
  transfers between devices with their start and end apart: 7, of which 4 were waited for; matrix products, arithmetic and copies ran while one was open for 0% of the time, Pallas kernels for 49%

profile of v4, /device:TPU:17, one launch (start us, length us, event | category | flops | bytes accessed | tf_op | source)
XLA Modules:
  0.0 54.8 jit_solution(9600289836898441689)
XLA Ops:
  0.0 0.7 %collective-permute-start.3 = (bf16[768,3072]{1,0:T(8,128)(2,1)}, bf16[768,3072]{1,0:T(8,128)(2,1)S(1)}, u32[]{:S(2)}, u32[]{:S(2)}) collective-permute-start(bf16[768,3072]{1,0:T(8,128)(2,1)} %w_hbm.1), channel_id=1, source_target_pairs={{0,1},{1,0},{2,3},{3,2},{4,5},{5,4},{6,7},{7,6},{8,9},{9,8},{10,11... | collective-permute-start | bytes 14155784 | tf_op jit(solution)/shard_map/ppermute | solution.py:560
  0.8 1.7 %pack_edges.1 = (bf16[336,768]{1,0:T(8,128)(2,1)S(1)}, bf16[336,768]{1,0:T(8,128)(2,1)S(1)}) custom-call(bf16[1024,768]{1,0:T(8,128)(2,1)} %q_hbm.1, bf16[1024,768]{1,0:T(8,128)(2,1)} %k_hbm.3, bf16[1024,768]{1,0:T(8,128)(2,1)} %v_hbm.3, bf16[1024,1536]{1,0:T(8,128)(2,1)} %refs_4_.1), custom_call_target="tpu_custom_call" | custom-call | tf_op jit(solution)/shard_map/pack_edges/pallas_call | solution.py:548
  2.5 0.2 copy-done.1
  2.8 8.3 %attend_inner.1 = (bf16[768,768]{1,0:T(8,128)(2,1)S(1)}, bf16[768,1536]{1,0:T(8,128)(2,1)S(1)}, bf16[768,1536]{1,0:T(8,128)(2,1)S(1)}) custom-call(s32[8]{0:T(128)S(1)} %copy-done.5, s32[8]{0:T(128)S(1)} %copy-done.6, bf16[1024,768]{1,0:T(8,128)(2,1)S(1)} %copy-done.1, bf16[1024,768]{1,0:T(8,128)(2,1)S(1)} %copy-done.2, bf16[1024,768]{1,0:T(8,128)(2,1)S(1)} %copy-done.3, ...), custom_call_target="tpu_custom_call" | custom-call | flops 400000 | bytes 1000 | tf_op jit(solution)/shard_map/attend_inner/pallas_call | solution.py:564
  11.1 0.7 %collective-permute-start.2 = (bf16[768,768]{1,0:T(8,128)(2,1)S(1)}, bf16[768,768]{1,0:T(8,128)(2,1)S(1)}, u32[]{:S(2)}, u32[]{:S(2)}) collective-permute-start(bf16[768,768]{1,0:T(8,128)(2,1)S(1)} %get-tuple-element.27.own_ref), channel_id=1, source_target_pairs={{0,1},{1,0},{2,3},{3,2},{4,5},{5,4},{6,7},{7,6},{8,9},{9,8},{10,11... | collective-permute-start | bytes 3538952 | tf_op jit(solution)/shard_map/ppermute | solution.py:605
  11.8 1.3 %collective-permute-start = (bf16[336,768]{1,0:T(8,128)(2,1)S(1)}, bf16[336,768]{1,0:T(8,128)(2,1)S(1)}, u32[]{:S(2)}, u32[]{:S(2)}) collective-permute-start(bf16[336,768]{1,0:T(8,128)(2,1)S(1)} %get-tuple-element.25), channel_id=1, source_target_pairs={{0,2},{2,0},{4,6},{6,4},{8,10},{10,8},{12,14},{14,12},{1,3},{3,1},... | collective-permute-start | bytes 1548296 | tf_op jit(solution)/shard_map/ppermute | solution.py:558
  13.1 2.2 %collective-permute-start.1 = (bf16[336,768]{1,0:T(8,128)(2,1)S(1)}, bf16[336,768]{1,0:T(8,128)(2,1)S(1)}, u32[]{:S(2)}, u32[]{:S(2)}) collective-permute-start(bf16[336,768]{1,0:T(8,128)(2,1)S(1)} %get-tuple-element.26), channel_id=1, source_target_pairs={{2,4},{4,2},{6,8},{8,6},{10,12},{12,10},{3,5},{5,3},{7,9},{9,7},{1... | collective-permute-start | bytes 1548296 | tf_op jit(solution)/shard_map/ppermute | solution.py:559
  15.3 0.0 collective-permute-done.3.more_hbm
  15.3 2.3 %project_own.1 = (f32[768,1536]{1,0:T(8,128)S(1)}, bf16[768,1536]{1,0:T(8,128)(2,1)S(1)}) custom-call(bf16[768,768]{1,0:T(8,128)(2,1)S(1)} %get-tuple-element.27.own_ref, bf16[768,1536]{1,0:T(8,128)(2,1)S(1)} %get-tuple-element.28.w_ref.refs_2_, bf16[768,1536]{1,0:T(8,128)(2,1)S(1)} %get-tuple-element.29.r_ref, ...), custom_call_target="tpu_custom_call" | custom-call | flops 4000000000 | bytes 1000 | tf_op jit(solution)/shard_map/project_own/pallas_call | solution.py:606
  17.6 0.0 copy-start.7
  17.6 0.0 copy-start.4
  17.7 3.1 %project_inner.1 = (f32[768,1536]{1,0:T(8,128)S(1)}, f32[16,768]{1,0:T(8,128)S(1)}) custom-call(bf16[768,768]{1,0:T(8,128)(2,1)S(1)} %collective-permute-done.2.refs_0_, bf16[768,1536]{1,0:T(8,128)(2,1)S(1)} %get-tuple-element.30.refs_1_.refs_3_, f32[768,1536]{1,0:T(8,128)S(1)} %get-tuple-element.31.refs_2_), custom_call_target="tpu_custom_call" | custom-call | flops 400000 | bytes 1000 | tf_op jit(solution)/shard_map/project_inner/pallas_call | solution.py:589
  20.7 0.7 %collective-permute-start.4 = (f32[16,768]{1,0:T(8,128)S(1)}, f32[16,768]{1,0:T(8,128)S(1)}, u32[]{:S(2)}, u32[]{:S(2)}) collective-permute-start(f32[16,768]{1,0:T(8,128)S(1)} %get-tuple-element.33.own_ref.s_in_ref), channel_id=1, source_target_pairs={{0,1},{1,0},{2,3},{3,2},{4,5},{5,4},{6,7},{7,6},{8,9},{9,8},{10,11... | collective-permute-start | bytes 147464 | tf_op jit(solution)/shard_map/ppermute | solution.py:617
  21.4 0.9 %collective-permute-done.4.other_ref.t_in_ref = f32[16,768]{1,0:T(8,128)S(1)} collective-permute-done((f32[16,768]{1,0:T(8,128)S(1)}, f32[16,768]{1,0:T(8,128)S(1)}, u32[]{:S(2)}, u32[]{:S(2)}) %collective-permute-start.4) | collective-permute-done | bytes 49184 | tf_op jit(solution)/shard_map/ppermute | solution.py:617
  22.3 11.5 %norm_conv_inner.1.done_ref = bf16[1024,1536]{1,0:T(8,128)(2,1)} custom-call(s32[8]{0:T(128)S(1)} %copy-done.5, s32[8]{0:T(128)S(1)} %copy-done.6, f32[768,1536]{1,0:T(8,128)S(1)} %get-tuple-element.32.h_ref.h_low_ref.h_high_ref, f32[16,768]{1,0:T(8,128)S(1)} %get-tuple-element.33.own_ref.s_in_ref, f32[16,768]{1,0:T(8,128)S(1)} %collective-permute-done.4.other_ref.t_in_ref, ...), custom_call_target="tpu_custom_call" | custom-call | flops 400000 | bytes 1000 | tf_op jit(solution)/shard_map/norm_conv_inner/pallas_call | solution.py:626
  33.8 0.0 copy-start
  33.8 2.4 %collective-permute-done.first_hbm.refs_5_ = bf16[336,768]{1,0:T(8,128)(2,1)S(1)} collective-permute-done((bf16[336,768]{1,0:T(8,128)(2,1)S(1)}, bf16[336,768]{1,0:T(8,128)(2,1)S(1)}, u32[]{:S(2)}, u32[]{:S(2)}) %collective-permute-start) | collective-permute-done | bytes 516128 | tf_op jit(solution)/shard_map/ppermute | solution.py:558
  36.2 5.5 %attend_ends.1.refs_0_ = bf16[288,768]{1,0:T(8,128)(2,1)S(1)} custom-call(s32[8]{0:T(128)S(1)} %copy-done.5, s32[8]{0:T(128)S(1)} %copy-done.6, bf16[1024,768]{1,0:T(8,128)(2,1)S(1)} %copy-done.1, bf16[1024,768]{1,0:T(8,128)(2,1)S(1)} %copy-done.2, bf16[1024,768]{1,0:T(8,128)(2,1)S(1)} %copy-done.3, ...), custom_call_target="tpu_custom_call" | custom-call | flops 2000000000 | bytes 1000 | tf_op jit(solution)/shard_map/attend_ends/pallas_call | solution.py:647
  41.7 0.9 %collective-permute-start.5 = (bf16[288,768]{1,0:T(8,128)(2,1)S(1)}, bf16[288,768]{1,0:T(8,128)(2,1)S(1)}, u32[]{:S(2)}, u32[]{:S(2)}) collective-permute-start(bf16[288,768]{1,0:T(8,128)(2,1)S(1)} %attend_ends.1.refs_0_), channel_id=1, source_target_pairs={{0,1},{1,0},{2,3},{3,2},{4,5},{5,4},{6,7},{7,6},{8,9},{9,8},{10,11... | collective-permute-start | bytes 1327112 | tf_op jit(solution)/shard_map/ppermute | solution.py:660
  42.7 1.4 %collective-permute-done.5.refs_1_ = bf16[288,768]{1,0:T(8,128)(2,1)S(1)} collective-permute-done((bf16[288,768]{1,0:T(8,128)(2,1)S(1)}, bf16[288,768]{1,0:T(8,128)(2,1)S(1)}, u32[]{:S(2)}, u32[]{:S(2)}) %collective-permute-start.5) | collective-permute-done | bytes 442400 | tf_op jit(solution)/shard_map/ppermute | solution.py:660
  44.1 2.7 %project_ends.1 = (f32[288,1536]{1,0:T(8,128)S(1)}, f32[16,384]{1,0:T(8,128)S(1)}) custom-call(bf16[288,768]{1,0:T(8,128)(2,1)S(1)} %attend_ends.1.refs_0_, bf16[288,768]{1,0:T(8,128)(2,1)S(1)} %collective-permute-done.5.refs_1_, bf16[768,1536]{1,0:T(8,128)(2,1)S(1)} %get-tuple-element.28.w_ref.refs_2_, ...), custom_call_target="tpu_custom_call" | custom-call | flops 1600000000 | bytes 1000 | tf_op jit(solution)/shard_map/project_ends/pallas_call | solution.py:589
  46.8 0.4 collective-permute-start.6
  47.2 0.8 %collective-permute-done.6.t_end_ref = f32[16,384]{1,0:T(8,128)S(1)} collective-permute-done((f32[16,384]{1,0:T(8,128)S(1)}, f32[16,384]{1,0:T(8,128)S(1)}, u32[]{:S(2)}, u32[]{:S(2)}) %collective-permute-start.6) | collective-permute-done | bytes 24608 | tf_op jit(solution)/shard_map/ppermute | solution.py:664
  48.1 6.5 %norm_conv_ends.1 = bf16[1024,1536]{1,0:T(8,128)(2,1)} custom-call(s32[8]{0:T(128)S(1)} %copy-done.5, s32[8]{0:T(128)S(1)} %copy-done.6, f32[288,1536]{1,0:T(8,128)S(1)} %get-tuple-element.36.h_end_ref, f32[768,1536]{1,0:T(8,128)S(1)} %get-tuple-element.32.h_ref.h_low_ref.h_high_ref, ...), custom_call_target="tpu_custom_call", output_to_operand_aliasing={{}: (11, {})} | custom-call | flops 2000000000 | bytes 1000 | tf_op jit(solution)/shard_map/norm_conv_ends/pallas_call | solution.py:668
  (15 shorter events, 0.0 us)
Async XLA Ops:
  0.0 2.5 %copy-start.2 = (bf16[1024,768]{1,0:T(8,128)(2,1)S(1)}, bf16[1024,768]{1,0:T(8,128)(2,1)}, u32[]{:S(2)}) copy-start(bf16[1024,768]{1,0:T(8,128)(2,1)} %k_hbm.3) | copy-start | bytes 4718596
  0.0 2.5 %copy-start.3 = (bf16[1024,768]{1,0:T(8,128)(2,1)S(1)}, bf16[1024,768]{1,0:T(8,128)(2,1)}, u32[]{:S(2)}) copy-start(bf16[1024,768]{1,0:T(8,128)(2,1)} %v_hbm.3) | copy-start | bytes 4718596
  0.0 2.8 %copy-start.1 = (bf16[1024,768]{1,0:T(8,128)(2,1)S(1)}, bf16[1024,768]{1,0:T(8,128)(2,1)}, u32[]{:S(2)}) copy-start(bf16[1024,768]{1,0:T(8,128)(2,1)} %q_hbm.1) | copy-start | bytes 4718596
  0.0 2.8 %copy-start.5 = (s32[8]{0:T(128)S(1)}, s32[8]{0:T(128)}, u32[]{:S(2)}) copy-start(s32[8]{0:T(128)} %starts_ref.7) | copy-start | bytes 100
  0.0 2.8 %copy-start.6 = (s32[8]{0:T(128)S(1)}, s32[8]{0:T(128)}, u32[]{:S(2)}) copy-start(s32[8]{0:T(128)} %lengths_ref.7) | copy-start | bytes 100
  0.0 15.3 %collective-permute-start.3 = (bf16[768,3072]{1,0:T(8,128)(2,1)}, bf16[768,3072]{1,0:T(8,128)(2,1)S(1)}, u32[]{:S(2)}, u32[]{:S(2)}) collective-permute-start(bf16[768,3072]{1,0:T(8,128)(2,1)} %w_hbm.1), channel_id=1, source_target_pairs={{0,1},{1,0},{2,3},{3,2},{4,5},{5,4},{6,7},{7,6},{8,9},{9,8},{10,11... | collective-permute-start | bytes 14155784 | tf_op jit(solution)/shard_map/ppermute | solution.py:560
  11.1 6.5 %collective-permute-start.2 = (bf16[768,768]{1,0:T(8,128)(2,1)S(1)}, bf16[768,768]{1,0:T(8,128)(2,1)S(1)}, u32[]{:S(2)}, u32[]{:S(2)}) collective-permute-start(bf16[768,768]{1,0:T(8,128)(2,1)S(1)} %get-tuple-element.27.own_ref), channel_id=1, source_target_pairs={{0,1},{1,0},{2,3},{3,2},{4,5},{5,4},{6,7},{7,6},{8,9},{9,8},{10,11... | collective-permute-start | bytes 3538952 | tf_op jit(solution)/shard_map/ppermute | solution.py:605
  11.8 24.4 %collective-permute-start = (bf16[336,768]{1,0:T(8,128)(2,1)S(1)}, bf16[336,768]{1,0:T(8,128)(2,1)S(1)}, u32[]{:S(2)}, u32[]{:S(2)}) collective-permute-start(bf16[336,768]{1,0:T(8,128)(2,1)S(1)} %get-tuple-element.25), channel_id=1, source_target_pairs={{0,2},{2,0},{4,6},{6,4},{8,10},{10,8},{12,14},{14,12},{1,3},{3,1},... | collective-permute-start | bytes 1548296 | tf_op jit(solution)/shard_map/ppermute | solution.py:558
  13.1 23.1 %collective-permute-start.1 = (bf16[336,768]{1,0:T(8,128)(2,1)S(1)}, bf16[336,768]{1,0:T(8,128)(2,1)S(1)}, u32[]{:S(2)}, u32[]{:S(2)}) collective-permute-start(bf16[336,768]{1,0:T(8,128)(2,1)S(1)} %get-tuple-element.26), channel_id=1, source_target_pairs={{2,4},{4,2},{6,8},{8,6},{10,12},{12,10},{3,5},{5,3},{7,9},{9,7},{1... | collective-permute-start | bytes 1548296 | tf_op jit(solution)/shard_map/ppermute | solution.py:559
  17.6 3.8 %copy-start.7 = (f32[1536]{0:T(1024)S(1)}, f32[1536]{0:T(1024)}, u32[]{:S(2)}) copy-start(f32[1536]{0:T(1024)} %param.14) | copy-start | bytes 18436
  17.6 4.7 %copy-start.4 = (f32[31,1536]{1,0:T(8,128)S(1)}, f32[31,1536]{1,0:T(8,128)}, u32[]{:S(2)}) copy-start(f32[31,1536]{1,0:T(8,128)} %w_ref.3) | copy-start | bytes 571396
  20.7 1.6 %collective-permute-start.4 = (f32[16,768]{1,0:T(8,128)S(1)}, f32[16,768]{1,0:T(8,128)S(1)}, u32[]{:S(2)}, u32[]{:S(2)}) collective-permute-start(f32[16,768]{1,0:T(8,128)S(1)} %get-tuple-element.33.own_ref.s_in_ref), channel_id=1, source_target_pairs={{0,1},{1,0},{2,3},{3,2},{4,5},{5,4},{6,7},{7,6},{8,9},{9,8},{10,11... | collective-permute-start | bytes 147464 | tf_op jit(solution)/shard_map/ppermute | solution.py:617
  33.8 10.3 %copy-start = (bf16[1024,1536]{1,0:T(8,128)(2,1)S(1)}, bf16[1024,1536]{1,0:T(8,128)(2,1)}, u32[]{:S(2)}) copy-start(bf16[1024,1536]{1,0:T(8,128)(2,1)} %refs_4_.1) | copy-start | bytes 9437188
  41.7 2.3 %collective-permute-start.5 = (bf16[288,768]{1,0:T(8,128)(2,1)S(1)}, bf16[288,768]{1,0:T(8,128)(2,1)S(1)}, u32[]{:S(2)}, u32[]{:S(2)}) collective-permute-start(bf16[288,768]{1,0:T(8,128)(2,1)S(1)} %attend_ends.1.refs_0_), channel_id=1, source_target_pairs={{0,1},{1,0},{2,3},{3,2},{4,5},{5,4},{6,7},{7,6},{8,9},{9,8},{10,11... | collective-permute-start | bytes 1327112 | tf_op jit(solution)/shard_map/ppermute | solution.py:660
  46.8 1.3 %collective-permute-start.6 = (f32[16,384]{1,0:T(8,128)S(1)}, f32[16,384]{1,0:T(8,128)S(1)}, u32[]{:S(2)}, u32[]{:S(2)}) collective-permute-start(f32[16,384]{1,0:T(8,128)S(1)} %get-tuple-element.37.s_end_ref), channel_id=1, source_target_pairs={{0,1},{1,0},{2,3},{3,2},{4,5},{5,4},{6,7},{7,6},{8,9},{9,8},{10,11... | collective-permute-start | bytes 73736 | tf_op jit(solution)/shard_map/ppermute | solution.py:664

commit v5 on v4

--- a/solution.py
+++ b/solution.py
@@ -18,7 +18,7 @@
 SPAN = 512
 LANES = 128
 NEG = -1e30
-SHARE = 4
+SHARE = 3
 EXP_SCALE = HSIZE ** (-0.5) * 1.4426950408889634
 SMEM = pl.BlockSpec(memory_space=pltpu.SMEM)
 

time: 55.1 us -> 55 us (level)
  no operation moved by 1% of the time
where the time goes in v5:
time: 55 us; the launch traced here: 54.7 us
  Pallas kernels  41.4 us (75%)
  starting transfers between devices  6.96 us (13%)
  waiting for transfers between devices  5.75 us (10%)
    pallas_call x1, Pallas kernels, on_device(): pl.pallas_call(functools.partial(norm_conv_inner, frames), grid=(width //...  11.3 us
    pallas_call x1, Pallas kernels, on_device(): pl.pallas_call(functools.partial(attend_inner, frames), out_shape=[jax.Sh...  8.31 us
    pallas_call x1, Pallas kernels, on_device(): pl.pallas_call(functools.partial(norm_conv_ends, frames), grid=(width //...  6.43 us
    pallas_call x2, Pallas kernels, projection(): pl.pallas_call(functools.partial(project, inside), in_specs=[anywhere, an...  5.77 us
    pallas_call x1, Pallas kernels, on_device(): pl.pallas_call(functools.partial(attend_ends, frames), out_shape=jax.Shap...  5.51 us
    ppermute x1, waiting for transfers between devices, on_device(): first = lax.ppermute(first_edge, 'seq', [(i, i ^ 1) for i in range(count)])  2.6 us
    pallas_call x1, Pallas kernels, on_device(): pl.pallas_call(project_own, in_specs=[vmem, vmem, vmem, hbm], out_specs=[...  2.33 us
    ppermute x1, starting transfers between devices, on_device(): lax.ppermute(second_edge, 'seq', [(i, (i + 1 ^ 1) - 1) for i in range(1,...  2.19 us
  transfers between devices with their start and end apart: 7, of which 4 were waited for; matrix products, arithmetic and copies ran while one was open for 0% of the time, Pallas kernels for 49%

profile of v5, /device:TPU:17, one launch (start us, length us, event | category | flops | bytes accessed | tf_op | source)
XLA Modules:
  0.0 54.7 jit_solution(10123193061565280490)
XLA Ops:
  0.0 0.7 %collective-permute-start.3 = (bf16[768,3072]{1,0:T(8,128)(2,1)}, bf16[768,3072]{1,0:T(8,128)(2,1)S(1)}, u32[]{:S(2)}, u32[]{:S(2)}) collective-permute-start(bf16[768,3072]{1,0:T(8,128)(2,1)} %w_hbm.1), channel_id=1, source_target_pairs={{0,1},{1,0},{2,3},{3,2},{4,5},{5,4},{6,7},{7,6},{8,9},{9,8},{10,11... | collective-permute-start | bytes 14155784 | tf_op jit(solution)/shard_map/ppermute | solution.py:560
  0.8 1.7 %pack_edges.1 = (bf16[336,768]{1,0:T(8,128)(2,1)S(1)}, bf16[336,768]{1,0:T(8,128)(2,1)S(1)}) custom-call(bf16[1024,768]{1,0:T(8,128)(2,1)} %q_hbm.1, bf16[1024,768]{1,0:T(8,128)(2,1)} %k_hbm.3, bf16[1024,768]{1,0:T(8,128)(2,1)} %v_hbm.3, bf16[1024,1536]{1,0:T(8,128)(2,1)} %refs_4_.1), custom_call_target="tpu_custom_call" | custom-call | tf_op jit(solution)/shard_map/pack_edges/pallas_call | solution.py:548
  2.5 0.2 copy-done.1
  2.8 8.3 %attend_inner.1 = (bf16[768,768]{1,0:T(8,128)(2,1)S(1)}, bf16[768,1536]{1,0:T(8,128)(2,1)S(1)}, bf16[768,1536]{1,0:T(8,128)(2,1)S(1)}) custom-call(s32[8]{0:T(128)S(1)} %copy-done.5, s32[8]{0:T(128)S(1)} %copy-done.6, bf16[1024,768]{1,0:T(8,128)(2,1)S(1)} %copy-done.1, bf16[1024,768]{1,0:T(8,128)(2,1)S(1)} %copy-done.2, bf16[1024,768]{1,0:T(8,128)(2,1)S(1)} %copy-done.3, ...), custom_call_target="tpu_custom_call" | custom-call | flops 400000 | bytes 1000 | tf_op jit(solution)/shard_map/attend_inner/pallas_call | solution.py:564
  11.1 0.7 %collective-permute-start.2 = (bf16[768,768]{1,0:T(8,128)(2,1)S(1)}, bf16[768,768]{1,0:T(8,128)(2,1)S(1)}, u32[]{:S(2)}, u32[]{:S(2)}) collective-permute-start(bf16[768,768]{1,0:T(8,128)(2,1)S(1)} %get-tuple-element.27.own_ref), channel_id=1, source_target_pairs={{0,1},{1,0},{2,3},{3,2},{4,5},{5,4},{6,7},{7,6},{8,9},{9,8},{10,11... | collective-permute-start | bytes 3538952 | tf_op jit(solution)/shard_map/ppermute | solution.py:605
  11.8 1.3 %collective-permute-start = (bf16[336,768]{1,0:T(8,128)(2,1)S(1)}, bf16[336,768]{1,0:T(8,128)(2,1)S(1)}, u32[]{:S(2)}, u32[]{:S(2)}) collective-permute-start(bf16[336,768]{1,0:T(8,128)(2,1)S(1)} %get-tuple-element.25), channel_id=1, source_target_pairs={{0,2},{2,0},{4,6},{6,4},{8,10},{10,8},{12,14},{14,12},{1,3},{3,1},... | collective-permute-start | bytes 1548296 | tf_op jit(solution)/shard_map/ppermute | solution.py:558
  13.1 2.2 %collective-permute-start.1 = (bf16[336,768]{1,0:T(8,128)(2,1)S(1)}, bf16[336,768]{1,0:T(8,128)(2,1)S(1)}, u32[]{:S(2)}, u32[]{:S(2)}) collective-permute-start(bf16[336,768]{1,0:T(8,128)(2,1)S(1)} %get-tuple-element.26), channel_id=1, source_target_pairs={{2,4},{4,2},{6,8},{8,6},{10,12},{12,10},{3,5},{5,3},{7,9},{9,7},{1... | collective-permute-start | bytes 1548296 | tf_op jit(solution)/shard_map/ppermute | solution.py:559
  15.3 0.0 collective-permute-done.3.more_hbm
  15.3 2.3 %project_own.1 = (f32[768,1536]{1,0:T(8,128)S(1)}, bf16[768,1536]{1,0:T(8,128)(2,1)S(1)}) custom-call(bf16[768,768]{1,0:T(8,128)(2,1)S(1)} %get-tuple-element.27.own_ref, bf16[768,1536]{1,0:T(8,128)(2,1)S(1)} %get-tuple-element.28.w_ref.refs_2_, bf16[768,1536]{1,0:T(8,128)(2,1)S(1)} %get-tuple-element.29.r_ref, ...), custom_call_target="tpu_custom_call" | custom-call | flops 4000000000 | bytes 1000 | tf_op jit(solution)/shard_map/project_own/pallas_call | solution.py:606
  17.6 0.0 copy-start.7
  17.6 0.0 copy-start.4
  17.7 3.1 %project_inner.1 = (f32[768,1536]{1,0:T(8,128)S(1)}, f32[16,768]{1,0:T(8,128)S(1)}) custom-call(bf16[768,768]{1,0:T(8,128)(2,1)S(1)} %collective-permute-done.2.refs_0_, bf16[768,1536]{1,0:T(8,128)(2,1)S(1)} %get-tuple-element.30.refs_1_.refs_3_, f32[768,1536]{1,0:T(8,128)S(1)} %get-tuple-element.31.refs_2_), custom_call_target="tpu_custom_call" | custom-call | flops 400000 | bytes 1000 | tf_op jit(solution)/shard_map/project_inner/pallas_call | solution.py:589
  20.7 0.7 %collective-permute-start.4 = (f32[16,768]{1,0:T(8,128)S(1)}, f32[16,768]{1,0:T(8,128)S(1)}, u32[]{:S(2)}, u32[]{:S(2)}) collective-permute-start(f32[16,768]{1,0:T(8,128)S(1)} %get-tuple-element.33.own_ref.s_in_ref), channel_id=1, source_target_pairs={{0,1},{1,0},{2,3},{3,2},{4,5},{5,4},{6,7},{7,6},{8,9},{9,8},{10,11... | collective-permute-start | bytes 147464 | tf_op jit(solution)/shard_map/ppermute | solution.py:617
  21.4 0.9 %collective-permute-done.4.other_ref.t_in_ref = f32[16,768]{1,0:T(8,128)S(1)} collective-permute-done((f32[16,768]{1,0:T(8,128)S(1)}, f32[16,768]{1,0:T(8,128)S(1)}, u32[]{:S(2)}, u32[]{:S(2)}) %collective-permute-start.4) | collective-permute-done | bytes 49184 | tf_op jit(solution)/shard_map/ppermute | solution.py:617
  22.3 11.3 %norm_conv_inner.1.done_ref = bf16[1024,1536]{1,0:T(8,128)(2,1)} custom-call(s32[8]{0:T(128)S(1)} %copy-done.5, s32[8]{0:T(128)S(1)} %copy-done.6, f32[768,1536]{1,0:T(8,128)S(1)} %get-tuple-element.32.h_ref.h_low_ref.h_high_ref, f32[16,768]{1,0:T(8,128)S(1)} %get-tuple-element.33.own_ref.s_in_ref, f32[16,768]{1,0:T(8,128)S(1)} %collective-permute-done.4.other_ref.t_in_ref, ...), custom_call_target="tpu_custom_call" | custom-call | flops 400000 | bytes 1000 | tf_op jit(solution)/shard_map/norm_conv_inner/pallas_call | solution.py:626
  33.6 0.0 copy-start
  33.6 2.6 %collective-permute-done.first_hbm.refs_5_ = bf16[336,768]{1,0:T(8,128)(2,1)S(1)} collective-permute-done((bf16[336,768]{1,0:T(8,128)(2,1)S(1)}, bf16[336,768]{1,0:T(8,128)(2,1)S(1)}, u32[]{:S(2)}, u32[]{:S(2)}) %collective-permute-start) | collective-permute-done | bytes 516128 | tf_op jit(solution)/shard_map/ppermute | solution.py:558
  36.2 5.5 %attend_ends.1.refs_0_ = bf16[288,768]{1,0:T(8,128)(2,1)S(1)} custom-call(s32[8]{0:T(128)S(1)} %copy-done.5, s32[8]{0:T(128)S(1)} %copy-done.6, bf16[1024,768]{1,0:T(8,128)(2,1)S(1)} %copy-done.1, bf16[1024,768]{1,0:T(8,128)(2,1)S(1)} %copy-done.2, bf16[1024,768]{1,0:T(8,128)(2,1)S(1)} %copy-done.3, ...), custom_call_target="tpu_custom_call" | custom-call | flops 2000000000 | bytes 1000 | tf_op jit(solution)/shard_map/attend_ends/pallas_call | solution.py:647
  41.7 0.9 %collective-permute-start.5 = (bf16[288,768]{1,0:T(8,128)(2,1)S(1)}, bf16[288,768]{1,0:T(8,128)(2,1)S(1)}, u32[]{:S(2)}, u32[]{:S(2)}) collective-permute-start(bf16[288,768]{1,0:T(8,128)(2,1)S(1)} %attend_ends.1.refs_0_), channel_id=1, source_target_pairs={{0,1},{1,0},{2,3},{3,2},{4,5},{5,4},{6,7},{7,6},{8,9},{9,8},{10,11... | collective-permute-start | bytes 1327112 | tf_op jit(solution)/shard_map/ppermute | solution.py:660
  42.7 1.4 %collective-permute-done.5.refs_1_ = bf16[288,768]{1,0:T(8,128)(2,1)S(1)} collective-permute-done((bf16[288,768]{1,0:T(8,128)(2,1)S(1)}, bf16[288,768]{1,0:T(8,128)(2,1)S(1)}, u32[]{:S(2)}, u32[]{:S(2)}) %collective-permute-start.5) | collective-permute-done | bytes 442400 | tf_op jit(solution)/shard_map/ppermute | solution.py:660
  44.1 2.7 %project_ends.1 = (f32[288,1536]{1,0:T(8,128)S(1)}, f32[16,384]{1,0:T(8,128)S(1)}) custom-call(bf16[288,768]{1,0:T(8,128)(2,1)S(1)} %attend_ends.1.refs_0_, bf16[288,768]{1,0:T(8,128)(2,1)S(1)} %collective-permute-done.5.refs_1_, bf16[768,1536]{1,0:T(8,128)(2,1)S(1)} %get-tuple-element.28.w_ref.refs_2_, ...), custom_call_target="tpu_custom_call" | custom-call | flops 1600000000 | bytes 1000 | tf_op jit(solution)/shard_map/project_ends/pallas_call | solution.py:589
  46.8 0.4 collective-permute-start.6
  47.2 0.8 %collective-permute-done.6.t_end_ref = f32[16,384]{1,0:T(8,128)S(1)} collective-permute-done((f32[16,384]{1,0:T(8,128)S(1)}, f32[16,384]{1,0:T(8,128)S(1)}, u32[]{:S(2)}, u32[]{:S(2)}) %collective-permute-start.6) | collective-permute-done | bytes 24608 | tf_op jit(solution)/shard_map/ppermute | solution.py:664
  48.1 6.4 %norm_conv_ends.1 = bf16[1024,1536]{1,0:T(8,128)(2,1)} custom-call(s32[8]{0:T(128)S(1)} %copy-done.5, s32[8]{0:T(128)S(1)} %copy-done.6, f32[288,1536]{1,0:T(8,128)S(1)} %get-tuple-element.36.h_end_ref, f32[768,1536]{1,0:T(8,128)S(1)} %get-tuple-element.32.h_ref.h_low_ref.h_high_ref, ...), custom_call_target="tpu_custom_call", output_to_operand_aliasing={{}: (11, {})} | custom-call | flops 2000000000 | bytes 1000 | tf_op jit(solution)/shard_map/norm_conv_ends/pallas_call | solution.py:668
  (15 shorter events, 0.0 us)
Async XLA Ops:
  0.0 2.5 %copy-start.2 = (bf16[1024,768]{1,0:T(8,128)(2,1)S(1)}, bf16[1024,768]{1,0:T(8,128)(2,1)}, u32[]{:S(2)}) copy-start(bf16[1024,768]{1,0:T(8,128)(2,1)} %k_hbm.3) | copy-start | bytes 4718596
  0.0 2.5 %copy-start.3 = (bf16[1024,768]{1,0:T(8,128)(2,1)S(1)}, bf16[1024,768]{1,0:T(8,128)(2,1)}, u32[]{:S(2)}) copy-start(bf16[1024,768]{1,0:T(8,128)(2,1)} %v_hbm.3) | copy-start | bytes 4718596
  0.0 2.8 %copy-start.1 = (bf16[1024,768]{1,0:T(8,128)(2,1)S(1)}, bf16[1024,768]{1,0:T(8,128)(2,1)}, u32[]{:S(2)}) copy-start(bf16[1024,768]{1,0:T(8,128)(2,1)} %q_hbm.1) | copy-start | bytes 4718596
  0.0 2.8 %copy-start.5 = (s32[8]{0:T(128)S(1)}, s32[8]{0:T(128)}, u32[]{:S(2)}) copy-start(s32[8]{0:T(128)} %starts_ref.7) | copy-start | bytes 100
  0.0 2.8 %copy-start.6 = (s32[8]{0:T(128)S(1)}, s32[8]{0:T(128)}, u32[]{:S(2)}) copy-start(s32[8]{0:T(128)} %lengths_ref.7) | copy-start | bytes 100
  0.0 15.3 %collective-permute-start.3 = (bf16[768,3072]{1,0:T(8,128)(2,1)}, bf16[768,3072]{1,0:T(8,128)(2,1)S(1)}, u32[]{:S(2)}, u32[]{:S(2)}) collective-permute-start(bf16[768,3072]{1,0:T(8,128)(2,1)} %w_hbm.1), channel_id=1, source_target_pairs={{0,1},{1,0},{2,3},{3,2},{4,5},{5,4},{6,7},{7,6},{8,9},{9,8},{10,11... | collective-permute-start | bytes 14155784 | tf_op jit(solution)/shard_map/ppermute | solution.py:560
  11.1 6.5 %collective-permute-start.2 = (bf16[768,768]{1,0:T(8,128)(2,1)S(1)}, bf16[768,768]{1,0:T(8,128)(2,1)S(1)}, u32[]{:S(2)}, u32[]{:S(2)}) collective-permute-start(bf16[768,768]{1,0:T(8,128)(2,1)S(1)} %get-tuple-element.27.own_ref), channel_id=1, source_target_pairs={{0,1},{1,0},{2,3},{3,2},{4,5},{5,4},{6,7},{7,6},{8,9},{9,8},{10,11... | collective-permute-start | bytes 3538952 | tf_op jit(solution)/shard_map/ppermute | solution.py:605
  11.8 24.4 %collective-permute-start = (bf16[336,768]{1,0:T(8,128)(2,1)S(1)}, bf16[336,768]{1,0:T(8,128)(2,1)S(1)}, u32[]{:S(2)}, u32[]{:S(2)}) collective-permute-start(bf16[336,768]{1,0:T(8,128)(2,1)S(1)} %get-tuple-element.25), channel_id=1, source_target_pairs={{0,2},{2,0},{4,6},{6,4},{8,10},{10,8},{12,14},{14,12},{1,3},{3,1},... | collective-permute-start | bytes 1548296 | tf_op jit(solution)/shard_map/ppermute | solution.py:558
  13.1 23.1 %collective-permute-start.1 = (bf16[336,768]{1,0:T(8,128)(2,1)S(1)}, bf16[336,768]{1,0:T(8,128)(2,1)S(1)}, u32[]{:S(2)}, u32[]{:S(2)}) collective-permute-start(bf16[336,768]{1,0:T(8,128)(2,1)S(1)} %get-tuple-element.26), channel_id=1, source_target_pairs={{2,4},{4,2},{6,8},{8,6},{10,12},{12,10},{3,5},{5,3},{7,9},{9,7},{1... | collective-permute-start | bytes 1548296 | tf_op jit(solution)/shard_map/ppermute | solution.py:559
  17.6 3.8 %copy-start.7 = (f32[1536]{0:T(1024)S(1)}, f32[1536]{0:T(1024)}, u32[]{:S(2)}) copy-start(f32[1536]{0:T(1024)} %param.14) | copy-start | bytes 18436
  17.6 4.7 %copy-start.4 = (f32[31,1536]{1,0:T(8,128)S(1)}, f32[31,1536]{1,0:T(8,128)}, u32[]{:S(2)}) copy-start(f32[31,1536]{1,0:T(8,128)} %w_ref.3) | copy-start | bytes 571396
  20.7 1.6 %collective-permute-start.4 = (f32[16,768]{1,0:T(8,128)S(1)}, f32[16,768]{1,0:T(8,128)S(1)}, u32[]{:S(2)}, u32[]{:S(2)}) collective-permute-start(f32[16,768]{1,0:T(8,128)S(1)} %get-tuple-element.33.own_ref.s_in_ref), channel_id=1, source_target_pairs={{0,1},{1,0},{2,3},{3,2},{4,5},{5,4},{6,7},{7,6},{8,9},{9,8},{10,11... | collective-permute-start | bytes 147464 | tf_op jit(solution)/shard_map/ppermute | solution.py:617
  33.6 10.5 %copy-start = (bf16[1024,1536]{1,0:T(8,128)(2,1)S(1)}, bf16[1024,1536]{1,0:T(8,128)(2,1)}, u32[]{:S(2)}) copy-start(bf16[1024,1536]{1,0:T(8,128)(2,1)} %refs_4_.1) | copy-start | bytes 9437188
  41.7 2.3 %collective-permute-start.5 = (bf16[288,768]{1,0:T(8,128)(2,1)S(1)}, bf16[288,768]{1,0:T(8,128)(2,1)S(1)}, u32[]{:S(2)}, u32[]{:S(2)}) collective-permute-start(bf16[288,768]{1,0:T(8,128)(2,1)S(1)} %attend_ends.1.refs_0_), channel_id=1, source_target_pairs={{0,1},{1,0},{2,3},{3,2},{4,5},{5,4},{6,7},{7,6},{8,9},{9,8},{10,11... | collective-permute-start | bytes 1327112 | tf_op jit(solution)/shard_map/ppermute | solution.py:660
  46.8 1.3 %collective-permute-start.6 = (f32[16,384]{1,0:T(8,128)S(1)}, f32[16,384]{1,0:T(8,128)S(1)}, u32[]{:S(2)}, u32[]{:S(2)}) collective-permute-start(f32[16,384]{1,0:T(8,128)S(1)} %get-tuple-element.37.s_end_ref), channel_id=1, source_target_pairs={{0,1},{1,0},{2,3},{3,2},{4,5},{5,4},{6,7},{7,6},{8,9},{9,8},{10,11... | collective-permute-start | bytes 73736 | tf_op jit(solution)/shard_map/ppermute | solution.py:664
